TPU v7x, 256 devices: a whole 4x4x8 slice. The times are simulated.
256 devices in a mesh: dp: 32 (over y, z), section: 8 (over x, core).
Axes of the slice: x: 4, y: 4, z: 8, core: 2. Of those that a mesh axis runs over, the one named last changes fastest.
Arguments:
- grad_rows: bfloat16 [131072, 1280], P(('dp', 'section')), may hold values from -24 to 24
- layer_input: bfloat16 [196608, 1280], P(('dp', 'section')), may hold values from -18 to 18
- saved_qkv: bfloat16 [196608, 1920], P(('dp', 'section')), may hold values from -30 to 30
- image_patches: int32 [32, 32], P('dp'), may hold values from 0 to 256, as said below
- image_owner: int32 [32, 32], P('dp'), may hold values from 0 to 7, as said below
- norm_gain: float32 [1280], replicated, may hold values from 0.1 to 1.9
- norm_bias: float32 [1280], replicated, may hold values from -3 to 3
- w_qkv: bfloat16 [1280, 1920], P('dp'), may hold values from -0.15625 to 0.15625
- w_out: bfloat16 [1280, 640], P('dp'), may hold values from -0.25 to 0.25
Outputs:
- layer_grad: bfloat16 [196608, 1280], P(('dp', 'section'))
- qkv_weight_grad: float32 [1280, 1920], P('dp')
- out_weight_grad: float32 [1280, 640], P('dp')
Inputs may be any that keep to these rules, and one draw needn't show every extreme that they name: `image_patches`: each row lists one dp index's images in order; their counts, multiples of 128, fill that index's 8 devices with exactly 512 rows each, in section order; an image may run on from the last tile of one device to the first tile of the next; after the last image the entries are 0. `image_owner`: the images of one owner in one row hold at most 768 rows together, exactly 768 for some owner of every row; each device hands at most 128 rows to one owner; entries after the last image are 0.
All inputs are finite; a program needn't handle non-finite values.
Results may differ from a plain program's by a relative error of at most 0.019.
Values may be sent and summed in bfloat16 or wider, within the bound.
No kernel may reach another device: no remote copies, remote signals or barrier semaphores. Data moves between devices by JAX's collectives and lax.ppermute only.
A program may use at most 192 MiB of HBM per device.

v0:
```python
import math

import jax
import jax.numpy as jnp
from jax import lax
from jax.sharding import PartitionSpec as P

HEADS = 8
HEAD_DIM = 80
TILE = 128


norm_eps = 1e-06


def route_column(patches, owners):
    image_count = patches.shape[0]
    tile_counts = patches // TILE
    index_list = jnp.arange(image_count, dtype=jnp.int32)
    earlier = index_list[:, None] > index_list[None, :]
    begins = jnp.sum(jnp.where(earlier, tile_counts[None, :], 0), axis=1)
    same_owner = owners[:, None] == owners[None, :]
    slot_start = jnp.sum(jnp.where(earlier & same_owner, tile_counts[None, :], 0), axis=1)
    return (tile_counts, begins, slot_start)


def tile_targets(tile_counts, begins, slot_start, owners, tile_total):
    position = jnp.arange(tile_total, dtype=jnp.int32)
    ends = begins + tile_counts
    image_of = jnp.sum((ends[None, :] <= position[:, None]).astype(jnp.int32), axis=1)
    chosen = image_of[:, None] == jnp.arange(tile_counts.shape[0], dtype=jnp.int32)[None, :]
    tile_owner = jnp.sum(jnp.where(chosen, owners[None, :], 0), axis=1)
    tile_slot = jnp.sum(jnp.where(chosen, (slot_start - begins)[None, :], 0), axis=1) + position
    return (tile_owner, tile_slot)


def owner_segments(tile_counts, slot_start, owners, section_index, own_tiles):
    image_count = tile_counts.shape[0]
    slot_grid = jnp.arange(own_tiles, dtype=jnp.int32)[:, None]
    covered = (
        (owners[None, :] == section_index)
        & (slot_start[None, :] <= slot_grid)
        & (slot_grid < (slot_start + tile_counts)[None, :])
    )
    image_id = jnp.sum(
        jnp.where(covered, jnp.arange(image_count, dtype=jnp.int32)[None, :], 0), axis=1
    )
    return jnp.where(jnp.any(covered, axis=1), image_id, -1)


def attend(qkv, segment):
    row_count = qkv.shape[0]
    heads = qkv.reshape(row_count, 3, HEADS, HEAD_DIM)
    score_scale = 1.0 / math.sqrt(HEAD_DIM)
    scores = (
        jnp.einsum("rhd,shd->hrs", heads[:, 0], heads[:, 1], preferred_element_type=jnp.float32)
        * score_scale
    )
    scores = jnp.where((segment[:, None] == segment[None, :])[None], scores, -jnp.inf)
    shifted = jnp.exp(scores - jnp.max(scores, axis=2, keepdims=True))
    probabilities = shifted / jnp.sum(shifted, axis=2, keepdims=True)
    weights = probabilities.astype(jnp.bfloat16)
    attended = jnp.einsum("hrs,shd->rhd", weights, heads[:, 2], preferred_element_type=jnp.float32)
    return (
        probabilities,
        weights,
        attended.astype(jnp.bfloat16).reshape(row_count, HEADS * HEAD_DIM),
    )


def attend_back(qkv, probabilities, weights, attended, d_attn):
    row_count = qkv.shape[0]
    heads = qkv.reshape(row_count, 3, HEADS, HEAD_DIM)
    score_scale = 1.0 / math.sqrt(HEAD_DIM)
    grad_out = d_attn.reshape(row_count, HEADS, HEAD_DIM)
    row_delta = jnp.sum(
        grad_out.astype(jnp.float32)
        * attended.reshape(row_count, HEADS, HEAD_DIM).astype(jnp.float32),
        axis=2,
    )
    prob_grad = jnp.einsum(
        "rhd,shd->hrs", grad_out, heads[:, 2], preferred_element_type=jnp.float32
    )
    dscore = (
        probabilities * (prob_grad - jnp.transpose(row_delta)[:, :, None]) * score_scale
    ).astype(jnp.bfloat16)
    dquery = jnp.einsum("hrs,shd->rhd", dscore, heads[:, 1], preferred_element_type=jnp.float32)
    key_grad = jnp.einsum("hrs,rhd->shd", dscore, heads[:, 0], preferred_element_type=jnp.float32)
    dvalues = jnp.einsum("hrs,rhd->shd", weights, grad_out, preferred_element_type=jnp.float32)
    return (
        jnp.stack([dquery, key_grad, dvalues], axis=1)
        .reshape(row_count, 3 * HEADS * HEAD_DIM)
        .astype(jnp.bfloat16)
    )


def on_device(
    grad_rows,
    layer_input,
    saved_qkv,
    image_patches,
    image_owner,
    norm_gain,
    norm_bias,
    w_qkv,
    w_out,
):
    sections = lax.axis_size("section")
    section_index = lax.axis_index("section")
    feature_count = grad_rows.shape[1]
    src_tiles = grad_rows.shape[0] // TILE
    own_tiles = layer_input.shape[0] // TILE
    tile_total = sections * src_tiles
    owners = image_owner[0]
    tile_counts, begins, slot_start = route_column(image_patches[0], owners)
    tile_owner, tile_slot = tile_targets(tile_counts, begins, slot_start, owners, tile_total)
    segment = jnp.repeat(
        owner_segments(tile_counts, slot_start, owners, section_index, own_tiles), TILE
    )
    wanted = (tile_owner[None, :] == section_index) & (
        tile_slot[None, :] == jnp.arange(own_tiles, dtype=jnp.int32)[:, None]
    )
    pair_slots = src_tiles // 4
    position = jnp.arange(tile_total, dtype=jnp.int32)
    source = position // src_tiles
    before = (
        (position[:, None] > position[None, :])
        & (source[:, None] == source[None, :])
        & (tile_owner[:, None] == tile_owner[None, :])
    )
    pair_rank = jnp.sum(before.astype(jnp.int32), axis=1)
    own_owner = lax.dynamic_slice_in_dim(tile_owner, section_index * src_tiles, src_tiles)
    own_rank = lax.dynamic_slice_in_dim(pair_rank, section_index * src_tiles, src_tiles)
    buffer_slot = jnp.arange(sections * pair_slots, dtype=jnp.int32)
    packing = ((own_owner * pair_slots + own_rank)[None, :] == buffer_slot[:, None]).astype(
        jnp.bfloat16
    )
    flat_rows = grad_rows.reshape(src_tiles, TILE * feature_count)
    outgoing = jnp.dot(packing, flat_rows, preferred_element_type=jnp.float32).astype(jnp.bfloat16)
    outgoing = outgoing.reshape(sections * pair_slots * TILE, feature_count)
    arrived = lax.all_to_all(outgoing, "section", split_axis=0, concat_axis=0, tiled=True)
    labels = ((source * pair_slots + pair_rank)[:, None] == buffer_slot[None, :]).astype(
        jnp.float32
    )
    selector = jnp.dot(wanted.astype(jnp.float32), labels).astype(jnp.bfloat16)
    incoming = jnp.dot(
        selector,
        arrived.reshape(sections * pair_slots, TILE * feature_count),
        preferred_element_type=jnp.float32,
    )
    incoming = incoming.astype(jnp.bfloat16).reshape(own_tiles * TILE, feature_count)
    incoming_cols = incoming
    d_attn = jnp.dot(
        incoming_cols,
        lax.all_gather(w_out, "dp", axis=0, tiled=True),
        preferred_element_type=jnp.float32,
    ).astype(jnp.bfloat16)
    widened = layer_input.astype(jnp.float32)
    average = jnp.mean(widened, axis=1, keepdims=True)
    centered = widened - average
    inv_scale = lax.rsqrt(jnp.mean(centered * centered, axis=1, keepdims=True) + norm_eps)
    normalized = centered * inv_scale
    normed = (normalized * norm_gain + norm_bias).astype(jnp.bfloat16)
    probabilities, weights, attended = attend(saved_qkv, segment)
    dqkv = attend_back(saved_qkv, probabilities, weights, attended, d_attn)
    dnormed = lax.dot_general(
        dqkv,
        lax.all_gather(w_qkv, "dp", axis=0, tiled=True),
        (((1,), (1,)), ((), ())),
        preferred_element_type=jnp.float32,
    )
    scaled_grad = dnormed * norm_gain
    branch = inv_scale * (
        scaled_grad
        - jnp.mean(scaled_grad, axis=1, keepdims=True)
        - normalized * jnp.mean(scaled_grad * normalized, axis=1, keepdims=True)
    )
    layer_grad = (incoming.astype(jnp.float32) + branch).astype(jnp.bfloat16)
    incoming_cols = incoming
    qkv_part = lax.dot_general(
        normed, dqkv, (((0,), (0,)), ((), ())), preferred_element_type=jnp.float32
    )
    out_part = lax.dot_general(
        incoming_cols, attended, (((0,), (0,)), ((), ())), preferred_element_type=jnp.float32
    )
    reduced = lax.psum_scatter(
        jnp.concatenate([qkv_part, out_part], axis=1), "dp", scatter_dimension=0, tiled=True
    )
    reduced = lax.psum(reduced, "section")
    devices = lax.axis_size("dp") * sections
    reduced = reduced / devices
    qkv_width = w_qkv.shape[1]
    return (layer_grad, reduced[:, :qkv_width], reduced[:, qkv_width:])


def solution(mesh):
    return jax.shard_map(
        on_device,
        mesh=mesh,
        in_specs=(
            P(("dp", "section"), None),
            P(("dp", "section"), None),
            P(("dp", "section"), None),
            P("dp", None),
            P("dp", None),
            P(),
            P(),
            P("dp", None),
            P("dp", None),
        ),
        out_specs=(P(("dp", "section"), None), P("dp", None), P("dp", None)),
        check_vma=False,
    )
```

profile of v0, /device:TPU:1, one launch (start us, length us, event | category | flops | bytes accessed | tf_op | source)
XLA Modules:
  0.0 488.8 jit_solution(15332816329754664877)
XLA Ops:
  7.2 0.0 all-gather.3.cloned.1.call-start
  7.2 0.7 all-gather.3.cloned.1.call-update
  7.9 2.3 reshape.144
  10.2 0.7 fusion.70
  10.9 0.9 select_reduce_fusion.1
  11.8 0.7 fusion.47
  12.5 0.1 convert_reduce_fusion.2
  12.6 0.8 select_reduce_fusion
  13.4 0.2 convert_reduce_fusion.1
  13.6 0.1 dynamic-slice_add_fusion
  13.7 0.8 convolution_convert_fusion.1
  14.6 1.9 copy.27
  16.5 0.0 copy-start.4
  16.5 7.6 %all-to-all-start = ((bf16[8,128,1280]{2,1,0:T(8,128)(2,1)}), bf16[8,128,1280]{2,1,0:T(8,128)(2,1)}, u32[]{:S(2)}, u32[]{:S(2)}) async-start(bf16[8,128,1280]{2,1,0:T(8,128)(2,1)} %copy.27), calls=%async_computation | async-start | bytes 5242880 | tf_op jit(solution)/shard_map/all_to_all | solution.py:141
  24.1 0.0 all-gather.5.cloned.1.call-start
  24.1 0.7 all-gather.5.cloned.1.call-update
  24.9 0.0 reduce-scatter.2.cloned.1.call-start
  24.9 0.0 copy-done.4
  24.9 0.1 fusion.41
  25.1 0.1 select_reduce_fusion.4
  25.2 0.0 copy-done
  25.2 0.3 convert_reduce_fusion
  25.6 0.1 broadcast_bitcast_fusion
  25.6 0.4 broadcast_compare_fusion
  26.0 4.6 copy.28
  30.6 11.4 %fusion.53 = (f32[8,768]{1,0:T(8,128)S(1)}, f32[8,768,768]{1,2,0:T(8,128)}) fusion(pred[768,768]{0,1:T(8,128)(4,1)S(1)} %broadcast_compare_fusion, bf16[768,3,8,80]{0,3,2,1:T(8,128)(2,1)} %bitcast.90), kind=kOutput, calls=%fused_computation.104 | convolution fusion | flops 773849856 | bytes 21454848 | tf_op jit(solution)/shard_map/sub | solution.py:60
  42.0 11.5 %fusion.5 = bf16[8,768,768]{1,2,0:T(8,128)(2,1)} fusion(f32[8,768,768]{1,2,0:T(8,128)} %get-tuple-element.12, f32[8,768]{1,0:T(8,128)S(1)} %get-tuple-element.11), kind=kLoop, calls=%fused_computation.12 | loop fusion | flops 9437184 | bytes 28336128 | tf_op jit(solution)/shard_map/convert_element_type | solution.py:62
  53.5 0.6 fusion.20
  54.2 2.0 all-to-all-done
  56.2 4.6 copy.41
  60.9 4.3 convolution_convert_fusion
  65.1 5.9 %reshape.146 = bf16[768,1280]{1,0:T(8,128)(2,1)} reshape(bf16[6,163840]{1,0:T(8,128)(2,1)} %convolution_convert_fusion) | data formatting | bytes 3932160 | tf_op jit(solution)/shard_map/reshape | solution.py:151
  71.1 16.4 %all-gather.3.cloned.1.call-done = bf16[1280,640]{1,0:T(8,128)(2,1)} async-done(((bf16[40,640]{1,0:T(8,128)(2,1)}), bf16[1280,640]{1,0:T(8,128)(2,1)}) %all-gather.3.cloned.1.call-update) | async-done | bytes 1638416 | tf_op jit(solution)/shard_map/all_gather | solution.py:155
  87.5 3.7 convolution_convert_fusion.6
  91.2 0.0 slice-start.2
  91.2 7.7 %fusion.28 = bf16[768,1,8,80]{0,3,2,1:T(8,128)(2,1)} fusion(bf16[768,8,80]{0,2,1:T(8,128)(2,1)S(1)} %bitcast.96, bf16[8,768,768]{1,2,0:T(8,128)(2,1)} %fusion.5), kind=kOutput, calls=%fused_computation.43 | convolution fusion | flops 755466240 | bytes 11403264 | tf_op jit(solution)/shard_map/hrs,rhd->shd/dot_general | solution.py:89
  98.9 0.0 slice-done
  98.9 0.0 slice-done.1
  98.9 0.0 slice-done.2
  98.9 4.0 multiply_reduce_fusion
  102.9 8.7 %multiply_convert_fusion = bf16[8,768,768]{1,2,0:T(8,128)(2,1)S(1)} fusion(f32[8,768]{1,0:T(8,128)S(1)} %bitcast.102, bf16[768,8,80]{0,2,1:T(8,128)(2,1)S(1)} %bitcast.98, f32[8,768,768]{1,2,0:T(8,128)} %get-tuple-element.12, f32[8,768]{1,0:T(8,128)S(1)} %get-tuple-element.11, bf16[768,3,8,80]{0,3,2,1:T(8,128)(2,1)} %bitcast.92), kind=kOutput, calls=%fused_computation.3 | convolution fusion | flops 778567680 | bytes 30326784 | tf_op jit(solution)/shard_map/rhd,shd->hrs/dot_general | solution.py:81
  111.5 2.9 fusion.29
  114.5 5.1 %fusion.27 = bf16[768,1,8,80]{0,3,2,1:T(8,128)(2,1)} fusion(bf16[8,768,768]{1,2,0:T(8,128)(2,1)S(1)} %multiply_convert_fusion, bf16[768,3,8,80]{0,3,2,1:T(8,128)(2,1)} %bitcast.94), kind=kOutput, calls=%fused_computation.42 | convolution fusion | flops 755466240 | bytes 11403264 | tf_op jit(solution)/shard_map/hrs,rhd->shd/dot_general | solution.py:88
  119.6 2.0 pad_maximum_fusion.1
  121.5 0.0 copy-start.2
  121.5 0.2 copy-done.1
  121.7 0.2 copy-done.3
  121.9 1.8 fusion.54
  123.7 0.0 copy-done.2
  123.7 0.0 copy-done.5
  123.7 0.0 copy-done.6
  123.7 4.8 fusion.21
  128.5 5.3 %pad_maximum_fusion = f32[1280,2560]{1,0:T(8,128)} fusion(f32[1280,640]{1,0:T(8,128)S(1)} %fusion.54, f32[1280,1920]{1,0:T(8,128)S(1)} %fusion.21), kind=kLoop, calls=%fused_computation.7 | loop fusion | flops 3276800 | bytes 26214400 | tf_op jit(solution)/shard_map/concatenate | solution.py:187
  133.8 0.0 reduce-scatter.2.cloned.1.call-update
  133.8 0.3 all-reduce.2.cloned.1.call-start
  134.1 39.5 %all-gather.5.cloned.1.call-done = bf16[1280,1920]{1,0:T(8,128)(2,1)} async-done(((bf16[40,1920]{1,0:T(8,128)(2,1)}), bf16[1280,1920]{1,0:T(8,128)(2,1)}) %all-gather.5.cloned.1.call-update) | async-done | bytes 4915216 | tf_op jit(solution)/shard_map/all_gather | solution.py:168
  173.6 9.9 %fusion.52 = (f32[768]{0:T(1024)S(1)}, f32[768]{0:T(1024)S(1)}, f32[768,1280]{1,0:T(8,128)}) fusion(f32[768]{0:T(1024)S(1)} %add_rsqrt_fusion, f32[768]{0:T(1024)S(1)} %broadcast_multiply_fusion.3, bf16[768,1280]{1,0:T(8,128)(2,1)S(1)} %copy-done, f32[1280]{0:T(1024)S(1)} %copy-done.6, bf16[768,1920]{0,1:T(8,128)(2,1)} %bitcast.100, ...), kind=kOutput, calls=%fused_computation.103 | convolution fusion | flops 3781753344 | bytes 13779968 | tf_op jit(solution)/shard_map/dot_general | solution.py:166
  183.5 228.1 %reduce-scatter.2.cloned.1.call-done = f32[40,2560]{1,0:T(8,128)} async-done(((f32[1280,2560]{1,0:T(8,128)}), f32[40,2560]{1,0:T(8,128)}) %reduce-scatter.2.cloned.1.call-update) | async-done | bytes 409616 | tf_op jit(solution)/shard_map/reduce_scatter | solution.py:186
  411.6 0.0 all-reduce.2.cloned.1.call-update
  411.7 4.4 fusion.17
  416.0 63.8 %all-reduce.2.cloned.1.call-done = f32[40,2560]{1,0:T(8,128)} async-done(((f32[40,2560]{1,0:T(8,128)}), f32[40,2560]{1,0:T(8,128)}) %all-reduce.2.cloned.1.call-update) | async-done | bytes 409616 | tf_op jit(solution)/shard_map/psum | solution.py:189
  479.8 1.0 broadcast_multiply_fusion
  480.9 0.7 slice.26
  481.6 0.6 slice.27
  (18 shorter events, 0.1 us)
Async XLA Ops:
  7.2 80.4 %all-gather.3.cloned.1.call-start = ((), (), s32[]{:S(2)}) async-start(), calls=%async_computation.2 | async-start | bytes 1689600 | tf_op jit(solution)/shard_map/all_gather | solution.py:155
  16.5 8.4 %copy-start.4 = (s32[1,32]{1,0:T(1,128)S(1)}, s32[1,32]{1,0:T(1,128)}, u32[]{:S(2)}) copy-start(s32[1,32]{1,0:T(1,128)} %param.13) | copy-start | bytes 388
  16.5 8.7 %copy-start = (bf16[768,1280]{1,0:T(8,128)(2,1)S(1)}, bf16[768,1280]{1,0:T(8,128)(2,1)}, u32[]{:S(2)}) copy-start(bf16[768,1280]{1,0:T(8,128)(2,1)} %param.10) | copy-start | bytes 5898244
  16.5 39.7 %all-to-all-start = ((bf16[8,128,1280]{2,1,0:T(8,128)(2,1)}), bf16[8,128,1280]{2,1,0:T(8,128)(2,1)}, u32[]{:S(2)}, u32[]{:S(2)}) async-start(bf16[8,128,1280]{2,1,0:T(8,128)(2,1)} %copy.27), calls=%async_computation | async-start | bytes 5242880 | tf_op jit(solution)/shard_map/all_to_all | solution.py:141
  24.1 149.5 %all-gather.5.cloned.1.call-start = ((), (), s32[]{:S(2)}) async-start(), calls=%async_computation.3 | async-start | bytes 5068800 | tf_op jit(solution)/shard_map/all_gather | solution.py:168
  24.9 386.8 %reduce-scatter.2.cloned.1.call-start = ((), (), s32[]{:S(2)}) async-start(), calls=%async_computation.4 | async-start | bytes 13516800 | tf_op jit(solution)/shard_map/reduce_scatter | solution.py:186
  87.5 11.4 %slice-start = ((s8[9437184]{0:T(1024)(128)(4,1)}), s8[4194304]{0:T(1024)(128)(4,1)S(1)}, s32[]{:S(2)}) async-start(s8[9437184]{0:T(1024)(128)(4,1)} %bitcast.87), calls=%async_computation.6 | async-start | bytes 8388608
  87.5 11.4 %slice-start.1 = ((s8[9437184]{0:T(1024)(128)(4,1)}), s8[4194304]{0:T(1024)(128)(4,1)S(1)}, s32[]{:S(2)}) async-start(s8[9437184]{0:T(1024)(128)(4,1)} %bitcast.87), calls=%async_computation.7 | async-start | bytes 8388608
  91.2 7.7 %slice-start.2 = ((s8[9437184]{0:T(1024)(128)(4,1)}), s8[1048576]{0:T(1024)(128)(4,1)S(1)}, s32[]{:S(2)}) async-start(s8[9437184]{0:T(1024)(128)(4,1)} %bitcast.87), calls=%async_computation.8 | async-start | bytes 2097152
  119.6 2.1 copy-start.1
  119.6 2.4 copy-start.3
  121.5 2.2 copy-start.2
  121.9 1.8 copy-start.5
  121.9 1.8 copy-start.6
  133.8 346.0 %all-reduce.2.cloned.1.call-start = ((), (), s32[]{:S(2)}) async-start(), calls=%async_computation.5 | async-start | bytes 819200 | tf_op jit(solution)/shard_map/psum | solution.py:189
Sparse Core Ops, SparseCore 0:
  10.6 76.8 all-gather.2
  90.1 83.4 all-gather.4
  177.8 233.8 reduce-scatter.1
  413.8 65.9 all-reduce.1
where the time goes:
time: 491 us; the launch traced here: 489 us
  waiting for transfers between devices  351 us (71%)
  matrix products  64.9 us (13%)
  other arithmetic  29.3 us (6%)
  local copies, waits for them, and re-layouts  21.3 us (4%)
  between operations  13.9 us (3%)
  starting transfers between devices  8.03 us (2%)
    reduce_scatter x1, waiting for transfers between devices, on_device(): lax.psum_scatter(jnp.concatenate([qkv_part, out_part], axis=1), 'dp', sca...  228 us
    psum x1, waiting for transfers between devices, on_device(): reduced = lax.psum(reduced, 'section')  63.8 us
    all_gather x1, waiting for transfers between devices, on_device(): lax.all_gather(w_qkv, 'dp', axis=0, tiled=True)  39.5 us
    all_gather x1, waiting for transfers between devices, on_device(): lax.all_gather(w_out, 'dp', axis=0, tiled=True)  16.4 us
    convert_element_type x1, other arithmetic, attend(): weights = probabilities.astype(jnp.bfloat16)  11.5 us
    sub x1, matrix products, attend(): shifted = jnp.exp(scores - jnp.max(scores, axis=2, keepdims=True))  11.4 us
    dot_general x1, matrix products, on_device(): lax.dot_general(dqkv, lax.all_gather(w_qkv, 'dp', axis=0, tiled=True), ((...  9.88 us
  transfers between devices with their start and end apart: 5, of which 5 were waited for; matrix products, arithmetic and copies ran while one was open for 23% of the time, Pallas kernels for 0%

commit v1 on v0

v1 whole, which is shorter than its diff:
```python
import functools
import math

import jax
import jax.numpy as jnp
from jax import lax
from jax.experimental import pallas as pl
from jax.experimental.pallas import tpu as pltpu
from jax.sharding import Mesh, PartitionSpec as P

HEADS = 8
HEAD_DIM = 80
TILE = 128
WINDOW = 2 * TILE
HW = HEADS * HEAD_DIM
SCALE = 1.0 / math.sqrt(HEAD_DIM)
BLOCKS = 4
AXES = {"y": 4, "z": 8, "x": 4, "core": 2}
VMEM_LIMIT = 56 * 1024 * 1024

norm_eps = 1e-06
f32 = jnp.float32
bf16 = jnp.bfloat16

SOURCE, START, JOINED, META = 0, 8, 16, 24


def lane_window(head):
    first, last = head * HEAD_DIM, (head + 1) * HEAD_DIM
    return first // 128 * 128, -(-last // 128) * 128


def params():
    return pltpu.CompilerParams(vmem_limit_bytes=VMEM_LIMIT)


def cost(flops, moved):
    return pl.CostEstimate(flops=flops, bytes_accessed=moved, transcendentals=0)


def route_kernel(patches, owners, place, rows, table, *rest, own_tiles, src_tiles, sections):
    outgoing = rest[:sections]
    used, segment, own_partner, sems = rest[sections:]
    me = place[0]
    for j in range(8):
        used[j] = 0
        segment[j] = -1
        table[SOURCE + j] = -1
    for j in range(src_tiles):
        own_partner[j] = 0

    def image(i, begin):
        count = patches[0, i] // TILE
        owner = owners[0, i]
        slot = used[owner]
        used[owner] = slot + count
        for t in range(2):

            @pl.when(t < count)
            def _():
                position = begin + t
                source = position // src_tiles

                @pl.when(owner == me)
                def _():
                    table[SOURCE + slot + t] = source ^ me
                    segment[slot + t] = i

                @pl.when(source == me)
                def _():
                    own_partner[position % src_tiles] = owner ^ me

        return begin + count

    lax.fori_loop(0, patches.shape[1], image, jnp.int32(0))
    copies = []
    for j in range(src_tiles):
        for k in range(sections):
            copy = pltpu.make_async_copy(rows.at[pl.ds(j * TILE, TILE)], outgoing[k], sems.at[j])
            pl.when(own_partner[j] == k)(copy.start)
        copies.append(copy)

    last = own_tiles - 1
    for b in range(8):
        table[START + b] = 0
        table[JOINED + b] = 0
        table[META + b] = 0
    table[META + 1] = place[1]
    at = jnp.int32(0)
    count = jnp.int32(0)
    lone = jnp.int32(0)

    def block(_, carry):
        at, count, lone = carry
        here = segment[at]
        after = segment[jnp.minimum(at + 1, last)]
        beyond = segment[jnp.minimum(at + 2, last)]
        joined = here == after
        splits = (at + 2 <= last) & (after == beyond) & jnp.logical_not(joined)
        active = at <= last
        is_lone = at == last

        @pl.when(active & jnp.logical_not(is_lone))
        def _():
            table[START + 1 + count] = at
            table[JOINED + 1 + count] = joined.astype(jnp.int32)

        @pl.when(is_lone)
        def _():
            table[START] = last - 1
            table[JOINED] = (segment[last - 1] == here).astype(jnp.int32)

        step = jnp.where(splits, 1, 2)
        return (
            jnp.where(active, at + step, at),
            count + jnp.where(active & jnp.logical_not(is_lone), 1, 0),
            lone | is_lone.astype(jnp.int32),
        )

    at, count, lone = lax.fori_loop(0, BLOCKS, block, (at, count, lone))
    table[META] = count
    table[META + 2] = lone
    for copy in copies:
        copy.wait()


def route(patches, owners, place, rows, own_tiles, sections):
    src_tiles = rows.shape[0] // TILE
    smem = pl.BlockSpec(memory_space=pltpu.SMEM)
    hbm = pl.BlockSpec(memory_space=pl.ANY)
    return pl.pallas_call(
        functools.partial(
            route_kernel, own_tiles=own_tiles, src_tiles=src_tiles, sections=sections
        ),
        out_shape=(
            jax.ShapeDtypeStruct((32,), jnp.int32),
            *(jax.ShapeDtypeStruct((TILE, rows.shape[1]), bf16) for _ in range(sections)),
        ),
        in_specs=[smem, smem, smem, pl.BlockSpec(memory_space=pltpu.VMEM)],
        out_specs=(smem, *(hbm for _ in range(sections))),
        scratch_shapes=[
            pltpu.SMEM((8,), jnp.int32),
            pltpu.SMEM((8,), jnp.int32),
            pltpu.SMEM((src_tiles,), jnp.int32),
            pltpu.SemaphoreType.DMA((src_tiles,)),
        ],
        compiler_params=params(),
        cost_estimate=cost(0, 4 * rows.size),
        name="route",
    )(patches, owners, place, rows)


def norm_kernel(x, gain, bias, out):
    wide = x[...].astype(f32)
    average = jnp.mean(wide, axis=1, keepdims=True)
    centered = wide - average
    inv_scale = lax.rsqrt(jnp.mean(centered * centered, axis=1, keepdims=True) + norm_eps)
    normed = centered * inv_scale * gain[...] + bias[...]
    out[...] = jnp.transpose(normed.astype(bf16))


def norm_transposed(x, gain, bias):
    rows, width = x.shape
    return pl.pallas_call(
        norm_kernel,
        grid=(rows // TILE,),
        out_shape=jax.ShapeDtypeStruct((width, rows), bf16),
        in_specs=[
            pl.BlockSpec((TILE, width), lambda t: (t, 0)),
            pl.BlockSpec((1, width), lambda t: (0, 0)),
            pl.BlockSpec((1, width), lambda t: (0, 0)),
        ],
        out_specs=pl.BlockSpec((width, TILE), lambda t: (0, t)),
        compiler_params=params(),
        cost_estimate=cost(20 * rows * width, 4 * rows * width),
        name="norm",
    )(x, gain.reshape(1, width), bias.reshape(1, width))


def padded_rows(values, head):
    low, high = lane_window(head)
    first = head * HEAD_DIM
    parts = []
    if first > low:
        parts.append(jnp.zeros((first - low, values.shape[1]), values.dtype))
    parts.append(values[first : first + HEAD_DIM])
    if high > first + HEAD_DIM:
        parts.append(jnp.zeros((high - first - HEAD_DIM, values.shape[1]), values.dtype))
    return jnp.concatenate(parts, axis=0) if len(parts) > 1 else parts[0]


def lane_mask(head):
    low, high = lane_window(head)
    lanes = lax.broadcasted_iota(jnp.int32, (1, high - low), 1) + low
    return ((lanes >= head * HEAD_DIM) & (lanes < (head + 1) * HEAD_DIM)).astype(f32).astype(bf16)


def matmul(a, b):
    return lax.dot_general(a, b, (((1,), (0,)), ((), ())), preferred_element_type=f32)


def block_is_used(table, b):
    return jnp.where(b == 0, table[META + 2], (b <= table[META]).astype(jnp.int32)) == 1


def forward_kernel(table, qkv, attended, attended_t, probabilities):
    b = pl.program_id(0)

    @pl.when(block_is_used(table, b))
    def _():
        start = pl.multiple_of(table[START + b] * TILE, TILE)
        rows = pl.ds(start, WINDOW)
        joined = table[JOINED + b] == 1
        key_tile = lax.broadcasted_iota(jnp.int32, (WINDOW, WINDOW), 0) // TILE
        query_tile = lax.broadcasted_iota(jnp.int32, (WINDOW, WINDOW), 1) // TILE
        kept = (key_tile == query_tile) | joined
        queries_t = jnp.transpose(qkv[rows, 0:HW])
        values_t = jnp.transpose(qkv[rows, 2 * HW : 3 * HW])
        heads = []
        for h in range(HEADS):
            low, high = lane_window(h)
            scores = matmul(qkv[rows, HW + low : HW + high], padded_rows(queries_t, h)) * SCALE
            scores = jnp.where(kept, scores, -jnp.inf)
            shifted = jnp.exp(scores - jnp.max(scores, axis=0, keepdims=True))
            probs = shifted * (1.0 / jnp.sum(shifted, axis=0, keepdims=True))
            probabilities[0, h] = probs
            heads.append(
                matmul(values_t[h * HEAD_DIM : (h + 1) * HEAD_DIM], probs.astype(bf16)).astype(bf16)
            )
        whole = jnp.concatenate(heads, axis=0)
        attended_t[0] = whole
        attended[rows, :] = jnp.transpose(whole)


def forward(table, qkv):
    rows, width = qkv.shape
    return pl.pallas_call(
        forward_kernel,
        grid_spec=pltpu.PrefetchScalarGridSpec(
            num_scalar_prefetch=1,
            grid=(BLOCKS + 1,),
            in_specs=[pl.BlockSpec((rows, width), lambda b, t: (0, 0))],
            out_specs=(
                pl.BlockSpec((rows, HW), lambda b, t: (0, 0)),
                pl.BlockSpec((1, HW, WINDOW), lambda b, t: (b, 0, 0)),
                pl.BlockSpec((1, HEADS, WINDOW, WINDOW), lambda b, t: (b, 0, 0, 0)),
            ),
        ),
        out_shape=(
            jax.ShapeDtypeStruct((rows, HW), bf16),
            jax.ShapeDtypeStruct((BLOCKS + 1, HW, WINDOW), bf16),
            jax.ShapeDtypeStruct((BLOCKS + 1, HEADS, WINDOW, WINDOW), f32),
        ),
        compiler_params=params(),
        cost_estimate=cost(8 * 10**9, 20 * 10**6),
        name="attend",
    )(table, qkv)


def incoming_kernel(table, own_w, mate_w, normed_t, *rest, sections, tiles):
    arrived = rest[:sections]
    incoming, d_attn, left_own, left_send, landing, sems = rest[sections:]
    t = pl.program_id(0)

    @pl.when(t == 0)
    def _():
        for j in range(tiles):
            for k in range(sections):
                copy = pltpu.make_async_copy(arrived[k], landing.at[j], sems.at[j])
                pl.when(table[SOURCE + j] == k)(copy.start)

    held = table[SOURCE + t] >= 0

    @pl.when(held)
    def _():
        pltpu.make_async_copy(arrived[0], landing.at[t], sems.at[t]).wait()

    rows = jnp.where(held, landing[t], jnp.zeros(landing.shape[1:], bf16))
    incoming[...] = rows
    rows_t = jnp.transpose(rows)
    first = table[META + 1] == 0
    left_own[...] = jnp.where(first, normed_t[...], rows_t)
    left_send[...] = jnp.where(first, rows_t, normed_t[...])

    @pl.when(first)
    def _():
        d_attn[:, 0:384] = matmul(rows, own_w[...]).astype(bf16)
        d_attn[:, 384:640] = matmul(rows, mate_w[:, 128:384]).astype(bf16)

    @pl.when(jnp.logical_not(first))
    def _():
        d_attn[:, 0:384] = matmul(rows, mate_w[...]).astype(bf16)
        d_attn[:, 384:640] = matmul(rows, own_w[:, 128:384]).astype(bf16)


def place_incoming(table, arrived, own_w, mate_w, normed_t):
    width, rows = normed_t.shape
    sections, tiles = len(arrived), rows // TILE
    tall = pl.BlockSpec((width, TILE), lambda i, t: (0, i))
    half = pl.BlockSpec((width, 384), lambda i, t: (0, 0))
    return pl.pallas_call(
        functools.partial(incoming_kernel, sections=sections, tiles=tiles),
        grid_spec=pltpu.PrefetchScalarGridSpec(
            num_scalar_prefetch=1,
            grid=(tiles,),
            in_specs=[half, half, tall] + [pl.BlockSpec(memory_space=pl.ANY)] * sections,
            out_specs=(
                pl.BlockSpec((TILE, width), lambda i, t: (i, 0)),
                pl.BlockSpec((TILE, HW), lambda i, t: (i, 0)),
                tall,
                tall,
            ),
            scratch_shapes=[
                pltpu.VMEM((tiles, TILE, width), bf16),
                pltpu.SemaphoreType.DMA((tiles,)),
            ],
        ),
        out_shape=(
            jax.ShapeDtypeStruct((rows, width), bf16),
            jax.ShapeDtypeStruct((rows, HW), bf16),
            jax.ShapeDtypeStruct((width, rows), bf16),
            jax.ShapeDtypeStruct((width, rows), bf16),
        ),
        compiler_params=params(),
        cost_estimate=cost(2 * rows * width * HW, 14 * rows * width),
        name="incoming",
    )(table, own_w, mate_w, normed_t, *arrived)


def backward_kernel(
    table,
    qkv,
    d_attn,
    attended,
    attended_t,
    probabilities,
    dqkv,
    first_own,
    first_send,
    second_own,
    second_send,
):
    b = pl.program_id(0)

    @pl.when(block_is_used(table, b))
    def _():
        start = pl.multiple_of(table[START + b] * TILE, TILE)
        rows = pl.ds(start, WINDOW)
        grad = d_attn[rows, :]
        grad_t = jnp.transpose(grad)
        keys_t = jnp.transpose(qkv[rows, HW : 2 * HW])
        query_grads = []
        key_tiles = [None] * (HW // 128)
        value_tiles = [None] * (HW // 128)

        def add(tiles, low, part):
            for j in range(part.shape[1] // 128):
                at = low // 128 + j
                piece = part[:, j * 128 : (j + 1) * 128]
                tiles[at] = piece if tiles[at] is None else tiles[at] + piece

        for h in range(HEADS):
            low, high = lane_window(h)
            mine = slice(h * HEAD_DIM, (h + 1) * HEAD_DIM)
            mask = lane_mask(h)
            probs = probabilities[0, h]
            prob_grad = matmul(qkv[rows, 2 * HW + low : 2 * HW + high], padded_rows(grad_t, h))
            row_delta = jnp.sum(
                grad_t[mine].astype(f32) * attended_t[0, mine].astype(f32), axis=0, keepdims=True
            )
            dscore = (probs * (prob_grad - row_delta) * SCALE).astype(bf16)
            query_grads.append(matmul(keys_t[mine], dscore).astype(bf16))
            add(key_tiles, low, matmul(dscore, qkv[rows, low:high] * mask))
            add(value_tiles, low, matmul(probs.astype(bf16), grad[:, low:high] * mask))
        dqkv[rows, 0:HW] = jnp.transpose(jnp.concatenate(query_grads, axis=0))
        for j in range(HW // 128):
            dqkv[rows, HW + j * 128 : HW + (j + 1) * 128] = key_tiles[j].astype(bf16)
            dqkv[rows, 2 * HW + j * 128 : 2 * HW + (j + 1) * 128] = value_tiles[j].astype(bf16)

    @pl.when(b == BLOCKS)
    def _():
        first = table[META + 1] == 0
        d_query, d_key, d_value = (dqkv[:, i * HW : (i + 1) * HW] for i in range(3))
        first_own[...] = jnp.where(first, d_value, attended[...])
        first_send[...] = jnp.where(first, attended[...], d_value)
        second_own[...] = jnp.where(first, d_query, d_key)
        second_send[...] = jnp.where(first, d_key, d_query)


def backward(table, qkv, d_attn, attended, attended_t, probabilities):
    rows, width = qkv.shape
    whole = pl.BlockSpec((rows, HW), lambda b, t: (0, 0))
    return pl.pallas_call(
        backward_kernel,
        grid_spec=pltpu.PrefetchScalarGridSpec(
            num_scalar_prefetch=1,
            grid=(BLOCKS + 1,),
            in_specs=[
                pl.BlockSpec((rows, width), lambda b, t: (0, 0)),
                whole,
                whole,
                pl.BlockSpec((1, HW, WINDOW), lambda b, t: (b, 0, 0)),
                pl.BlockSpec((1, HEADS, WINDOW, WINDOW), lambda b, t: (b, 0, 0, 0)),
            ],
            out_specs=(pl.BlockSpec((rows, width), lambda b, t: (0, 0)), whole, whole, whole, whole),
        ),
        out_shape=(
            jax.ShapeDtypeStruct((rows, width), bf16),
            *(jax.ShapeDtypeStruct((rows, HW), bf16) for _ in range(4)),
        ),
        compiler_params=params(),
        cost_estimate=cost(12 * 10**9, 25 * 10**6),
        name="attend_back",
    )(table, qkv, d_attn, attended, attended_t, probabilities)


def weight_kernel(left_own, left_mate, right_own, right_mate, out):
    total = matmul(left_own[...], right_own[...]) + matmul(left_mate[...], right_mate[...])
    rows = total.shape[0]
    group = rows // 4
    fifth = total[:, 512:640]
    quarter = lax.broadcasted_iota(jnp.int32, (group, 128), 1) // 32
    for x in range(4):
        packed = jnp.zeros((group, 128), f32)
        for g in range(4):
            piece = fifth[g * group : (g + 1) * group]
            shift = (g - x) * 32 % 128
            packed = jnp.where(quarter == g, pltpu.roll(piece, shift, 1) if shift else piece, packed)
        out[x, 0:rows] = total[:, x * 128 : (x + 1) * 128].astype(bf16)
        out[x, rows:] = packed.astype(bf16)


def weight_part(left_own, left_mate, right_own, right_mate, y_first):
    width, rows = left_own.shape
    piece = width // 4
    packed = piece * 5 // 4
    left = pl.BlockSpec((piece, rows), lambda i: (i, 0))
    right = pl.BlockSpec((rows, HW), lambda i: (0, 0))
    if y_first:
        out_spec = pl.BlockSpec((None, 4, packed, 128), lambda i: (i, 0, 0, 0))
    else:
        out_spec = pl.BlockSpec((4, None, packed, 128), lambda i: (0, i, 0, 0))
    return pl.pallas_call(
        weight_kernel,
        grid=(4,),
        out_shape=jax.ShapeDtypeStruct((4, 4, packed, 128), bf16),
        in_specs=[left, left, right, right],
        out_specs=out_spec,
        compiler_params=params(),
        cost_estimate=cost(4 * width * rows * HW, 4 * width * rows + 2 * width * HW),
        name="weight_part",
    )(left_own, left_mate, right_own, right_mate)


def unpacked(part):
    rest = part[320:]
    return jnp.concatenate(
        [part[:320], jnp.concatenate([rest[:, i * 32 : (i + 1) * 32] for i in range(4)], axis=0)], axis=1
    )


def to_mate(value):
    return lax.ppermute(value, "core", [(0, 1), (1, 0)])


def permuted_sum(value, axis):
    count = AXES[axis]
    here = lax.axis_index(axis)
    parts = [lax.dynamic_index_in_dim(value, here, 0, keepdims=False)]
    for k in range(1, count):
        part = lax.dynamic_index_in_dim(value, lax.rem(here + k, count), 0, keepdims=False)
        parts.append(lax.ppermute(part, axis, [(i, (i + k) % count) for i in range(count)]))
    return sum(part.astype(f32) for part in parts)


def exchanged(value, axes):
    return lax.all_to_all(value, axes, split_axis=0, concat_axis=0, tiled=True)


def on_device(
    grad_rows,
    layer_input,
    saved_qkv,
    image_patches,
    image_owner,
    norm_gain,
    norm_bias,
    w_qkv,
    w_out,
):
    width = layer_input.shape[1]
    own_tiles = layer_input.shape[0] // TILE
    section = ("x", "core")
    sections = AXES["x"] * AXES["core"]
    core = lax.axis_index("core")
    place = jnp.stack([lax.axis_index(section), core]).astype(jnp.int32)

    table, *outgoing = route(image_patches, image_owner, place, grad_rows, own_tiles, sections)
    all_w_qkv = lax.all_gather(w_qkv, ("y", "z"), axis=0, tiled=True)
    arrived = [outgoing[0]] + [
        lax.ppermute(outgoing[k], section, [(i, i ^ k) for i in range(sections)])
        for k in range(1, sections)
    ]
    w_out, _ = lax.optimization_barrier((w_out, table))
    half_w = lax.dynamic_slice_in_dim(w_out, 256 * core, 384, axis=1)
    half_w = exchanged(jnp.broadcast_to(half_w, (32,) + half_w.shape), ("y", "z"))
    half_w = half_w.reshape(width, 384)
    mate_w = to_mate(half_w)

    normed_t = norm_transposed(layer_input, norm_gain, norm_bias)
    mate_normed_t = to_mate(normed_t)
    attended, attended_t, probabilities = forward(table, saved_qkv)

    incoming, d_attn, left_own, left_send = place_incoming(table, arrived, half_w, mate_w, normed_t)
    left_mate = to_mate(left_send)
    dqkv, first_own, first_send, second_own, second_send = backward(
        table, saved_qkv, d_attn, attended, attended_t, probabilities
    )
    first_mate, second_mate = to_mate(first_send), to_mate(second_send)
    first = weight_part(left_own, left_mate, first_own, first_mate, True)
    second = weight_part(normed_t, mate_normed_t, second_own, second_mate, False)
    layer_grad = norm_back(layer_input, incoming, norm_gain, dqkv, all_w_qkv)

    first = jnp.sum(exchanged(first, "y").astype(f32), axis=0).astype(bf16)
    second = permuted_sum(second, "x").astype(bf16)
    first, second, layer_grad = lax.optimization_barrier((first, second, layer_grad))
    first = permuted_sum(first, "x")
    second = jnp.sum(exchanged(second, "y").astype(f32), axis=0)
    columns = jnp.concatenate([unpacked(first), unpacked(second)], axis=1)
    by_z = exchanged(columns.astype(bf16).reshape(8, 40, 320), "z")
    share = jnp.sum(by_z.astype(f32), axis=0) / (AXES["y"] * AXES["z"] * sections)
    shares = exchanged(jnp.broadcast_to(share, (sections,) + share.shape), section)

    def assemble(core, first_column):
        mine = [shares[2 * x + core][:, first_column : first_column + 160] for x in range(4)]
        return [part[:, :128] for part in mine] + [part[:, 128:] for part in mine]

    qkv_weight_grad = jnp.concatenate(assemble(0, 160) + assemble(1, 160) + assemble(0, 0), axis=1)
    out_weight_grad = jnp.concatenate(assemble(1, 0), axis=1)
    return layer_grad, qkv_weight_grad, out_weight_grad


def norm_back(layer_input, incoming, norm_gain, dqkv, w_qkv):
    widened = layer_input.astype(f32)
    average = jnp.mean(widened, axis=1, keepdims=True)
    centered = widened - average
    inv_scale = lax.rsqrt(jnp.mean(centered * centered, axis=1, keepdims=True) + norm_eps)
    normalized = centered * inv_scale
    dnormed = lax.dot_general(dqkv, w_qkv, (((1,), (1,)), ((), ())), preferred_element_type=f32)
    scaled_grad = dnormed * norm_gain
    branch = inv_scale * (
        scaled_grad
        - jnp.mean(scaled_grad, axis=1, keepdims=True)
        - normalized * jnp.mean(scaled_grad * normalized, axis=1, keepdims=True)
    )
    return (incoming.astype(f32) + branch).astype(bf16)


def solution(mesh):
    fine = Mesh(mesh.devices.reshape(tuple(AXES.values())), tuple(AXES))
    rows = P(("y", "z", "x", "core"), None)
    dp = P(("y", "z"), None)
    return jax.shard_map(
        on_device,
        mesh=fine,
        in_specs=(rows, rows, rows, dp, dp, P(), P(), dp, dp),
        out_specs=(rows, dp, dp),
        check_vma=False,
    )
```

time: 491 us -> 235 us (0.48)
  waiting for transfers between devices: 351 us -> 54.5 us
  Pallas kernels: 0 us -> 66.7 us
  matrix products: 64.9 us -> 8.07 us
  starting transfers between devices: 8.03 us -> 43 us
  blocking collectives: 0 us -> 29.5 us
  other arithmetic: 29.3 us -> 8.17 us
  local copies, waits for them, and re-layouts: 21.3 us -> 10.3 us
    reduce_scatter x1 -> x0, waiting for transfers between devices: 228 us -> none  [on_device(): lax.psum_scatter(jnp.concatenate([qkv_part, out_part], axis=1), 'dp', sca...]
    pallas_call x0 -> x7, Pallas kernels: none -> 66.7 us  [the longest x1 17.1 us: backward(): pl.pallas_call(backward_kernel, grid_spec=pltpu.PrefetchScalarGridSpec(nu...]
    psum x1 -> x0, waiting for transfers between devices: 63.8 us -> none  [on_device(): reduced = lax.psum(reduced, 'section')]
    all_gather x2 -> x1, waiting for transfers between devices: 55.9 us -> 0.02 us  [on_device(): all_w_qkv = lax.all_gather(w_qkv, ('y', 'z'), axis=0, tiled=True)]
    dot_general x11 -> x1, matrix products: 53.5 us -> 8.07 us  [norm_back(): lax.dot_general(dqkv, w_qkv, (((1,), (1,)), ((), ())), preferred_element_...]
    all_to_all x0 -> x2, blocking collectives: none -> 29.5 us  [exchanged(): return lax.all_to_all(value, axes, split_axis=0, concat_axis=0, tiled=True)]
    all_to_all x1 -> x3, waiting for transfers between devices: 2.03 us -> 30.6 us  [exchanged(): return lax.all_to_all(value, axes, split_axis=0, concat_axis=0, tiled=True)]
    ppermute x0 -> x18, waiting for transfers between devices: none -> 23.2 us  [the longest x6 18.5 us: permuted_sum(): lax.ppermute(part, axis, [(i, (i + k) % count) for i in range(count)])]
  transfers between devices with their start and end apart: 5 -> 22, of which waited for: 5 -> 7; matrix products, arithmetic and copies ran while one was open for 23% -> 4% of each run, Pallas kernels for 0% -> 28%
where the time goes in v1:
time: 235 us
  Pallas kernels  66.7 us (28%)
  waiting for transfers between devices  54.5 us (23%)
  starting transfers between devices  43 us (18%)
  blocking collectives  29.5 us (13%)
  between operations  14.4 us (6%)
  local copies, waits for them, and re-layouts  10.3 us (4%)
  other arithmetic  8.17 us (3%)
  matrix products  8.07 us (3%)
    all_to_all x3, waiting for transfers between devices, exchanged(): return lax.all_to_all(value, axes, split_axis=0, concat_axis=0, tiled=True)  30.6 us
    all_to_all x2, blocking collectives, exchanged(): return lax.all_to_all(value, axes, split_axis=0, concat_axis=0, tiled=True)  29.5 us
    all_to_all x3, starting transfers between devices, exchanged(): return lax.all_to_all(value, axes, split_axis=0, concat_axis=0, tiled=True)  20.5 us
    ppermute x6, waiting for transfers between devices, permuted_sum(): lax.ppermute(part, axis, [(i, (i + k) % count) for i in range(count)])  18.5 us
    pallas_call x1, Pallas kernels, backward(): pl.pallas_call(backward_kernel, grid_spec=pltpu.PrefetchScalarGridSpec(nu...  17.1 us
    pallas_call x1, Pallas kernels, forward(): pl.pallas_call(forward_kernel, grid_spec=pltpu.PrefetchScalarGridSpec(num...  16.4 us
    pallas_call x2, Pallas kernels, weight_part(): pl.pallas_call(weight_kernel, grid=(4,), out_shape=jax.ShapeDtypeStruct((...  14 us
    pallas_call x1, Pallas kernels, place_incoming(): pl.pallas_call(functools.partial(incoming_kernel, sections=sections, tile...  9.61 us
  transfers between devices with their start and end apart: 22, of which 7 were waited for; matrix products, arithmetic and copies ran while one was open for 4% of the time, Pallas kernels for 28%

profile of v1, /device:TPU:1, one launch (start us, length us, event | category | flops | bytes accessed | tf_op | source)
XLA Modules:
  0.0 234.6 jit_solution(13492600172864944668)
XLA Ops:
  7.2 0.7 all-gather.2.cloned.1.call-update
  7.9 0.6 pad_add_fusion.place
  8.5 3.9 %route.1 = (s32[32]{0:T(128)}, bf16[128,1280]{1,0:T(8,128)(2,1)}, bf16[128,1280]{1,0:T(8,128)(2,1)}, bf16[128,1280]{1,0:T(8,128)(2,1)}, bf16[128,1280]{1,0:T(8,1...) custom-call(s32[1,32]{1,0:T(1,128)} %patches.1, ...), custom_call_target="tpu_custom_call" | custom-call | bytes 2621440 | tf_op jit(solution)/shard_map/route/pallas_call | solution.py:131
  12.4 1.0 broadcast_in_dim.4
  13.4 12.1 %all-to-all-start = ((bf16[32,40,384]{2,1,0:T(8,128)(2,1)}), bf16[32,40,384]{2,1,0:T(8,128)(2,1)S(1)}, u32[]{:S(2)}, u32[]{:S(2)}) async-start(bf16[32,40,384]{2,1,0:T(8,128)(2,1)} %broadcast_in_dim.4), calls=%async_computation | async-start | bytes 1966080 | tf_op jit(solution)/shard_map/all_to_all | solution.py:477
  25.5 1.0 collective-permute-start.1
  26.5 1.2 collective-permute-start.2
  27.7 0.5 collective-permute-start.3
  28.3 25.2 %all-to-all-done = bf16[32,40,384]{2,1,0:T(8,128)(2,1)S(1)} async-done(((bf16[32,40,384]{2,1,0:T(8,128)(2,1)}), bf16[32,40,384]{2,1,0:T(8,128)(2,1)S(1)}, u32[]{:S(2)}, u32[]{:S(2)}) %all-to-all-start) | async-done | bytes 983072 | tf_op jit(solution)/shard_map/all_to_all | solution.py:477
  53.4 5.5 %collective-permute-start = (bf16[1280,384]{1,0:T(8,128)(2,1)S(1)}, bf16[1280,384]{1,0:T(8,128)(2,1)S(1)}, u32[]{:S(2)}, u32[]{:S(2)}) collective-permute-start(bf16[1280,384]{1,0:T(8,128)(2,1)S(1)} %bitcast.43), channel_id=1, source_target_pairs={{0,1},{1,0},{2,3},{3,2},{4,5},{5,4},{6,7},{7,6},{8,9},{9,8},{10,11... | collective-permute-start | bytes 2949128 | tf_op jit(solution)/shard_map/ppermute | solution.py:463
  59.0 2.0 collective-permute-start.4
  61.0 1.1 collective-permute-start.5
  62.1 2.2 collective-permute-start.6
  64.3 1.0 collective-permute-start.7
  65.3 16.4 %attend.1 = (bf16[768,640]{1,0:T(8,128)(2,1)}, bf16[5,640,256]{2,1,0:T(8,128)(2,1)}, f32[5,8,256,256]{3,2,1,0:T(8,128)}) custom-call(s32[32]{0:T(128)} %get-tuple-element.28.table, bf16[768,1920]{1,0:T(8,128)(2,1)} %qkv.3), custom_call_target="tpu_custom_call" | custom-call | flops 8000000000 | bytes 20000000 | tf_op jit(solution)/shard_map/attend/pallas_call | solution.py:237
  81.7 0.6 reshape.50.gain
  82.3 0.6 reshape.51.bias
  82.9 5.8 %norm.1.normed_t.left_own = bf16[1280,768]{1,0:T(8,128)(2,1)} custom-call(bf16[768,1280]{1,0:T(8,128)(2,1)} %x.1, f32[1,1280]{1,0:T(1,128)} %reshape.50.gain, f32[1,1280]{1,0:T(1,128)} %reshape.51.bias), custom_call_target="tpu_custom_call" | custom-call | flops 19660800 | bytes 3932160 | tf_op jit(solution)/shard_map/norm/pallas_call | solution.py:164
  88.7 0.1 collective-permute-start.10
  88.8 2.7 %collective-permute-done.7.rest_7_ = bf16[128,1280]{1,0:T(8,128)(2,1)S(1)} collective-permute-done((bf16[128,1280]{1,0:T(8,128)(2,1)}, bf16[128,1280]{1,0:T(8,128)(2,1)S(1)}, u32[]{:S(2)}, u32[]{:S(2)}) %collective-permute-start.7) | collective-permute-done | bytes 327712 | tf_op jit(solution)/shard_map/ppermute | solution.py:501
  91.6 0.7 copy-done.12
  92.3 0.4 copy-done.5
  92.7 9.6 %incoming.1 = (bf16[768,1280]{1,0:T(8,128)(2,1)}, bf16[768,640]{1,0:T(8,128)(2,1)}, bf16[1280,768]{1,0:T(8,128)(2,1)}, bf16[1280,768]{1,0:T(8,128)(2,1)}) custom-call(s32[32]{0:T(128)} %get-tuple-element.28.table, bf16[1280,384]{1,0:T(8,128)(2,1)} %bitcast.44, bf16[1280,384]{1,0:T(8,128)(2,1)} %copy-done.5, bf16[1280,768]{1,0:T(8,128)(2,1)} %norm.1.normed_t.left_own, ...), custom_call_target="tpu_custom_call" | custom-call | flops 1258291200 | bytes 13762560 | tf_op jit(solution)/shard_map/incoming/pallas_call | solution.py:301
  102.3 0.5 collective-permute-start.8
  102.8 17.1 %attend_back.1 = (bf16[768,1920]{1,0:T(8,128)(2,1)}, bf16[768,640]{1,0:T(8,128)(2,1)}, bf16[768,640]{1,0:T(8,128)(2,1)}, bf16[768,640]{1,0:T(8,128)(2,1)}, bf16[768,640]{1,0:T(8,128)(2,1)}) custom-call(s32[32]{0:T(128)} %get-tuple-element.28.table, bf16[768,1920]{1,0:T(8,128)(2,1)} %qkv.3, bf16[768,640]{1,0:T(8,128)(2,1)} %get-tuple-element.40.d_attn, ...), custom_call_target="tpu_custom_call" | custom-call | flops 12000000000 | bytes 25000000 | tf_op jit(solution)/shard_map/attend_back/pallas_call | solution.py:393
  119.9 0.2 collective-permute-start.9
  120.1 0.3 collective-permute-start.11
  120.4 0.3 convert_reduce_fusion
  120.7 1.9 collective-permute-done.9.right_mate
  122.7 0.9 copy-done.17
  123.6 0.7 copy-done.15
  124.3 7.0 %weight_part.2 = bf16[4,4,400,128]{3,2,1,0:T(8,128)(2,1)} custom-call(bf16[1280,768]{1,0:T(8,128)(2,1)} %get-tuple-element.38.left_own, bf16[1280,768]{1,0:T(8,128)(2,1)} %copy-done.15, bf16[768,640]{1,0:T(8,128)(2,1)} %get-tuple-element.44.right_own, bf16[768,640]{1,0:T(8,128)(2,1)} %copy-done.17), custom_call_target="tpu_custom_call" | custom-call | flops 2516582400 | bytes 5570560 | tf_op jit(solution)/shard_map/weight_part/pallas_call | solution.py:443
  131.3 4.4 %all-to-all-start.1 = ((bf16[4,4,400,128]{3,2,1,0:T(8,128)(2,1)}), bf16[4,4,400,128]{3,2,1,0:T(8,128)(2,1)}, u32[]{:S(2)}, u32[]{:S(2)}) async-start(bf16[4,4,400,128]{3,2,1,0:T(8,128)(2,1)} %weight_part.2), calls=%async_computation.1 | async-start | bytes 3276800 | tf_op jit(solution)/shard_map/all_to_all | solution.py:477
  135.7 0.9 copy-done.16
  136.7 7.0 %weight_part.3 = bf16[4,4,400,128]{3,2,1,0:T(8,128)(2,1)} custom-call(bf16[1280,768]{1,0:T(8,128)(2,1)} %norm.1.normed_t.left_own, bf16[1280,768]{1,0:T(8,128)(2,1)} %collective-permute-done.10.left_mate, bf16[768,640]{1,0:T(8,128)(2,1)} %get-tuple-element.46.right_own, bf16[768,640]{1,0:T(8,128)(2,1)} %copy-done.16), custom_call_target="tpu_custom_call" | custom-call | flops 2516582400 | bytes 5570560 | tf_op jit(solution)/shard_map/weight_part/pallas_call | solution.py:443
  143.7 1.3 dynamic-slice_bitcast_fusion.2
  145.0 0.1 collective-permute-start.12
  145.1 1.6 collective-permute-start.13
  146.7 1.1 collective-permute-start.14
  147.8 0.6 fusion.9
  148.4 17.5 %collective-permute-done.12 = bf16[4,400,128]{2,1,0:T(8,128)(2,1)S(1)} collective-permute-done((bf16[4,400,128]{2,1,0:T(8,128)(2,1)S(1)}, bf16[4,400,128]{2,1,0:T(8,128)(2,1)S(1)}, u32[]{:S(2)}, u32[]{:S(2)}) %collective-permute-start.12) | collective-permute-done | bytes 409632 | tf_op jit(solution)/shard_map/ppermute | solution.py:472
  165.9 0.3 collective-permute-done.14
  166.2 2.0 fusion.12
  168.2 1.7 reduce_sum.66
  170.0 8.1 %fusion.16 = (f32[768]{0:T(1024)S(1)}, f32[768]{0:T(1024)S(1)}, f32[768,1280]{1,0:T(8,128)S(1)}) fusion(f32[768]{0:T(1024)S(1)} %add_rsqrt_fusion, f32[768]{0:T(1024)S(1)} %broadcast_multiply_fusion.3, bf16[768,1280]{1,0:T(8,128)(2,1)S(1)} %copy-done.2, f32[1280]{0:T(1024)S(1)} %copy-done.14, bf16[768,1920]{1,0:T(8,128)(2,1)} %get-tuple-element.49, ...), kind=kOutput, calls=%fused_computation.46 | convolution fusion | flops 3781753344 | bytes 13779968 | tf_op jit(solution)/shard_map/dot_general | solution.py:549
  178.1 2.5 %fusion.8 = bf16[768,1280]{1,0:T(8,128)(2,1)} fusion(bf16[768,1280]{1,0:T(8,128)(2,1)S(1)} %copy-done.2, f32[768,1280]{1,0:T(8,128)S(1)} %get-tuple-element.109, bf16[768,1280]{1,0:T(8,128)(2,1)S(1)} %copy-done.4, f32[768]{0:T(1024)S(1)} %get-tuple-element.110, f32[768]{0:T(1024)S(1)} %get-tuple-element.111, f32[768]{0:T(1024)S(1)} %add_rsqrt_fusion, ...), kind=kLoop, calls=%fused_computation.11 | loop fusion | flops 9830400 | bytes 9842688 | tf_op jit(solution)/shard_map/convert_element_type | solution.py:556
  180.6 0.9 collective-permute-start.15
  181.5 3.0 %collective-permute-start.16 = (bf16[400,128]{1,0:T(8,128)(2,1)S(1)}, bf16[400,128]{1,0:T(8,128)(2,1)S(1)}, u32[]{:S(2)}, u32[]{:S(2)}) collective-permute-start(bf16[400,128]{1,0:T(8,128)(2,1)S(1)} %get-tuple-element.68), channel_id=1, source_target_pairs={{0,4},{2,6},{4,0},{6,2},{1,5},{3,7},{5,1},{7,3},{8,12},{10,14},{12... | collective-permute-start | bytes 307208 | tf_op jit(solution)/shard_map/ppermute | solution.py:472
  184.5 4.1 %all-to-all-start.2 = ((bf16[4,400,128]{2,1,0:T(8,128)(2,1)}), bf16[4,400,128]{2,1,0:T(8,128)(2,1)S(1)}, u32[]{:S(2)}, u32[]{:S(2)}) async-start(bf16[4,400,128]{2,1,0:T(8,128)(2,1)} %fusion.12), calls=%async_computation.2 | async-start | bytes 819200 | tf_op jit(solution)/shard_map/all_to_all | solution.py:477
  188.7 0.7 collective-permute-done.17
  189.5 0.1 fusion.17
  189.6 5.4 %all-to-all-done.2 = bf16[4,400,128]{2,1,0:T(8,128)(2,1)S(1)} async-done(((bf16[4,400,128]{2,1,0:T(8,128)(2,1)}), bf16[4,400,128]{2,1,0:T(8,128)(2,1)S(1)}, u32[]{:S(2)}, u32[]{:S(2)}) %all-to-all-start.2) | async-done | bytes 409632 | tf_op jit(solution)/shard_map/all_to_all | solution.py:477
  195.1 0.1 fusion.18
  195.2 0.1 pad_maximum_fusion
  195.4 12.9 %all_to_all.25 = bf16[8,40,320]{2,1,0:T(8,128)(2,1)S(1)} all-to-all(bf16[8,40,320]{2,1,0:T(8,128)(2,1)S(1)} %pad_maximum_fusion), channel_id=1, replica_groups=mesh['y'=4,'z'=8,'x'=4,'core'=2] {'z'}, dimensions={0} | all-to-all | bytes 409600 | tf_op jit(solution)/shard_map/all_to_all | solution.py:477
  208.3 16.6 %all_to_all.26 = f32[8,40,320]{2,1,0:T(8,128)S(1)} all-to-all(f32[8,40,320]{2,1,0:T(8,128)S(1)} %broadcast_in_dim.5), channel_id=1, replica_groups=mesh['y'=4,'z'=8,'x'=4,'core'=2] {'x','core'}, dimensions={0} | all-to-all | bytes 819200 | tf_op jit(solution)/shard_map/all_to_all | solution.py:477
  225.0 0.1 fusion.19
  225.0 0.1 fusion.23
  225.2 0.1 fusion.24
  225.5 0.1 fusion.26
  225.6 0.1 fusion.34
  225.7 0.1 fusion.31
  226.1 0.8 concatenate.35
  226.9 0.8 concatenate.34
  (73 shorter events, 1.2 us)
Async XLA Ops:
  7.2 5.2 %copy-start = (bf16[40,640]{1,0:T(8,128)(2,1)S(1)}, bf16[40,640]{1,0:T(8,128)(2,1)}, u32[]{:S(2)}) copy-start(bf16[40,640]{1,0:T(8,128)(2,1)} %param.17) | copy-start | bytes 153604
  7.2 162.8 %all-gather.2.cloned.1.call-start = ((), (), s32[]{:S(2)}) async-start(), calls=%async_computation.5 | async-start | bytes 5068800 | tf_op jit(solution)/shard_map/all_gather | solution.py:499
  13.4 40.0 %all-to-all-start = ((bf16[32,40,384]{2,1,0:T(8,128)(2,1)}), bf16[32,40,384]{2,1,0:T(8,128)(2,1)S(1)}, u32[]{:S(2)}, u32[]{:S(2)}) async-start(bf16[32,40,384]{2,1,0:T(8,128)(2,1)} %broadcast_in_dim.4), calls=%async_computation | async-start | bytes 1966080 | tf_op jit(solution)/shard_map/all_to_all | solution.py:477
  25.5 35.5 %collective-permute-start.1 = (bf16[128,1280]{1,0:T(8,128)(2,1)}, bf16[128,1280]{1,0:T(8,128)(2,1)S(1)}, u32[]{:S(2)}, u32[]{:S(2)}) collective-permute-start(bf16[128,1280]{1,0:T(8,128)(2,1)} %get-tuple-element.31), channel_id=1, source_target_pairs={{0,1},{1,0},{2,3},{3,2},{4,5},{5,4},{6,7},{7,6},{8,9},{9,8},{10,11... | collective-permute-start | bytes 983048 | tf_op jit(solution)/shard_map/ppermute | solution.py:501
  26.5 35.6 %collective-permute-start.2 = (bf16[128,1280]{1,0:T(8,128)(2,1)}, bf16[128,1280]{1,0:T(8,128)(2,1)S(1)}, u32[]{:S(2)}, u32[]{:S(2)}) collective-permute-start(bf16[128,1280]{1,0:T(8,128)(2,1)} %get-tuple-element.32), channel_id=1, source_target_pairs={{0,2},{1,3},{2,0},{3,1},{4,6},{5,7},{6,4},{7,5},{8,10},{9,11},{10,... | collective-permute-start | bytes 983048 | tf_op jit(solution)/shard_map/ppermute | solution.py:501
  27.7 36.5 %collective-permute-start.3 = (bf16[128,1280]{1,0:T(8,128)(2,1)}, bf16[128,1280]{1,0:T(8,128)(2,1)S(1)}, u32[]{:S(2)}, u32[]{:S(2)}) collective-permute-start(bf16[128,1280]{1,0:T(8,128)(2,1)} %get-tuple-element.33), channel_id=1, source_target_pairs={{0,3},{1,2},{2,1},{3,0},{4,7},{5,6},{6,5},{7,4},{8,11},{9,10},{10,... | collective-permute-start | bytes 983048 | tf_op jit(solution)/shard_map/ppermute | solution.py:501
  53.4 28.3 %copy-start.3 = (bf16[32,40,384]{2,1,0:T(8,128)(2,1)}, bf16[32,40,384]{2,1,0:T(8,128)(2,1)S(1)}, u32[]{:S(2)}) copy-start(bf16[32,40,384]{2,1,0:T(8,128)(2,1)S(1)} %all-to-all-done) | copy-start | bytes 2949124
  53.4 38.1 %collective-permute-start = (bf16[1280,384]{1,0:T(8,128)(2,1)S(1)}, bf16[1280,384]{1,0:T(8,128)(2,1)S(1)}, u32[]{:S(2)}, u32[]{:S(2)}) collective-permute-start(bf16[1280,384]{1,0:T(8,128)(2,1)S(1)} %bitcast.43), channel_id=1, source_target_pairs={{0,1},{1,0},{2,3},{3,2},{4,5},{5,4},{6,7},{7,6},{8,9},{9,8},{10,11... | collective-permute-start | bytes 2949128 | tf_op jit(solution)/shard_map/ppermute | solution.py:463
  59.0 29.7 %collective-permute-start.4 = (bf16[128,1280]{1,0:T(8,128)(2,1)}, bf16[128,1280]{1,0:T(8,128)(2,1)S(1)}, u32[]{:S(2)}, u32[]{:S(2)}) collective-permute-start(bf16[128,1280]{1,0:T(8,128)(2,1)} %get-tuple-element.34), channel_id=1, source_target_pairs={{0,4},{1,5},{2,6},{3,7},{4,0},{5,1},{6,2},{7,3},{8,12},{9,13},{10,... | collective-permute-start | bytes 983048 | tf_op jit(solution)/shard_map/ppermute | solution.py:501
  61.0 20.7 %copy-start.6 = (bf16[128,1280]{1,0:T(8,128)(2,1)}, bf16[128,1280]{1,0:T(8,128)(2,1)S(1)}, u32[]{:S(2)}) copy-start(bf16[128,1280]{1,0:T(8,128)(2,1)S(1)} %collective-permute-done.1.rest_1_) | copy-start | bytes 983044
  61.0 27.8 %collective-permute-start.5 = (bf16[128,1280]{1,0:T(8,128)(2,1)}, bf16[128,1280]{1,0:T(8,128)(2,1)S(1)}, u32[]{:S(2)}, u32[]{:S(2)}) collective-permute-start(bf16[128,1280]{1,0:T(8,128)(2,1)} %get-tuple-element.35), channel_id=1, source_target_pairs={{0,5},{1,4},{2,7},{3,6},{4,1},{5,0},{6,3},{7,2},{8,13},{9,12},{10,... | collective-permute-start | bytes 983048 | tf_op jit(solution)/shard_map/ppermute | solution.py:501
  62.1 19.6 %copy-start.7 = (bf16[128,1280]{1,0:T(8,128)(2,1)}, bf16[128,1280]{1,0:T(8,128)(2,1)S(1)}, u32[]{:S(2)}) copy-start(bf16[128,1280]{1,0:T(8,128)(2,1)S(1)} %collective-permute-done.2.rest_2_) | copy-start | bytes 983044
  62.1 26.7 %collective-permute-start.6 = (bf16[128,1280]{1,0:T(8,128)(2,1)}, bf16[128,1280]{1,0:T(8,128)(2,1)S(1)}, u32[]{:S(2)}, u32[]{:S(2)}) collective-permute-start(bf16[128,1280]{1,0:T(8,128)(2,1)} %get-tuple-element.36), channel_id=1, source_target_pairs={{0,6},{1,7},{2,4},{3,5},{4,2},{5,3},{6,0},{7,1},{8,14},{9,15},{10,... | collective-permute-start | bytes 983048 | tf_op jit(solution)/shard_map/ppermute | solution.py:501
  64.3 17.4 %copy-start.8 = (bf16[128,1280]{1,0:T(8,128)(2,1)}, bf16[128,1280]{1,0:T(8,128)(2,1)S(1)}, u32[]{:S(2)}) copy-start(bf16[128,1280]{1,0:T(8,128)(2,1)S(1)} %collective-permute-done.3.rest_3_) | copy-start | bytes 983044
  64.3 17.4 %copy-start.14 = (f32[1280]{0:T(1024)S(1)}, f32[1280]{0:T(1024)}, u32[]{:S(2)}) copy-start(f32[1280]{0:T(1024)} %param.14) | copy-start | bytes 15364
  64.3 18.0 %copy-start.13 = (f32[1280]{0:T(1024)S(1)}, f32[1280]{0:T(1024)}, u32[]{:S(2)}) copy-start(f32[1280]{0:T(1024)} %param.15) | copy-start | bytes 15364
  64.3 27.3 %collective-permute-start.7 = (bf16[128,1280]{1,0:T(8,128)(2,1)}, bf16[128,1280]{1,0:T(8,128)(2,1)S(1)}, u32[]{:S(2)}, u32[]{:S(2)}) collective-permute-start(bf16[128,1280]{1,0:T(8,128)(2,1)} %get-tuple-element.37), channel_id=1, source_target_pairs={{0,7},{1,6},{2,5},{3,4},{4,3},{5,2},{6,1},{7,0},{8,15},{9,14},{10,... | collective-permute-start | bytes 983048 | tf_op jit(solution)/shard_map/ppermute | solution.py:501
  88.7 2.9 %copy-start.9 = (bf16[128,1280]{1,0:T(8,128)(2,1)}, bf16[128,1280]{1,0:T(8,128)(2,1)S(1)}, u32[]{:S(2)}) copy-start(bf16[128,1280]{1,0:T(8,128)(2,1)S(1)} %collective-permute-done.4.rest_4_) | copy-start | bytes 983044
  88.7 47.0 %collective-permute-start.10 = (bf16[1280,768]{1,0:T(8,128)(2,1)}, bf16[1280,768]{1,0:T(8,128)(2,1)}, u32[]{:S(2)}, u32[]{:S(2)}) collective-permute-start(bf16[1280,768]{1,0:T(8,128)(2,1)} %norm.1.normed_t.left_own), channel_id=1, source_target_pairs={{0,1},{1,0},{2,3},{3,2},{4,5},{5,4},{6,7},{7,6},{8,9},{9,8},{10,11... | collective-permute-start | bytes 5898248 | tf_op jit(solution)/shard_map/ppermute | solution.py:463
  88.8 2.8 %copy-start.10 = (bf16[128,1280]{1,0:T(8,128)(2,1)}, bf16[128,1280]{1,0:T(8,128)(2,1)S(1)}, u32[]{:S(2)}) copy-start(bf16[128,1280]{1,0:T(8,128)(2,1)S(1)} %collective-permute-done.5.rest_5_) | copy-start | bytes 983044
  88.8 2.8 %copy-start.11 = (bf16[128,1280]{1,0:T(8,128)(2,1)}, bf16[128,1280]{1,0:T(8,128)(2,1)S(1)}, u32[]{:S(2)}) copy-start(bf16[128,1280]{1,0:T(8,128)(2,1)S(1)} %collective-permute-done.6.rest_6_) | copy-start | bytes 983044
  91.6 0.7 copy-start.12
  91.6 1.1 copy-start.5
  102.3 20.4 %collective-permute-start.8 = (bf16[1280,768]{1,0:T(8,128)(2,1)}, bf16[1280,768]{1,0:T(8,128)(2,1)S(1)}, u32[]{:S(2)}, u32[]{:S(2)}) collective-permute-start(bf16[1280,768]{1,0:T(8,128)(2,1)} %get-tuple-element.39), channel_id=1, source_target_pairs={{0,1},{1,0},{2,3},{3,2},{4,5},{5,4},{6,7},{7,6},{8,9},{9,8},{10,11... | collective-permute-start | bytes 5898248 | tf_op jit(solution)/shard_map/ppermute | solution.py:463
  102.8 17.6 %copy-start.2 = (bf16[768,1280]{1,0:T(8,128)(2,1)S(1)}, bf16[768,1280]{1,0:T(8,128)(2,1)}, u32[]{:S(2)}) copy-start(bf16[768,1280]{1,0:T(8,128)(2,1)} %x.1) | copy-start | bytes 5898244
  119.9 2.8 %collective-permute-start.9 = (bf16[768,640]{1,0:T(8,128)(2,1)}, bf16[768,640]{1,0:T(8,128)(2,1)S(1)}, u32[]{:S(2)}, u32[]{:S(2)}) collective-permute-start(bf16[768,640]{1,0:T(8,128)(2,1)} %get-tuple-element.45), channel_id=1, source_target_pairs={{0,1},{1,0},{2,3},{3,2},{4,5},{5,4},{6,7},{7,6},{8,9},{9,8},{10,11... | collective-permute-start | bytes 2949128 | tf_op jit(solution)/shard_map/ppermute | solution.py:463
  120.1 15.6 %collective-permute-start.11 = (bf16[768,640]{1,0:T(8,128)(2,1)}, bf16[768,640]{1,0:T(8,128)(2,1)S(1)}, u32[]{:S(2)}, u32[]{:S(2)}) collective-permute-start(bf16[768,640]{1,0:T(8,128)(2,1)} %get-tuple-element.47), channel_id=1, source_target_pairs={{0,1},{1,0},{2,3},{3,2},{4,5},{5,4},{6,7},{7,6},{8,9},{9,8},{10,11... | collective-permute-start | bytes 2949128 | tf_op jit(solution)/shard_map/ppermute | solution.py:463
  122.7 0.9 copy-start.17
  122.7 1.6 copy-start.15
  131.3 36.9 %all-to-all-start.1 = ((bf16[4,4,400,128]{3,2,1,0:T(8,128)(2,1)}), bf16[4,4,400,128]{3,2,1,0:T(8,128)(2,1)}, u32[]{:S(2)}, u32[]{:S(2)}) async-start(bf16[4,4,400,128]{3,2,1,0:T(8,128)(2,1)} %weight_part.2), calls=%async_computation.1 | async-start | bytes 3276800 | tf_op jit(solution)/shard_map/all_to_all | solution.py:477
  135.7 1.0 copy-start.16
  145.0 20.9 %collective-permute-start.12 = (bf16[4,400,128]{2,1,0:T(8,128)(2,1)S(1)}, bf16[4,400,128]{2,1,0:T(8,128)(2,1)S(1)}, u32[]{:S(2)}, u32[]{:S(2)}) collective-permute-start(bf16[4,400,128]{2,1,0:T(8,128)(2,1)S(1)} %get-tuple-element.55), channel_id=1, source_target_pairs={{0,2},{2,4},{4,6},{6,0},{1,3},{3,5},{5,7},{7,1},{8,10},{10,12},{12... | collective-permute-start | bytes 1228808 | tf_op jit(solution)/shard_map/ppermute | solution.py:472
  145.1 20.8 %collective-permute-start.13 = (bf16[4,400,128]{2,1,0:T(8,128)(2,1)S(1)}, bf16[4,400,128]{2,1,0:T(8,128)(2,1)S(1)}, u32[]{:S(2)}, u32[]{:S(2)}) collective-permute-start(bf16[4,400,128]{2,1,0:T(8,128)(2,1)S(1)} %get-tuple-element.57), channel_id=1, source_target_pairs={{0,4},{2,6},{4,0},{6,2},{1,5},{3,7},{5,1},{7,3},{8,12},{10,14},{12... | collective-permute-start | bytes 1228808 | tf_op jit(solution)/shard_map/ppermute | solution.py:472
  146.7 19.5 %collective-permute-start.14 = (bf16[4,400,128]{2,1,0:T(8,128)(2,1)S(1)}, bf16[4,400,128]{2,1,0:T(8,128)(2,1)S(1)}, u32[]{:S(2)}, u32[]{:S(2)}) collective-permute-start(bf16[4,400,128]{2,1,0:T(8,128)(2,1)S(1)} %get-tuple-element.56), channel_id=1, source_target_pairs={{0,6},{2,0},{4,2},{6,4},{1,7},{3,1},{5,3},{7,5},{8,14},{10,8},{12,... | collective-permute-start | bytes 1228808 | tf_op jit(solution)/shard_map/ppermute | solution.py:472
  170.0 8.1 %copy-start.4 = (bf16[768,1280]{1,0:T(8,128)(2,1)S(1)}, bf16[768,1280]{1,0:T(8,128)(2,1)}, u32[]{:S(2)}) copy-start(bf16[768,1280]{1,0:T(8,128)(2,1)} %get-tuple-element.48) | copy-start | bytes 5898244
  180.6 8.0 %collective-permute-start.15 = (bf16[400,128]{1,0:T(8,128)(2,1)S(1)}, bf16[400,128]{1,0:T(8,128)(2,1)S(1)}, u32[]{:S(2)}, u32[]{:S(2)}) collective-permute-start(bf16[400,128]{1,0:T(8,128)(2,1)S(1)} %get-tuple-element.66), channel_id=1, source_target_pairs={{0,2},{2,4},{4,6},{6,0},{1,3},{3,5},{5,7},{7,1},{8,10},{10,12},{12... | collective-permute-start | bytes 307208 | tf_op jit(solution)/shard_map/ppermute | solution.py:472
  181.5 7.1 %collective-permute-start.16 = (bf16[400,128]{1,0:T(8,128)(2,1)S(1)}, bf16[400,128]{1,0:T(8,128)(2,1)S(1)}, u32[]{:S(2)}, u32[]{:S(2)}) collective-permute-start(bf16[400,128]{1,0:T(8,128)(2,1)S(1)} %get-tuple-element.68), channel_id=1, source_target_pairs={{0,4},{2,6},{4,0},{6,2},{1,5},{3,7},{5,1},{7,3},{8,12},{10,14},{12... | collective-permute-start | bytes 307208 | tf_op jit(solution)/shard_map/ppermute | solution.py:472
  184.5 4.8 %collective-permute-start.17 = (bf16[400,128]{1,0:T(8,128)(2,1)S(1)}, bf16[400,128]{1,0:T(8,128)(2,1)S(1)}, u32[]{:S(2)}, u32[]{:S(2)}) collective-permute-start(bf16[400,128]{1,0:T(8,128)(2,1)S(1)} %get-tuple-element.67), channel_id=1, source_target_pairs={{0,6},{2,0},{4,2},{6,4},{1,7},{3,1},{5,3},{7,5},{8,14},{10,8},{12,... | collective-permute-start | bytes 307208 | tf_op jit(solution)/shard_map/ppermute | solution.py:472
  184.5 10.5 %all-to-all-start.2 = ((bf16[4,400,128]{2,1,0:T(8,128)(2,1)}), bf16[4,400,128]{2,1,0:T(8,128)(2,1)S(1)}, u32[]{:S(2)}, u32[]{:S(2)}) async-start(bf16[4,400,128]{2,1,0:T(8,128)(2,1)} %fusion.12), calls=%async_computation.2 | async-start | bytes 819200 | tf_op jit(solution)/shard_map/all_to_all | solution.py:477
  189.4 38.3 %copy-start.1 = (bf16[40,640]{1,0:T(8,128)(2,1)S(1)}, bf16[40,640]{1,0:T(8,128)(2,1)}, u32[]{:S(2)}) copy-start(bf16[40,640]{1,0:T(8,128)(2,1)} %param.17) | copy-start | bytes 153604
Sparse Core Ops, SparseCore 0:
  10.6 89.7 all-gather.1

commit v2 on v1

v2 whole, which is shorter than its diff:
```python
import functools
import math

import jax
import jax.numpy as jnp
from jax import lax
from jax.experimental import pallas as pl
from jax.experimental.pallas import tpu as pltpu
from jax.sharding import Mesh, PartitionSpec as P

HEADS = 8
HEAD_DIM = 80
TILE = 128
WINDOW = 2 * TILE
HW = HEADS * HEAD_DIM
SCALE = 1.0 / math.sqrt(HEAD_DIM)
BLOCKS = 4
AXES = {"y": 4, "z": 8, "x": 4, "core": 2}
VMEM_LIMIT = 60 * 1024 * 1024

norm_eps = 1e-06
f32 = jnp.float32
bf16 = jnp.bfloat16

SOURCE, START, JOINED, META = 0, 8, 16, 24


def lane_window(head):
    first, last = head * HEAD_DIM, (head + 1) * HEAD_DIM
    return first // 128 * 128, -(-last // 128) * 128


def params():
    return pltpu.CompilerParams(vmem_limit_bytes=VMEM_LIMIT)


def cost(flops, moved):
    return pl.CostEstimate(flops=flops, bytes_accessed=moved, transcendentals=0)


def route_kernel(
    patches, owners, place, rows, table, outgoing, used, segment, own_owner, sems, *, own_tiles, src_tiles
):
    me = place[0]
    for j in range(8):
        used[j] = 0
        segment[j] = -1
        table[SOURCE + j] = -1
    for j in range(src_tiles):
        own_owner[j] = 0

    def image(i, begin):
        count = patches[0, i] // TILE
        owner = owners[0, i]
        slot = used[owner]
        used[owner] = slot + count
        for t in range(2):

            @pl.when(t < count)
            def _():
                position = begin + t
                source = position // src_tiles

                @pl.when(owner == me)
                def _():
                    table[SOURCE + slot + t] = source
                    segment[slot + t] = i

                @pl.when(source == me)
                def _():
                    own_owner[position % src_tiles] = owner

        return begin + count

    lax.fori_loop(0, patches.shape[1], image, jnp.int32(0))
    copies = []
    for j in range(src_tiles):
        first_row = pl.multiple_of(own_owner[j] * TILE, TILE)
        copy = pltpu.make_async_copy(
            rows.at[pl.ds(j * TILE, TILE)], outgoing.at[pl.ds(first_row, TILE)], sems.at[j]
        )
        copy.start()
        copies.append(copy)

    last = own_tiles - 1
    for b in range(8):
        table[START + b] = 0
        table[JOINED + b] = 0
        table[META + b] = 0
    table[META + 1] = place[1]

    def step(at):
        here = segment[at]
        after = segment[jnp.minimum(at + 1, last)]
        beyond = segment[jnp.minimum(at + 2, last)]
        joined = here == after
        splits = (at + 2 <= last) & (after == beyond) & jnp.logical_not(joined)
        return at + jnp.where(splits, 1, 2), joined

    def find(_, carry):
        at, lone = carry
        moved, _ = step(jnp.minimum(at, last))
        return jnp.where(at <= last, moved, at), lone | (at == last).astype(jnp.int32)

    _, lone = lax.fori_loop(0, BLOCKS, find, (jnp.int32(0), jnp.int32(0)))

    @pl.when(lone == 1)
    def _():
        table[START] = last - 1
        table[JOINED] = (segment[last - 1] == segment[last]).astype(jnp.int32)

    def block(_, carry):
        at, count = carry
        moved, joined = step(jnp.minimum(at, last))
        active = at < last

        @pl.when(active)
        def _():
            table[START + count] = at
            table[JOINED + count] = joined.astype(jnp.int32)

        return jnp.where(active, moved, at), count + active.astype(jnp.int32)

    _, count = lax.fori_loop(0, BLOCKS, block, (jnp.int32(0), lone))
    table[META] = count
    for copy in copies:
        copy.wait()


def route(patches, owners, place, rows, own_tiles, sections):
    src_tiles = rows.shape[0] // TILE
    smem = pl.BlockSpec(memory_space=pltpu.SMEM)
    hbm = pl.BlockSpec(memory_space=pl.ANY)
    return pl.pallas_call(
        functools.partial(route_kernel, own_tiles=own_tiles, src_tiles=src_tiles),
        out_shape=(
            jax.ShapeDtypeStruct((32,), jnp.int32),
            jax.ShapeDtypeStruct((sections * TILE, rows.shape[1]), bf16),
        ),
        in_specs=[smem, smem, smem, pl.BlockSpec(memory_space=pltpu.VMEM)],
        out_specs=(smem, hbm),
        scratch_shapes=[
            pltpu.SMEM((8,), jnp.int32),
            pltpu.SMEM((8,), jnp.int32),
            pltpu.SMEM((src_tiles,), jnp.int32),
            pltpu.SemaphoreType.DMA((src_tiles,)),
        ],
        compiler_params=params(),
        cost_estimate=cost(0, 4 * rows.size),
        name="route",
    )(patches, owners, place, rows)


def norm_kernel(x, gain, bias, out):
    wide = x[...].astype(f32)
    average = jnp.mean(wide, axis=1, keepdims=True)
    centered = wide - average
    inv_scale = lax.rsqrt(jnp.mean(centered * centered, axis=1, keepdims=True) + norm_eps)
    normed = centered * inv_scale * gain[...] + bias[...]
    out[...] = jnp.transpose(normed.astype(bf16))


def norm_transposed(x, gain, bias):
    rows, width = x.shape
    return pl.pallas_call(
        norm_kernel,
        grid=(rows // TILE,),
        out_shape=jax.ShapeDtypeStruct((width, rows), bf16),
        in_specs=[
            pl.BlockSpec((TILE, width), lambda t: (t, 0)),
            pl.BlockSpec((1, width), lambda t: (0, 0)),
            pl.BlockSpec((1, width), lambda t: (0, 0)),
        ],
        out_specs=pl.BlockSpec((width, TILE), lambda t: (0, t)),
        compiler_params=params(),
        cost_estimate=cost(10**6, 10**5),
        name="norm",
    )(x, gain.reshape(1, width), bias.reshape(1, width))


def padded_rows(values, head):
    low, high = lane_window(head)
    first = head * HEAD_DIM
    parts = []
    if first > low:
        parts.append(jnp.zeros((first - low, values.shape[1]), values.dtype))
    parts.append(values[first : first + HEAD_DIM])
    if high > first + HEAD_DIM:
        parts.append(jnp.zeros((high - first - HEAD_DIM, values.shape[1]), values.dtype))
    return jnp.concatenate(parts, axis=0) if len(parts) > 1 else parts[0]


def lane_mask(head):
    low, high = lane_window(head)
    lanes = lax.broadcasted_iota(jnp.int32, (1, high - low), 1) + low
    return ((lanes >= head * HEAD_DIM) & (lanes < (head + 1) * HEAD_DIM)).astype(f32).astype(bf16)


def matmul(a, b):
    return lax.dot_general(a, b, (((1,), (0,)), ((), ())), preferred_element_type=f32)


def block_at(rank):
    return lambda b, t: (jnp.minimum(b, jnp.maximum(t[META] - 1, 0)),) + (0,) * (rank - 1)


def softmax_over_rows(scores):
    scores = scores * (SCALE * math.log2(math.e))
    shifted = jnp.exp2(scores - jnp.max(scores, axis=0, keepdims=True))
    return (shifted * (1.0 / jnp.sum(shifted, axis=0, keepdims=True))).astype(bf16)


def forward_kernel(table, qkv, attended, attended_t, weights):
    b = pl.program_id(0)
    rows = pl.ds(pl.multiple_of(table[START + b] * TILE, TILE), WINDOW)
    joined = table[JOINED + b] == 1

    def attend(whole_window):
        queries_t = jnp.transpose(qkv[rows, 0:HW])
        values_t = jnp.transpose(qkv[rows, 2 * HW : 3 * HW])

        def scores_of(h):
            low, high = lane_window(h)
            return matmul(qkv[rows, HW + low : HW + high], padded_rows(queries_t, h))

        heads = []
        for h in range(HEADS):
            scores = scores_of(h)
            if whole_window:
                kept = softmax_over_rows(scores)
            else:
                nothing = jnp.zeros((TILE, TILE), bf16)
                top = softmax_over_rows(scores[:TILE, :TILE])
                bottom = softmax_over_rows(scores[TILE:, TILE:])
                kept = jnp.concatenate(
                    [
                        jnp.concatenate([top, nothing], axis=1),
                        jnp.concatenate([nothing, bottom], axis=1),
                    ],
                    axis=0,
                )
            weights[0, h] = kept
            heads.append(matmul(values_t[h * HEAD_DIM : (h + 1) * HEAD_DIM], kept).astype(bf16))
        whole = jnp.concatenate(heads, axis=0)
        attended_t[0] = whole
        attended[rows, :] = jnp.transpose(whole)

    pl.when((b < table[META]) & joined)(lambda: attend(True))
    pl.when((b < table[META]) & jnp.logical_not(joined))(lambda: attend(False))


def forward(table, qkv):
    rows, width = qkv.shape
    return pl.pallas_call(
        forward_kernel,
        grid_spec=pltpu.PrefetchScalarGridSpec(
            num_scalar_prefetch=1,
            grid=(BLOCKS,),
            in_specs=[pl.BlockSpec((rows, width), lambda b, t: (0, 0))],
            out_specs=(
                pl.BlockSpec((rows, HW), lambda b, t: (0, 0)),
                pl.BlockSpec((1, HW, WINDOW), block_at(3)),
                pl.BlockSpec((1, HEADS, WINDOW, WINDOW), block_at(4)),
            ),
        ),
        out_shape=(
            jax.ShapeDtypeStruct((rows, HW), bf16),
            jax.ShapeDtypeStruct((BLOCKS, HW, WINDOW), bf16),
            jax.ShapeDtypeStruct((BLOCKS, HEADS, WINDOW, WINDOW), bf16),
        ),
        compiler_params=params(),
        cost_estimate=cost(10**6, 10**5),
        name="attend",
    )(table, qkv)


def incoming_kernel(table, arrived, w, incoming, d_attn, incoming_t, landing, sems, *, tiles):
    t = pl.program_id(0)

    def row_copy(j, source):
        first_row = pl.multiple_of(source * TILE, TILE)
        return pltpu.make_async_copy(
            arrived.at[pl.ds(first_row, TILE)], landing.at[pl.ds(j * TILE, TILE)], sems.at[j]
        )

    @pl.when(t == 0)
    def _():
        for j in range(tiles):
            source = table[SOURCE + j]

            @pl.when(source >= 0)
            def _():
                row_copy(j, source).start()

            @pl.when(source < 0)
            def _():
                landing[j * TILE : (j + 1) * TILE] = jnp.zeros((TILE, landing.shape[1]), bf16)

    for i in range(2):
        j = 2 * t + i
        pl.when(table[SOURCE + j] >= 0)(row_copy(j, 0).wait)
    rows = landing[pl.ds(pl.multiple_of(t * WINDOW, WINDOW), WINDOW)]
    incoming[...] = rows
    incoming_t[...] = jnp.transpose(rows)
    d_attn[...] = matmul(rows, w[...]).astype(bf16)


def place_incoming(table, arrived, w, rows):
    width = arrived.shape[1]
    return pl.pallas_call(
        functools.partial(incoming_kernel, tiles=rows // TILE),
        grid_spec=pltpu.PrefetchScalarGridSpec(
            num_scalar_prefetch=1,
            grid=(rows // WINDOW,),
            in_specs=[
                pl.BlockSpec(memory_space=pl.ANY),
                pl.BlockSpec((width, HW), lambda i, t: (0, 0)),
            ],
            out_specs=(
                pl.BlockSpec((WINDOW, width), lambda i, t: (i, 0)),
                pl.BlockSpec((WINDOW, HW), lambda i, t: (i, 0)),
                pl.BlockSpec((width, WINDOW), lambda i, t: (0, i)),
            ),
            scratch_shapes=[
                pltpu.VMEM((rows, width), bf16),
                pltpu.SemaphoreType.DMA((rows // TILE,)),
            ],
        ),
        out_shape=(
            jax.ShapeDtypeStruct((rows, width), bf16),
            jax.ShapeDtypeStruct((rows, HW), bf16),
            jax.ShapeDtypeStruct((width, rows), bf16),
        ),
        compiler_params=params(),
        cost_estimate=cost(2 * rows * width * HW, 10 * rows * width),
        name="incoming",
    )(table, arrived, w)


def add_lanes(tiles, low, part):
    for j in range(part.shape[1] // 128):
        piece = part[:, j * 128 : (j + 1) * 128]
        at = low // 128 + j
        tiles[at] = piece if tiles[at] is None else tiles[at] + piece


def backward_kernel(
    table, qkv, d_attn, attended, attended_t, weights, value_query, attended_key
):
    b = pl.program_id(0)

    @pl.when(b < table[META])
    def _():
        rows = pl.ds(pl.multiple_of(table[START + b] * TILE, TILE), WINDOW)
        grad_t = jnp.transpose(d_attn[rows, :])
        keys_t = jnp.transpose(qkv[rows, HW : 2 * HW])
        query_grads = []
        key_tiles = [None] * (HW // 128)
        value_tiles = [None] * (HW // 128)
        for h in range(HEADS):
            low, high = lane_window(h)
            mine = slice(h * HEAD_DIM, (h + 1) * HEAD_DIM)
            mask = lane_mask(h)
            prob_grad = matmul(qkv[rows, 2 * HW + low : 2 * HW + high], padded_rows(grad_t, h))
            row_delta = jnp.sum(
                grad_t[mine].astype(f32) * attended_t[0, mine].astype(f32), axis=0, keepdims=True
            )
            dscore = (weights[0, h].astype(f32) * ((prob_grad - row_delta) * SCALE)).astype(bf16)
            query_grads.append(matmul(keys_t[mine], dscore).astype(bf16))
            add_lanes(key_tiles, low, matmul(dscore, qkv[rows, low:high] * mask))
            add_lanes(value_tiles, low, matmul(weights[0, h], d_attn[rows, low:high] * mask))
        value_query[rows, HW:] = jnp.transpose(jnp.concatenate(query_grads, axis=0))
        for j in range(HW // 128):
            value_query[rows, j * 128 : (j + 1) * 128] = value_tiles[j].astype(bf16)
            attended_key[rows, HW + j * 128 : HW + (j + 1) * 128] = key_tiles[j].astype(bf16)
        attended_key[rows, :HW] = attended[rows, :]


def backward(table, qkv, d_attn, attended, attended_t, weights):
    rows, width = qkv.shape
    whole = pl.BlockSpec((rows, HW), lambda b, t: (0, 0))
    return pl.pallas_call(
        backward_kernel,
        grid_spec=pltpu.PrefetchScalarGridSpec(
            num_scalar_prefetch=1,
            grid=(BLOCKS,),
            in_specs=[
                pl.BlockSpec((rows, width), lambda b, t: (0, 0)),
                whole,
                whole,
                pl.BlockSpec((1, HW, WINDOW), block_at(3)),
                pl.BlockSpec((1, HEADS, WINDOW, WINDOW), block_at(4)),
            ],
            out_specs=(pl.BlockSpec((rows, 2 * HW), lambda b, t: (0, 0)),) * 2,
        ),
        out_shape=(jax.ShapeDtypeStruct((rows, 2 * HW), bf16),) * 2,
        compiler_params=params(),
        cost_estimate=cost(12 * 10**9, 20 * 10**6),
        name="attend_back",
    )(table, qkv, d_attn, attended, attended_t, weights)


def norm_back_kernel(table, x, incoming, gain, d_query, d_key, d_value, own_w, mate_w, out):
    def halves(low, high):
        grads = jnp.concatenate([d_query[...], d_key[...], d_value[...]], axis=1)
        contract = (((1,), (1,)), ((), ()))
        return lax.dot_general(
            grads[:, :1024], low[...], contract, preferred_element_type=f32
        ) + lax.dot_general(
            grads[:, 1024:], high[:, 128:1024], contract, preferred_element_type=f32
        )

    def finish(dnormed):
        wide = x[...].astype(f32)
        average = jnp.mean(wide, axis=1, keepdims=True)
        centered = wide - average
        inv_scale = lax.rsqrt(jnp.mean(centered * centered, axis=1, keepdims=True) + norm_eps)
        normalized = centered * inv_scale
        scaled_grad = dnormed * gain[...]
        branch = inv_scale * (
            scaled_grad
            - jnp.mean(scaled_grad, axis=1, keepdims=True)
            - normalized * jnp.mean(scaled_grad * normalized, axis=1, keepdims=True)
        )
        out[...] = (incoming[...].astype(f32) + branch).astype(bf16)

    first = table[META + 1] == 0

    @pl.when(first)
    def _():
        finish(halves(own_w, mate_w))

    @pl.when(jnp.logical_not(first))
    def _():
        finish(halves(mate_w, own_w))


def norm_back(table, x, incoming, gain, value_query, attended_key, own_w, mate_w):
    rows, width = x.shape
    wide = pl.BlockSpec((WINDOW, width), lambda i, t: (i, 0))
    weights = pl.BlockSpec((width, 1024), lambda i, t: (0, 0))
    return pl.pallas_call(
        norm_back_kernel,
        grid_spec=pltpu.PrefetchScalarGridSpec(
            num_scalar_prefetch=1,
            grid=(rows // WINDOW,),
            in_specs=[
                wide,
                wide,
                pl.BlockSpec((1, width), lambda i, t: (0, 0)),
                pl.BlockSpec((WINDOW, HW), lambda i, t: (i, 1)),
                pl.BlockSpec((WINDOW, HW), lambda i, t: (i, 1)),
                pl.BlockSpec((WINDOW, HW), lambda i, t: (i, 0)),
                weights,
                weights,
            ],
            out_specs=wide,
        ),
        out_shape=jax.ShapeDtypeStruct((rows, width), bf16),
        compiler_params=params(),
        cost_estimate=cost(2 * rows * width * 3 * HW, 20 * 10**6),
        name="norm_back",
    )(table, x, incoming, gain.reshape(1, width), value_query, attended_key, value_query, own_w, mate_w)


def packed_columns(total, out):
    rows = total.shape[0]
    group = rows // 4
    fifth = total[:, 512:640]
    quarter = lax.broadcasted_iota(jnp.int32, (group, 128), 1) // 32
    for x in range(4):
        packed = jnp.zeros((group, 128), f32)
        for g in range(4):
            piece = fifth[g * group : (g + 1) * group]
            shift = (g - x) * 32 % 128
            packed = jnp.where(quarter == g, pltpu.roll(piece, shift, 1) if shift else piece, packed)
        out[x, :rows] = total[:, x * 128 : (x + 1) * 128].astype(bf16)
        out[x, rows:] = packed.astype(bf16)


def weight_kernel(
    table, normed, mate_normed, incoming, mate_incoming, zero, one, mate_zero, mate_one, by_y, by_x, right, sems
):
    first = table[META + 1] == 0
    depth = zero.shape[0]

    def copy(side, source):
        return pltpu.make_async_copy(source, right.at[pl.ds(side * depth, depth)], sems.at[side])

    @pl.when(pl.program_id(0) == 0)
    def _():
        for side, (on_zero, on_one) in enumerate(((zero, one), (mate_zero, mate_one))):
            pl.when(first)(copy(side, on_zero).start)
            pl.when(jnp.logical_not(first))(copy(side, on_one).start)
        for side in range(2):
            copy(side, zero).wait()

    normed_both = jnp.concatenate([normed[...], mate_normed[...]], axis=1)
    incoming_both = jnp.concatenate([incoming[...], mate_incoming[...]], axis=1)
    left = jnp.where(first, normed_both, incoming_both)
    packed_columns(matmul(left, right[:, :HW]), by_y)
    packed_columns(matmul(normed_both, right[:, HW:]), by_x)


def weight_parts(table, normed, mate_normed, incoming, mate_incoming, rights):
    width, rows = normed.shape
    piece = width // 4
    packed = piece * 5 // 4
    left = pl.BlockSpec((piece, rows), lambda i, t: (i, 0))
    on_one = pl.BlockSpec((piece, rows), lambda i, t: (i * t[META + 1], 0))
    return pl.pallas_call(
        weight_kernel,
        grid_spec=pltpu.PrefetchScalarGridSpec(
            num_scalar_prefetch=1,
            grid=(4,),
            in_specs=[left, left, on_one, on_one] + [pl.BlockSpec(memory_space=pl.ANY)] * 4,
            out_specs=(
                pl.BlockSpec((None, 4, packed, 128), lambda i, t: (i, 0, 0, 0)),
                pl.BlockSpec((4, None, packed, 128), lambda i, t: (0, i, 0, 0)),
            ),
            scratch_shapes=[pltpu.VMEM((2 * rows, 2 * HW), bf16), pltpu.SemaphoreType.DMA((2,))],
        ),
        out_shape=(jax.ShapeDtypeStruct((4, 4, packed, 128), bf16),) * 2,
        compiler_params=params(),
        cost_estimate=cost(8 * width * rows * HW, 8 * width * rows + 4 * width * HW),
        name="weight_parts",
    )(table, normed, mate_normed, incoming, mate_incoming, *rights)


def unpacked(part):
    rest = part[320:]
    return jnp.concatenate(
        [part[:320], jnp.concatenate([rest[:, i * 32 : (i + 1) * 32] for i in range(4)], axis=0)], axis=1
    )


def to_mate(value):
    return lax.ppermute(value, "core", [(0, 1), (1, 0)])


def gathered(value, axis):
    count = AXES[axis]
    here = lax.axis_index(axis)
    out = jnp.zeros((count,) + value.shape, value.dtype)
    out = lax.dynamic_update_index_in_dim(out, value, here, 0)
    for k in range(1, count):
        part = lax.ppermute(value, axis, [(i, (i + k) % count) for i in range(count)])
        out = lax.dynamic_update_index_in_dim(out, part, lax.rem(here - k + count, count), 0)
    return out


def sent_to_owners(value, axis):
    count = AXES[axis]
    here = lax.axis_index(axis)
    parts = [lax.dynamic_index_in_dim(value, here, 0, keepdims=False)]
    for k in range(1, count):
        part = lax.dynamic_index_in_dim(value, lax.rem(here + k, count), 0, keepdims=False)
        parts.append(lax.ppermute(part, axis, [(i, (i + k) % count) for i in range(count)]))
    return parts


def added(parts):
    return sum(part.astype(f32) for part in parts)


def exchanged(value, axes):
    return lax.all_to_all(value, axes, split_axis=0, concat_axis=0, tiled=True)


def on_device(
    grad_rows,
    layer_input,
    saved_qkv,
    image_patches,
    image_owner,
    norm_gain,
    norm_bias,
    w_qkv,
    w_out,
):
    width = layer_input.shape[1]
    own_tiles = layer_input.shape[0] // TILE
    section = ("x", "core")
    sections = AXES["x"] * AXES["core"]
    core = lax.axis_index("core")
    place = jnp.stack([lax.axis_index(section), core]).astype(jnp.int32)

    columns = jnp.concatenate([w_out, lax.dynamic_slice_in_dim(w_qkv, 896 * core, 1024, axis=1)], axis=1)
    columns = gathered(columns, "y").reshape(4 * w_out.shape[0], HW + 1024)

    def gathered_z(value):
        return lax.all_gather(value, "z", axis=0, tiled=True)

    def in_order(whole):
        return jnp.swapaxes(whole.reshape(8, 4, -1, whole.shape[1]), 0, 1).reshape(whole.shape)

    table, outgoing = route(image_patches, image_owner, place, grad_rows, own_tiles, sections)
    arrived = exchanged(outgoing, section)
    out_w = gathered_z(columns[:, :HW])
    normed_t = norm_transposed(layer_input, norm_gain, norm_bias)
    attended, attended_t, weights = forward(table, saved_qkv)
    out_w, arrived, attended_t, normed_t, columns = lax.optimization_barrier(
        (out_w, arrived, attended_t, normed_t, columns)
    )
    mate_normed_t = to_mate(normed_t)
    out_w = in_order(out_w)
    qkv_w = gathered_z(columns[:, HW:])

    incoming, d_attn, incoming_t = place_incoming(table, arrived, out_w, own_tiles * TILE)
    mate_incoming_t = lax.ppermute(incoming_t, "core", [(0, 1)])
    value_query, attended_key = backward(table, saved_qkv, d_attn, attended, attended_t, weights)
    first, second = weight_parts(
        table,
        normed_t,
        mate_normed_t,
        incoming_t,
        mate_incoming_t,
        (
            value_query,
            attended_key,
            lax.ppermute(value_query, "core", [(1, 0)]),
            lax.ppermute(attended_key, "core", [(0, 1)]),
        ),
    )
    first, second, qkv_w = lax.optimization_barrier((first, second, qkv_w))
    qkv_w = in_order(qkv_w)
    layer_grad = norm_back(
        table, layer_input, incoming, norm_gain, value_query, attended_key, qkv_w, to_mate(qkv_w)
    )
    first = exchanged(first, "y")
    second = sent_to_owners(second, "x")
    first, second, layer_grad = lax.optimization_barrier((first, second, layer_grad))
    second = added(second).astype(bf16)
    first, second = lax.optimization_barrier((first, second))
    second = exchanged(second, "y")
    first = added(sent_to_owners(jnp.sum(first.astype(f32), axis=0).astype(bf16), "x"))
    second = jnp.sum(second.astype(f32), axis=0)
    columns = jnp.concatenate([unpacked(first), unpacked(second)], axis=1).astype(bf16)
    by_z = exchanged(columns.reshape(8, 40, 320), "z")
    share = jnp.sum(by_z.astype(f32), axis=0) / (AXES["y"] * AXES["z"] * sections)
    shares = gathered(gathered(share, "x"), "core")

    def assemble(core, first_column):
        mine = [shares[core, x][:, first_column : first_column + 160] for x in range(4)]
        return [part[:, :128] for part in mine] + [part[:, 128:] for part in mine]

    qkv_weight_grad = jnp.concatenate(assemble(0, 160) + assemble(1, 160) + assemble(0, 0), axis=1)
    out_weight_grad = jnp.concatenate(assemble(1, 0), axis=1)
    return layer_grad, qkv_weight_grad, out_weight_grad


def solution(mesh):
    fine = Mesh(mesh.devices.reshape(tuple(AXES.values())), tuple(AXES))
    rows = P(("y", "z", "x", "core"), None)
    dp = P(("y", "z"), None)
    return jax.shard_map(
        on_device,
        mesh=fine,
        in_specs=(rows, rows, rows, dp, dp, P(), P(), dp, dp),
        out_specs=(rows, dp, dp),
        check_vma=False,
    )
```

time: 235 us -> 207 us (0.88)
  blocking collectives: 29.5 us -> 0 us
  starting transfers between devices: 43 us -> 51.5 us
  matrix products: 8.07 us -> 0 us
  waiting for transfers between devices: 54.5 us -> 46.5 us
  local copies, waits for them, and re-layouts: 10.3 us -> 15 us
  Pallas kernels: 66.7 us -> 70.7 us
    all_to_all x2 -> x0, blocking collectives: 29.5 us -> none  [exchanged(): return lax.all_to_all(value, axes, split_axis=0, concat_axis=0, tiled=True)]
    ppermute x13 -> x16, starting transfers between devices: 15.7 us -> 30 us  [the longest x7 16.1 us: gathered(): lax.ppermute(value, axis, [(i, (i + k) % count) for i in range(count)])]
    dot_general x1 -> x0, matrix products: 8.07 us -> none  [norm_back(): lax.dot_general(dqkv, w_qkv, (((1,), (1,)), ((), ())), preferred_element_...]
    pallas_call x3, Pallas kernels: 23.6 us -> 30.3 us  [the longest x1 12.4 us: weight_parts(): pl.pallas_call(weight_kernel, grid_spec=pltpu.PrefetchScalarGridSpec(num_...]
    all_to_all x3 -> x4, waiting for transfers between devices: 30.6 us -> 24.6 us  [exchanged(): return lax.all_to_all(value, axes, split_axis=0, concat_axis=0, tiled=True)]
    transpose x0 -> x2, local copies, waits for them, and re-layouts: none -> 4.96 us  [in_order(): jnp.swapaxes(whole.reshape(8, 4, -1, whole.shape[1]), 0, 1)]
    ppermute x5 -> x2, starting transfers between devices: 6.71 us -> 1.81 us  [to_mate(): return lax.ppermute(value, 'core', [(0, 1), (1, 0)])]
    all_to_all x3 -> x4, starting transfers between devices: 20.5 us -> 19.7 us  [exchanged(): return lax.all_to_all(value, axes, split_axis=0, concat_axis=0, tiled=True)]
  transfers between devices with their start and end apart: 22 -> 24, of which waited for: 7 -> 12; matrix products, arithmetic and copies ran while one was open for 4% -> 4% of each run, Pallas kernels for 28% -> 34%
where the time goes in v2:
time: 207 us; the launch traced here: 205 us
  Pallas kernels  70.7 us (34%)
  starting transfers between devices  51.5 us (25%)
  waiting for transfers between devices  46.5 us (22%)
  local copies, waits for them, and re-layouts  15 us (7%)
  between operations  14.4 us (7%)
  other arithmetic  7.29 us (4%)
    all_to_all x4, waiting for transfers between devices, exchanged(): return lax.all_to_all(value, axes, split_axis=0, concat_axis=0, tiled=True)  24.6 us
    all_to_all x4, starting transfers between devices, exchanged(): return lax.all_to_all(value, axes, split_axis=0, concat_axis=0, tiled=True)  19.7 us
    ppermute x7, starting transfers between devices, gathered(): lax.ppermute(value, axis, [(i, (i + k) % count) for i in range(count)])  16.1 us
    pallas_call x1, Pallas kernels, backward(): pl.pallas_call(backward_kernel, grid_spec=pltpu.PrefetchScalarGridSpec(nu...  15.9 us
    pallas_call x1, Pallas kernels, forward(): pl.pallas_call(forward_kernel, grid_spec=pltpu.PrefetchScalarGridSpec(num...  15 us
    pallas_call x1, Pallas kernels, weight_parts(): pl.pallas_call(weight_kernel, grid_spec=pltpu.PrefetchScalarGridSpec(num_...  12.4 us
    pallas_call x1, Pallas kernels, norm_back(): pl.pallas_call(norm_back_kernel, grid_spec=pltpu.PrefetchScalarGridSpec(n...  11.3 us
    ppermute x6, starting transfers between devices, sent_to_owners(): lax.ppermute(part, axis, [(i, (i + k) % count) for i in range(count)])  9.89 us
  transfers between devices with their start and end apart: 24, of which 12 were waited for; matrix products, arithmetic and copies ran while one was open for 4% of the time, Pallas kernels for 34%

profile of v2, /device:TPU:1, one launch (start us, length us, event | category | flops | bytes accessed | tf_op | source)
XLA Modules:
  0.0 205.4 jit_solution(5241075023671045208)
XLA Ops:
  7.2 0.9 copy-done
  8.1 0.8 pad_maximum_fusion.1
  8.9 2.2 %collective-permute-start = (bf16[40,1664]{1,0:T(8,128)(2,1)S(1)}, bf16[40,1664]{1,0:T(8,128)(2,1)S(1)}, u32[]{:S(2)}, u32[]{:S(2)}) collective-permute-start(bf16[40,1664]{1,0:T(8,128)(2,1)S(1)} %pad_maximum_fusion.1), channel_id=1, source_target_pairs={{0,64},{64,128},{128,192},{192,0},{1,65},{65,129},{129,193},{193,1... | collective-permute-start | bytes 399368 | tf_op jit(solution)/shard_map/ppermute | solution.py:547
  11.1 2.6 %collective-permute-start.1 = (bf16[40,1664]{1,0:T(8,128)(2,1)S(1)}, bf16[40,1664]{1,0:T(8,128)(2,1)S(1)}, u32[]{:S(2)}, u32[]{:S(2)}) collective-permute-start(bf16[40,1664]{1,0:T(8,128)(2,1)S(1)} %pad_maximum_fusion.1), channel_id=1, source_target_pairs={{0,128},{64,192},{128,0},{192,64},{1,129},{65,193},{129,1},{193,65... | collective-permute-start | bytes 399368 | tf_op jit(solution)/shard_map/ppermute | solution.py:547
  13.7 1.1 collective-permute-start.2
  14.8 0.8 bitcast_dynamic-update-slice_fusion.5
  15.7 3.8 %collective-permute-done.1 = bf16[40,1664]{1,0:T(8,128)(2,1)S(1)} collective-permute-done((bf16[40,1664]{1,0:T(8,128)(2,1)S(1)}, bf16[40,1664]{1,0:T(8,128)(2,1)S(1)}, u32[]{:S(2)}, u32[]{:S(2)}) %collective-permute-start.1) | collective-permute-done | bytes 133152 | tf_op jit(solution)/shard_map/ppermute | solution.py:547
  19.6 0.7 slice.284
  20.3 0.6 pad_add_fusion.place
  20.9 3.8 %route.1 = (s32[32]{0:T(128)}, bf16[1024,1280]{1,0:T(8,128)(2,1)}) custom-call(s32[1,32]{1,0:T(1,128)} %patches.1, s32[1,32]{1,0:T(1,128)} %owners.1, s32[2]{0:T(128)} %pad_add_fusion.place, bf16[512,1280]{1,0:T(8,128)(2,1)} %rows.1), custom_call_target="tpu_custom_call" | custom-call | bytes 2621440 | tf_op jit(solution)/shard_map/route/pallas_call | solution.py:134
  24.8 5.9 %all-to-all-start = ((bf16[8,128,1280]{2,1,0:T(8,128)(2,1)}), bf16[8,128,1280]{2,1,0:T(8,128)(2,1)S(1)}, u32[]{:S(2)}, u32[]{:S(2)}) async-start(bf16[8,128,1280]{2,1,0:T(8,128)(2,1)} %bitcast.74), calls=%async_computation | async-start | bytes 5242880 | tf_op jit(solution)/shard_map/all_to_all | solution.py:567
  30.6 0.6 reshape.51.gain
  31.2 0.6 reshape.52.bias
  31.8 15.0 %attend.1 = (bf16[768,640]{1,0:T(8,128)(2,1)}, bf16[4,640,256]{2,1,0:T(8,128)(2,1)}, bf16[4,8,256,256]{3,2,1,0:T(8,128)(2,1)}) custom-call(s32[32]{0:T(128)} %get-tuple-element.31.table, bf16[768,1920]{1,0:T(8,128)(2,1)} %qkv.3), custom_call_target="tpu_custom_call" | custom-call | flops 1000000 | bytes 100000 | tf_op jit(solution)/shard_map/attend/pallas_call | solution.py:254
  46.8 5.8 %norm.1.normed = bf16[1280,768]{1,0:T(8,128)(2,1)} custom-call(bf16[768,1280]{1,0:T(8,128)(2,1)} %x.3, f32[1,1280]{1,0:T(1,128)} %reshape.51.gain, f32[1,1280]{1,0:T(1,128)} %reshape.52.bias), custom_call_target="tpu_custom_call" | custom-call | flops 1000000 | bytes 100000 | tf_op jit(solution)/shard_map/norm/pallas_call | solution.py:165
  52.7 9.9 %all-to-all-done = bf16[8,128,1280]{2,1,0:T(8,128)(2,1)S(1)} async-done(((bf16[8,128,1280]{2,1,0:T(8,128)(2,1)}), bf16[8,128,1280]{2,1,0:T(8,128)(2,1)S(1)}, u32[]{:S(2)}, u32[]{:S(2)}) %all-to-all-start) | async-done | bytes 2621472 | tf_op jit(solution)/shard_map/all_to_all | solution.py:567
  62.6 0.8 slice.233
  63.5 2.9 %copy.28 = bf16[4,8,40,640]{3,2,1,0:T(8,128)(2,1)} copy(bf16[4,8,40,640]{3,2,0,1:T(8,128)(2,1)} %bitcast.77) | data formatting | bytes 3276800 | tf_op jit(solution)/shard_map/transpose | solution.py:595
  66.4 6.5 %incoming.1 = (bf16[768,1280]{1,0:T(8,128)(2,1)}, bf16[768,640]{1,0:T(8,128)(2,1)}, bf16[1280,768]{1,0:T(8,128)(2,1)}) custom-call(s32[32]{0:T(128)} %get-tuple-element.31.table, bf16[1024,1280]{1,0:T(8,128)(2,1)} %bitcast.73, bf16[1280,640]{1,0:T(8,128)(2,1)} %bitcast.78), custom_call_target="tpu_custom_call" | custom-call | flops 1258291200 | bytes 9830400 | tf_op jit(solution)/shard_map/incoming/pallas_call | solution.py:310
  72.9 15.9 %attend_back.1 = (bf16[768,1280]{1,0:T(8,128)(2,1)}, bf16[768,1280]{1,0:T(8,128)(2,1)}) custom-call(s32[32]{0:T(128)} %get-tuple-element.31.table, bf16[768,1920]{1,0:T(8,128)(2,1)} %qkv.3, bf16[768,640]{1,0:T(8,128)(2,1)} %get-tuple-element.38.d_attn, bf16[768,640]{1,0:T(8,128)(2,1)} %get-tuple-element.39.attended, ...), custom_call_target="tpu_custom_call" | custom-call | flops 12000000000 | bytes 20000000 | tf_op jit(solution)/shard_map/attend_back/pallas_call | solution.py:382
  88.8 1.4 collective-permute-start.5
  90.2 1.3 collective-permute-start.6
  91.5 1.3 collective-permute-start.4
  92.8 1.6 collective-permute-start.3
  94.4 1.8 collective-permute-done.6.mate_one
  96.3 5.4 %collective-permute-done.4.mate_incoming = bf16[1280,768]{1,0:T(8,128)(2,1)S(1)} collective-permute-done((bf16[1280,768]{1,0:T(8,128)(2,1)S(1)}, bf16[1280,768]{1,0:T(8,128)(2,1)S(1)}, u32[]{:S(2)}, u32[]{:S(2)}) %collective-permute-start.4) | collective-permute-done | bytes 1966112 | tf_op jit(solution)/shard_map/ppermute | solution.py:610
  101.7 1.3 copy-done.9
  103.0 12.4 %weight_parts.1 = (bf16[4,4,400,128]{3,2,1,0:T(8,128)(2,1)}, bf16[4,4,400,128]{3,2,1,0:T(8,128)(2,1)}) custom-call(s32[32]{0:T(128)} %get-tuple-element.31.table, bf16[1280,768]{1,0:T(8,128)(2,1)} %norm.1.normed, bf16[1280,768]{1,0:T(8,128)(2,1)} %collective-permute-done.3.mate_normed, bf16[1280,768]{1,0:T(8,128)(2,1)} %get-tuple-element.37.incoming, ...), custom_call_target="tpu_custom_call" | custom-call | flops 5033164800 | bytes 11141120 | tf_op jit(solution)/shard_map/weight_parts/pallas_call | solution.py:511
  115.4 2.1 %copy.29 = bf16[4,8,40,1024]{3,2,1,0:T(8,128)(2,1)S(1)} copy(bf16[4,8,40,1024]{3,2,0,1:T(8,128)(2,1)} %bitcast.72) | data formatting | bytes 5242880 | tf_op jit(solution)/shard_map/transpose | solution.py:595
  117.5 0.2 collective-permute-start.10
  117.7 4.4 %all-to-all-start.1 = ((bf16[4,4,400,128]{3,2,1,0:T(8,128)(2,1)}), bf16[4,4,400,128]{3,2,1,0:T(8,128)(2,1)}, u32[]{:S(2)}, u32[]{:S(2)}) async-start(bf16[4,4,400,128]{3,2,1,0:T(8,128)(2,1)} %get-tuple-element.47), calls=%async_computation.1 | async-start | bytes 3276800 | tf_op jit(solution)/shard_map/all_to_all | solution.py:567
  122.1 2.4 %dynamic-slice_bitcast_fusion = (bf16[4,400,128]{2,1,0:T(8,128)(2,1)S(1)}, bf16[4,400,128]{2,1,0:T(8,128)(2,1)}, bf16[4,400,128]{2,1,0:T(8,128)(2,1)}, bf16[4,400,128]{2,1,0:T(8,128)(2,1)S(1)}) fusion(bf16[4,4,400,128]{3,2,1,0:T(8,128)(2,1)} %get-tuple-element.48, s32[]{:T(128)S(6)} %select_n.54, s32[]{:T(128)S(6)} %select_n.53, s32[]{:T(128)S(6)} %select_n.52, ...), kind=kLoop, calls=%fused_computation.2 | loop fusion | bytes 3276816 | tf_op jit(solution)/shard_map/jit(dynamic_index_in_dim)/squeeze | solution.py:557
  124.5 2.9 %collective-permute-start.7 = (bf16[4,400,128]{2,1,0:T(8,128)(2,1)}, bf16[4,400,128]{2,1,0:T(8,128)(2,1)}, u32[]{:S(2)}, u32[]{:S(2)}) collective-permute-start(bf16[4,400,128]{2,1,0:T(8,128)(2,1)} %get-tuple-element.61), channel_id=1, source_target_pairs={{0,2},{2,4},{4,6},{6,0},{1,3},{3,5},{5,7},{7,1},{8,10},{10,12},{12... | collective-permute-start | bytes 1228808 | tf_op jit(solution)/shard_map/ppermute | solution.py:558
  127.4 3.0 %collective-permute-start.8 = (bf16[4,400,128]{2,1,0:T(8,128)(2,1)}, bf16[4,400,128]{2,1,0:T(8,128)(2,1)}, u32[]{:S(2)}, u32[]{:S(2)}) collective-permute-start(bf16[4,400,128]{2,1,0:T(8,128)(2,1)} %get-tuple-element.60), channel_id=1, source_target_pairs={{0,4},{2,6},{4,0},{6,2},{1,5},{3,7},{5,1},{7,3},{8,12},{10,14},{12... | collective-permute-start | bytes 1228808 | tf_op jit(solution)/shard_map/ppermute | solution.py:558
  130.4 11.3 %norm_back.1 = bf16[768,1280]{1,0:T(8,128)(2,1)} custom-call(s32[32]{0:T(128)} %get-tuple-element.31.table, bf16[768,1280]{1,0:T(8,128)(2,1)} %x.3, bf16[768,1280]{1,0:T(8,128)(2,1)} %get-tuple-element.49.incoming, f32[1,1280]{1,0:T(1,128)} %reshape.51.gain, bf16[768,1280]{1,0:T(8,128)(2,1)} %get-tuple-element.42.zero.d_query.d_value, ...), custom_call_target="tpu_custom_call" | custom-call | flops 3774873600 | bytes 20000000 | tf_op jit(solution)/shard_map/norm_back/pallas_call | solution.py:442
  141.7 6.9 %collective-permute-done.8 = bf16[4,400,128]{2,1,0:T(8,128)(2,1)} collective-permute-done((bf16[4,400,128]{2,1,0:T(8,128)(2,1)}, bf16[4,400,128]{2,1,0:T(8,128)(2,1)}, u32[]{:S(2)}, u32[]{:S(2)}) %collective-permute-start.8) | collective-permute-done | bytes 409632 | tf_op jit(solution)/shard_map/ppermute | solution.py:558
  148.7 2.3 %add_convert_fusion = bf16[4,400,128]{2,1,0:T(8,128)(2,1)} fusion(bf16[4,400,128]{2,1,0:T(8,128)(2,1)} %collective-permute-done.9, bf16[4,400,128]{2,1,0:T(8,128)(2,1)} %collective-permute-done.8, bf16[4,400,128]{2,1,0:T(8,128)(2,1)} %collective-permute-done.7, bf16[4,400,128]{2,1,0:T(8,128)(2,1)S(1)} %get-tuple-element.53), kind=kLoop, calls=%fused_computation | loop fusion | flops 1638400 | bytes 2048000 | tf_op jit(solution)/shard_map/convert_element_type | solution.py:633
  150.9 1.7 reduce_sum.30
  152.7 0.9 collective-permute-start.11
  153.6 3.0 %collective-permute-start.12 = (bf16[400,128]{1,0:T(8,128)(2,1)S(1)}, bf16[400,128]{1,0:T(8,128)(2,1)S(1)}, u32[]{:S(2)}, u32[]{:S(2)}) collective-permute-start(bf16[400,128]{1,0:T(8,128)(2,1)S(1)} %get-tuple-element.73), channel_id=1, source_target_pairs={{0,4},{2,6},{4,0},{6,2},{1,5},{3,7},{5,1},{7,3},{8,12},{10,14},{12... | collective-permute-start | bytes 307208 | tf_op jit(solution)/shard_map/ppermute | solution.py:558
  156.6 4.2 %all-to-all-start.2 = ((bf16[4,400,128]{2,1,0:T(8,128)(2,1)}), bf16[4,400,128]{2,1,0:T(8,128)(2,1)S(1)}, u32[]{:S(2)}, u32[]{:S(2)}) async-start(bf16[4,400,128]{2,1,0:T(8,128)(2,1)} %add_convert_fusion), calls=%async_computation.2 | async-start | bytes 819200 | tf_op jit(solution)/shard_map/all_to_all | solution.py:567
  160.8 0.5 collective-permute-done.12
  161.3 0.2 collective-permute-done.13
  161.6 0.1 fusion.3
  161.7 5.5 %all-to-all-done.2 = bf16[4,400,128]{2,1,0:T(8,128)(2,1)S(1)} async-done(((bf16[4,400,128]{2,1,0:T(8,128)(2,1)}), bf16[4,400,128]{2,1,0:T(8,128)(2,1)S(1)}, u32[]{:S(2)}, u32[]{:S(2)}) %all-to-all-start.2) | async-done | bytes 409632 | tf_op jit(solution)/shard_map/all_to_all | solution.py:567
  167.3 0.1 fusion.4
  167.4 0.8 pad_maximum_fusion
  168.3 5.3 %all-to-all-start.3 = ((bf16[8,40,320]{2,1,0:T(8,128)(2,1)}), bf16[8,40,320]{2,1,0:T(8,128)(2,1)S(1)}, u32[]{:S(2)}, u32[]{:S(2)}) async-start(bf16[8,40,320]{2,1,0:T(8,128)(2,1)} %pad_maximum_fusion), calls=%async_computation.3 | async-start | bytes 491520 | tf_op jit(solution)/shard_map/all_to_all | solution.py:567
  173.5 9.2 %all-to-all-done.3 = bf16[8,40,320]{2,1,0:T(8,128)(2,1)S(1)} async-done(((bf16[8,40,320]{2,1,0:T(8,128)(2,1)}), bf16[8,40,320]{2,1,0:T(8,128)(2,1)S(1)}, u32[]{:S(2)}, u32[]{:S(2)}) %all-to-all-start.3) | async-done | bytes 204832 | tf_op jit(solution)/shard_map/all_to_all | solution.py:567
  182.8 1.8 collective-permute-start.14
  184.6 0.2 collective-permute-start.15
  184.7 2.3 %collective-permute-start.16 = (f32[40,320]{1,0:T(8,128)S(1)}, f32[40,320]{1,0:T(8,128)S(1)}, u32[]{:S(2)}, u32[]{:S(2)}) collective-permute-start(f32[40,320]{1,0:T(8,128)S(1)} %broadcast_multiply_fusion), channel_id=1, source_target_pairs={{0,6},{2,0},{4,2},{6,4},{1,7},{3,1},{5,3},{7,5},{8,14},{10,8},{12,... | collective-permute-start | bytes 153608 | tf_op jit(solution)/shard_map/ppermute | solution.py:547
  187.1 0.3 collective-permute-done.14
  187.4 1.8 collective-permute-done.15
  189.2 5.9 %collective-permute-start.17 = (f32[4,40,320]{2,1,0:T(8,128)S(1)}, f32[4,40,320]{2,1,0:T(8,128)S(1)}, u32[]{:S(2)}, u32[]{:S(2)}) collective-permute-start(f32[4,40,320]{2,1,0:T(8,128)S(1)} %bitcast_dynamic-update-slice_fusion.6), channel_id=1, source_target_pairs={{0,1},{1,0},{2,3},{3,2},{4,5},{5,4},{6,7},{7,6},{8,9},{9,8},{10,11... | collective-permute-start | bytes 614408 | tf_op jit(solution)/shard_map/ppermute | solution.py:547
  195.2 1.1 collective-permute-done.17
  196.3 0.1 fusion.5
  196.6 0.1 fusion.11
  196.7 0.1 fusion.13
  196.7 0.1 fusion.17
  196.8 0.1 fusion.15
  196.9 0.1 fusion.19
  197.0 0.7 concatenate.39
  197.7 0.8 concatenate.38
  (61 shorter events, 0.9 us)
Async XLA Ops:
  7.2 0.9 copy-start
  7.2 55.4 %all-gather.3.cloned.1.call-start = ((), (), s32[]{:S(2)}) async-start(), calls=%async_computation.4 | async-start | bytes 1843200 | tf_op jit(solution)/shard_map/all_gather | solution.py:592
  8.9 6.8 %collective-permute-start = (bf16[40,1664]{1,0:T(8,128)(2,1)S(1)}, bf16[40,1664]{1,0:T(8,128)(2,1)S(1)}, u32[]{:S(2)}, u32[]{:S(2)}) collective-permute-start(bf16[40,1664]{1,0:T(8,128)(2,1)S(1)} %pad_maximum_fusion.1), channel_id=1, source_target_pairs={{0,64},{64,128},{128,192},{192,0},{1,65},{65,129},{129,193},{193,1... | collective-permute-start | bytes 399368 | tf_op jit(solution)/shard_map/ppermute | solution.py:547
  11.1 8.4 %collective-permute-start.1 = (bf16[40,1664]{1,0:T(8,128)(2,1)S(1)}, bf16[40,1664]{1,0:T(8,128)(2,1)S(1)}, u32[]{:S(2)}, u32[]{:S(2)}) collective-permute-start(bf16[40,1664]{1,0:T(8,128)(2,1)S(1)} %pad_maximum_fusion.1), channel_id=1, source_target_pairs={{0,128},{64,192},{128,0},{192,64},{1,129},{65,193},{129,1},{193,65... | collective-permute-start | bytes 399368 | tf_op jit(solution)/shard_map/ppermute | solution.py:547
  13.7 5.8 %collective-permute-start.2 = (bf16[40,1664]{1,0:T(8,128)(2,1)S(1)}, bf16[40,1664]{1,0:T(8,128)(2,1)S(1)}, u32[]{:S(2)}, u32[]{:S(2)}) collective-permute-start(bf16[40,1664]{1,0:T(8,128)(2,1)S(1)} %pad_maximum_fusion.1), channel_id=1, source_target_pairs={{0,192},{64,0},{128,64},{192,128},{1,193},{65,1},{129,65},{193,129... | collective-permute-start | bytes 399368 | tf_op jit(solution)/shard_map/ppermute | solution.py:547
  24.7 5.9 %copy-start.4 = (f32[1280]{0:T(1024)S(1)}, f32[1280]{0:T(1024)}, u32[]{:S(2)}) copy-start(f32[1280]{0:T(1024)} %param.14) | copy-start | bytes 15364
  24.7 6.5 %copy-start.5 = (f32[1280]{0:T(1024)S(1)}, f32[1280]{0:T(1024)}, u32[]{:S(2)}) copy-start(f32[1280]{0:T(1024)} %param.15) | copy-start | bytes 15364
  24.8 37.8 %all-to-all-start = ((bf16[8,128,1280]{2,1,0:T(8,128)(2,1)}), bf16[8,128,1280]{2,1,0:T(8,128)(2,1)S(1)}, u32[]{:S(2)}, u32[]{:S(2)}) async-start(bf16[8,128,1280]{2,1,0:T(8,128)(2,1)} %bitcast.74), calls=%async_computation | async-start | bytes 5242880 | tf_op jit(solution)/shard_map/all_to_all | solution.py:567
  30.6 84.8 %all-gather.5.cloned.1.call-start = ((), (), s32[]{:S(2)}) async-start(), calls=%async_computation.5 | async-start | bytes 2949120 | tf_op jit(solution)/shard_map/all_gather | solution.py:592
  62.6 3.8 %copy-start.2 = (bf16[8,128,1280]{2,1,0:T(8,128)(2,1)}, bf16[8,128,1280]{2,1,0:T(8,128)(2,1)S(1)}, u32[]{:S(2)}) copy-start(bf16[8,128,1280]{2,1,0:T(8,128)(2,1)S(1)} %all-to-all-done) | copy-start | bytes 7864324
  72.9 18.6 %copy-start.6 = (bf16[1280,768]{1,0:T(8,128)(2,1)S(1)}, bf16[1280,768]{1,0:T(8,128)(2,1)}, u32[]{:S(2)}) copy-start(bf16[1280,768]{1,0:T(8,128)(2,1)} %get-tuple-element.37.incoming) | copy-start | bytes 5898244
  72.9 19.9 %copy-start.3 = (bf16[1280,768]{1,0:T(8,128)(2,1)S(1)}, bf16[1280,768]{1,0:T(8,128)(2,1)}, u32[]{:S(2)}) copy-start(bf16[1280,768]{1,0:T(8,128)(2,1)} %norm.1.normed) | copy-start | bytes 5898244
  88.8 5.7 %collective-permute-start.5 = (bf16[768,1280]{1,0:T(8,128)(2,1)}, bf16[768,1280]{1,0:T(8,128)(2,1)S(1)}, u32[]{:S(2)}, u32[]{:S(2)}) collective-permute-start(bf16[768,1280]{1,0:T(8,128)(2,1)} %get-tuple-element.42.zero.d_query.d_value), channel_id=1, source_target_pairs={{1,0},{3,2},{5,4},{7,6},{9,8},{11,10},{13,12},{15,14},{17,16},{19,... | collective-permute-start | bytes 5898248 | tf_op jit(solution)/shard_map/ppermute | solution.py:621
  90.2 6.1 %collective-permute-start.6 = (bf16[768,1280]{1,0:T(8,128)(2,1)}, bf16[768,1280]{1,0:T(8,128)(2,1)S(1)}, u32[]{:S(2)}, u32[]{:S(2)}) collective-permute-start(bf16[768,1280]{1,0:T(8,128)(2,1)} %get-tuple-element.43.one.d_key), channel_id=1, source_target_pairs={{0,1},{2,3},{4,5},{6,7},{8,9},{10,11},{12,13},{14,15},{16,17},{18,... | collective-permute-start | bytes 5898248 | tf_op jit(solution)/shard_map/ppermute | solution.py:622
  91.5 10.2 %collective-permute-start.4 = (bf16[1280,768]{1,0:T(8,128)(2,1)S(1)}, bf16[1280,768]{1,0:T(8,128)(2,1)S(1)}, u32[]{:S(2)}, u32[]{:S(2)}) collective-permute-start(bf16[1280,768]{1,0:T(8,128)(2,1)S(1)} %copy-done.6), channel_id=1, source_target_pairs={{0,1},{2,3},{4,5},{6,7},{8,9},{10,11},{12,13},{14,15},{16,17},{18,... | collective-permute-start | bytes 5898248 | tf_op jit(solution)/shard_map/ppermute | solution.py:610
  92.8 10.2 %collective-permute-start.3 = (bf16[1280,768]{1,0:T(8,128)(2,1)S(1)}, bf16[1280,768]{1,0:T(8,128)(2,1)}, u32[]{:S(2)}, u32[]{:S(2)}) collective-permute-start(bf16[1280,768]{1,0:T(8,128)(2,1)S(1)} %copy-done.3), channel_id=1, source_target_pairs={{0,1},{1,0},{2,3},{3,2},{4,5},{5,4},{6,7},{7,6},{8,9},{9,8},{10,11... | collective-permute-start | bytes 5898248 | tf_op jit(solution)/shard_map/ppermute | solution.py:538
  94.4 7.2 %copy-start.7 = (bf16[768,1280]{1,0:T(8,128)(2,1)}, bf16[768,1280]{1,0:T(8,128)(2,1)S(1)}, u32[]{:S(2)}) copy-start(bf16[768,1280]{1,0:T(8,128)(2,1)S(1)} %collective-permute-done.5.mate_zero) | copy-start | bytes 5898244
  96.2 5.4 %copy-start.8 = (bf16[768,1280]{1,0:T(8,128)(2,1)}, bf16[768,1280]{1,0:T(8,128)(2,1)S(1)}, u32[]{:S(2)}) copy-start(bf16[768,1280]{1,0:T(8,128)(2,1)S(1)} %collective-permute-done.6.mate_one) | copy-start | bytes 5898244
  101.7 1.3 copy-start.9
  117.5 7.0 %copy-start.1 = (bf16[4,8,40,1024]{3,2,1,0:T(8,128)(2,1)}, bf16[4,8,40,1024]{3,2,1,0:T(8,128)(2,1)S(1)}, u32[]{:S(2)}) copy-start(bf16[4,8,40,1024]{3,2,1,0:T(8,128)(2,1)S(1)} %copy.29) | copy-start | bytes 7864324
  117.5 12.9 %collective-permute-start.10 = (bf16[1280,1024]{1,0:T(8,128)(2,1)S(1)}, bf16[1280,1024]{1,0:T(8,128)(2,1)}, u32[]{:S(2)}, u32[]{:S(2)}) collective-permute-start(bf16[1280,1024]{1,0:T(8,128)(2,1)S(1)} %bitcast.70), channel_id=1, source_target_pairs={{0,1},{1,0},{2,3},{3,2},{4,5},{5,4},{6,7},{7,6},{8,9},{9,8},{10,11... | collective-permute-start | bytes 7864328 | tf_op jit(solution)/shard_map/ppermute | solution.py:538
  117.7 31.0 %all-to-all-start.1 = ((bf16[4,4,400,128]{3,2,1,0:T(8,128)(2,1)}), bf16[4,4,400,128]{3,2,1,0:T(8,128)(2,1)}, u32[]{:S(2)}, u32[]{:S(2)}) async-start(bf16[4,4,400,128]{3,2,1,0:T(8,128)(2,1)} %get-tuple-element.47), calls=%async_computation.1 | async-start | bytes 3276800 | tf_op jit(solution)/shard_map/all_to_all | solution.py:567
  124.5 17.3 %collective-permute-start.7 = (bf16[4,400,128]{2,1,0:T(8,128)(2,1)}, bf16[4,400,128]{2,1,0:T(8,128)(2,1)}, u32[]{:S(2)}, u32[]{:S(2)}) collective-permute-start(bf16[4,400,128]{2,1,0:T(8,128)(2,1)} %get-tuple-element.61), channel_id=1, source_target_pairs={{0,2},{2,4},{4,6},{6,0},{1,3},{3,5},{5,7},{7,1},{8,10},{10,12},{12... | collective-permute-start | bytes 1228808 | tf_op jit(solution)/shard_map/ppermute | solution.py:558
  127.4 21.3 %collective-permute-start.8 = (bf16[4,400,128]{2,1,0:T(8,128)(2,1)}, bf16[4,400,128]{2,1,0:T(8,128)(2,1)}, u32[]{:S(2)}, u32[]{:S(2)}) collective-permute-start(bf16[4,400,128]{2,1,0:T(8,128)(2,1)} %get-tuple-element.60), channel_id=1, source_target_pairs={{0,4},{2,6},{4,0},{6,2},{1,5},{3,7},{5,1},{7,3},{8,12},{10,14},{12... | collective-permute-start | bytes 1228808 | tf_op jit(solution)/shard_map/ppermute | solution.py:558
  130.4 18.2 %collective-permute-start.9 = (bf16[4,400,128]{2,1,0:T(8,128)(2,1)S(1)}, bf16[4,400,128]{2,1,0:T(8,128)(2,1)}, u32[]{:S(2)}, u32[]{:S(2)}) collective-permute-start(bf16[4,400,128]{2,1,0:T(8,128)(2,1)S(1)} %get-tuple-element.59), channel_id=1, source_target_pairs={{0,6},{2,0},{4,2},{6,4},{1,7},{3,1},{5,3},{7,5},{8,14},{10,8},{12,... | collective-permute-start | bytes 1228808 | tf_op jit(solution)/shard_map/ppermute | solution.py:558
  152.7 8.1 %collective-permute-start.11 = (bf16[400,128]{1,0:T(8,128)(2,1)S(1)}, bf16[400,128]{1,0:T(8,128)(2,1)S(1)}, u32[]{:S(2)}, u32[]{:S(2)}) collective-permute-start(bf16[400,128]{1,0:T(8,128)(2,1)S(1)} %get-tuple-element.71), channel_id=1, source_target_pairs={{0,2},{2,4},{4,6},{6,0},{1,3},{3,5},{5,7},{7,1},{8,10},{10,12},{12... | collective-permute-start | bytes 307208 | tf_op jit(solution)/shard_map/ppermute | solution.py:558
  153.6 7.7 %collective-permute-start.12 = (bf16[400,128]{1,0:T(8,128)(2,1)S(1)}, bf16[400,128]{1,0:T(8,128)(2,1)S(1)}, u32[]{:S(2)}, u32[]{:S(2)}) collective-permute-start(bf16[400,128]{1,0:T(8,128)(2,1)S(1)} %get-tuple-element.73), channel_id=1, source_target_pairs={{0,4},{2,6},{4,0},{6,2},{1,5},{3,7},{5,1},{7,3},{8,12},{10,14},{12... | collective-permute-start | bytes 307208 | tf_op jit(solution)/shard_map/ppermute | solution.py:558
  156.6 4.9 %collective-permute-start.13 = (bf16[400,128]{1,0:T(8,128)(2,1)S(1)}, bf16[400,128]{1,0:T(8,128)(2,1)S(1)}, u32[]{:S(2)}, u32[]{:S(2)}) collective-permute-start(bf16[400,128]{1,0:T(8,128)(2,1)S(1)} %get-tuple-element.72), channel_id=1, source_target_pairs={{0,6},{2,0},{4,2},{6,4},{1,7},{3,1},{5,3},{7,5},{8,14},{10,8},{12,... | collective-permute-start | bytes 307208 | tf_op jit(solution)/shard_map/ppermute | solution.py:558
  156.6 10.6 %all-to-all-start.2 = ((bf16[4,400,128]{2,1,0:T(8,128)(2,1)}), bf16[4,400,128]{2,1,0:T(8,128)(2,1)S(1)}, u32[]{:S(2)}, u32[]{:S(2)}) async-start(bf16[4,400,128]{2,1,0:T(8,128)(2,1)} %add_convert_fusion), calls=%async_computation.2 | async-start | bytes 819200 | tf_op jit(solution)/shard_map/all_to_all | solution.py:567
  168.3 14.5 %all-to-all-start.3 = ((bf16[8,40,320]{2,1,0:T(8,128)(2,1)}), bf16[8,40,320]{2,1,0:T(8,128)(2,1)S(1)}, u32[]{:S(2)}, u32[]{:S(2)}) async-start(bf16[8,40,320]{2,1,0:T(8,128)(2,1)} %pad_maximum_fusion), calls=%async_computation.3 | async-start | bytes 491520 | tf_op jit(solution)/shard_map/all_to_all | solution.py:567
  182.8 4.6 %collective-permute-start.14 = (f32[40,320]{1,0:T(8,128)S(1)}, f32[40,320]{1,0:T(8,128)S(1)}, u32[]{:S(2)}, u32[]{:S(2)}) collective-permute-start(f32[40,320]{1,0:T(8,128)S(1)} %broadcast_multiply_fusion), channel_id=1, source_target_pairs={{0,2},{2,4},{4,6},{6,0},{1,3},{3,5},{5,7},{7,1},{8,10},{10,12},{12... | collective-permute-start | bytes 153608 | tf_op jit(solution)/shard_map/ppermute | solution.py:547
  184.6 4.6 %collective-permute-start.15 = (f32[40,320]{1,0:T(8,128)S(1)}, f32[40,320]{1,0:T(8,128)S(1)}, u32[]{:S(2)}, u32[]{:S(2)}) collective-permute-start(f32[40,320]{1,0:T(8,128)S(1)} %broadcast_multiply_fusion), channel_id=1, source_target_pairs={{0,4},{2,6},{4,0},{6,2},{1,5},{3,7},{5,1},{7,3},{8,12},{10,14},{12... | collective-permute-start | bytes 153608 | tf_op jit(solution)/shard_map/ppermute | solution.py:547
  184.7 4.4 %collective-permute-start.16 = (f32[40,320]{1,0:T(8,128)S(1)}, f32[40,320]{1,0:T(8,128)S(1)}, u32[]{:S(2)}, u32[]{:S(2)}) collective-permute-start(f32[40,320]{1,0:T(8,128)S(1)} %broadcast_multiply_fusion), channel_id=1, source_target_pairs={{0,6},{2,0},{4,2},{6,4},{1,7},{3,1},{5,3},{7,5},{8,14},{10,8},{12,... | collective-permute-start | bytes 153608 | tf_op jit(solution)/shard_map/ppermute | solution.py:547
  189.2 7.1 %collective-permute-start.17 = (f32[4,40,320]{2,1,0:T(8,128)S(1)}, f32[4,40,320]{2,1,0:T(8,128)S(1)}, u32[]{:S(2)}, u32[]{:S(2)}) collective-permute-start(f32[4,40,320]{2,1,0:T(8,128)S(1)} %bitcast_dynamic-update-slice_fusion.6), channel_id=1, source_target_pairs={{0,1},{1,0},{2,3},{3,2},{4,5},{5,4},{6,7},{7,6},{8,9},{9,8},{10,11... | collective-permute-start | bytes 614408 | tf_op jit(solution)/shard_map/ppermute | solution.py:547
Sparse Core Ops, SparseCore 0:
  20.4 39.5 all-gather.2
  63.6 40.6 all-gather.4

commit v3 on v2

--- a/solution.py
+++ b/solution.py
@@ -88,6 +88,7 @@
         table[JOINED + b] = 0
         table[META + b] = 0
     table[META + 1] = place[1]
+    table[META + 3] = place[2]
 
     def step(at):
         here = segment[at]
@@ -274,8 +275,15 @@
     )(table, qkv)
 
 
-def incoming_kernel(table, arrived, w, incoming, d_attn, incoming_t, landing, sems, *, tiles):
+def incoming_kernel(table, arrived, spread, incoming, d_attn, incoming_t, landing, w, sems, *, tiles):
     t = pl.program_id(0)
+    places = AXES["y"]
+    piece = spread.shape[0]
+
+    def w_copy(y):
+        return pltpu.make_async_copy(
+            spread.at[:, pl.ds(y * HW, HW)], w.at[pl.ds(y * piece, piece)], sems.at[tiles + y]
+        )
 
     def row_copy(j, source):
         first_row = pl.multiple_of(source * TILE, TILE)
@@ -285,6 +293,8 @@
 
     @pl.when(t == 0)
     def _():
+        for y in range(places):
+            w_copy(y).start()
         for j in range(tiles):
             source = table[SOURCE + j]
 
@@ -302,10 +312,16 @@
     rows = landing[pl.ds(pl.multiple_of(t * WINDOW, WINDOW), WINDOW)]
     incoming[...] = rows
     incoming_t[...] = jnp.transpose(rows)
+
+    @pl.when(t == 0)
+    def _():
+        for y in range(places):
+            w_copy(y).wait()
+
     d_attn[...] = matmul(rows, w[...]).astype(bf16)
 
 
-def place_incoming(table, arrived, w, rows):
+def place_incoming(table, arrived, spread, rows):
     width = arrived.shape[1]
     return pl.pallas_call(
         functools.partial(incoming_kernel, tiles=rows // TILE),
@@ -314,7 +330,7 @@
             grid=(rows // WINDOW,),
             in_specs=[
                 pl.BlockSpec(memory_space=pl.ANY),
-                pl.BlockSpec((width, HW), lambda i, t: (0, 0)),
+                pl.BlockSpec(memory_space=pl.ANY),
             ],
             out_specs=(
                 pl.BlockSpec((WINDOW, width), lambda i, t: (i, 0)),
@@ -323,7 +339,8 @@
             ),
             scratch_shapes=[
                 pltpu.VMEM((rows, width), bf16),
-                pltpu.SemaphoreType.DMA((rows // TILE,)),
+                pltpu.VMEM((width, HW), bf16),
+                pltpu.SemaphoreType.DMA((rows // TILE + AXES["y"],)),
             ],
         ),
         out_shape=(
@@ -334,7 +351,7 @@
         compiler_params=params(),
         cost_estimate=cost(2 * rows * width * HW, 10 * rows * width),
         name="incoming",
-    )(table, arrived, w)
+    )(table, arrived, spread)
 
 
 def add_lanes(tiles, low, part):
@@ -463,7 +480,7 @@
     )(table, x, incoming, gain.reshape(1, width), value_query, attended_key, value_query, own_w, mate_w)
 
 
-def packed_columns(total, out):
+def packed_columns(total, store):
     rows = total.shape[0]
     group = rows // 4
     fifth = total[:, 512:640]
@@ -474,8 +491,7 @@
             piece = fifth[g * group : (g + 1) * group]
             shift = (g - x) * 32 % 128
             packed = jnp.where(quarter == g, pltpu.roll(piece, shift, 1) if shift else piece, packed)
-        out[x, :rows] = total[:, x * 128 : (x + 1) * 128].astype(bf16)
-        out[x, rows:] = packed.astype(bf16)
+        store(x, jnp.concatenate([total[:, x * 128 : (x + 1) * 128], packed], axis=0).astype(bf16))
 
 
 def weight_kernel(
@@ -498,25 +514,35 @@
     normed_both = jnp.concatenate([normed[...], mate_normed[...]], axis=1)
     incoming_both = jnp.concatenate([incoming[...], mate_incoming[...]], axis=1)
     left = jnp.where(first, normed_both, incoming_both)
-    packed_columns(matmul(left, right[:, :HW]), by_y)
-    packed_columns(matmul(normed_both, right[:, HW:]), by_x)
+    to_y, to_x = matmul(left, right[:, :HW]), matmul(normed_both, right[:, HW:])
+    piece = to_y.shape[0] // 2
+    for i in range(2):
+
+        def store_y(x, value):
+            by_y[i, x] = value
+
+        def store_x(x, value):
+            by_x[lax.rem(x - table[META + 3] + 4, 4), i] = value
+
+        packed_columns(to_y[i * piece : (i + 1) * piece], store_y)
+        packed_columns(to_x[i * piece : (i + 1) * piece], store_x)
 
 
 def weight_parts(table, normed, mate_normed, incoming, mate_incoming, rights):
     width, rows = normed.shape
     piece = width // 4
     packed = piece * 5 // 4
-    left = pl.BlockSpec((piece, rows), lambda i, t: (i, 0))
-    on_one = pl.BlockSpec((piece, rows), lambda i, t: (i * t[META + 1], 0))
+    left = pl.BlockSpec((2 * piece, rows), lambda i, t: (i, 0))
+    on_one = pl.BlockSpec((2 * piece, rows), lambda i, t: (i * t[META + 1], 0))
     return pl.pallas_call(
         weight_kernel,
         grid_spec=pltpu.PrefetchScalarGridSpec(
             num_scalar_prefetch=1,
-            grid=(4,),
+            grid=(2,),
             in_specs=[left, left, on_one, on_one] + [pl.BlockSpec(memory_space=pl.ANY)] * 4,
             out_specs=(
-                pl.BlockSpec((None, 4, packed, 128), lambda i, t: (i, 0, 0, 0)),
-                pl.BlockSpec((4, None, packed, 128), lambda i, t: (0, i, 0, 0)),
+                pl.BlockSpec((2, 4, packed, 128), lambda i, t: (i, 0, 0, 0)),
+                pl.BlockSpec((4, 2, packed, 128), lambda i, t: (0, i, 0, 0)),
             ),
             scratch_shapes=[pltpu.VMEM((2 * rows, 2 * HW), bf16), pltpu.SemaphoreType.DMA((2,))],
         ),
@@ -549,14 +575,16 @@
     return out
 
 
-def sent_to_owners(value, axis):
+def sent_by_distance(value, axis):
     count = AXES[axis]
-    here = lax.axis_index(axis)
-    parts = [lax.dynamic_index_in_dim(value, here, 0, keepdims=False)]
-    for k in range(1, count):
-        part = lax.dynamic_index_in_dim(value, lax.rem(here + k, count), 0, keepdims=False)
-        parts.append(lax.ppermute(part, axis, [(i, (i + k) % count) for i in range(count)]))
-    return parts
+    return [value[0]] + [
+        lax.ppermute(value[k], axis, [(i, (i + k) % count) for i in range(count)])
+        for k in range(1, count)
+    ]
+
+
+def by_distance(value, axis):
+    return jnp.roll(value, -lax.axis_index(axis), axis=0)
 
 
 def added(parts):
@@ -583,31 +611,26 @@
     section = ("x", "core")
     sections = AXES["x"] * AXES["core"]
     core = lax.axis_index("core")
-    place = jnp.stack([lax.axis_index(section), core]).astype(jnp.int32)
-
-    columns = jnp.concatenate([w_out, lax.dynamic_slice_in_dim(w_qkv, 896 * core, 1024, axis=1)], axis=1)
-    columns = gathered(columns, "y").reshape(4 * w_out.shape[0], HW + 1024)
-
-    def gathered_z(value):
-        return lax.all_gather(value, "z", axis=0, tiled=True)
-
-    def in_order(whole):
-        return jnp.swapaxes(whole.reshape(8, 4, -1, whole.shape[1]), 0, 1).reshape(whole.shape)
-
+    place = jnp.stack([lax.axis_index(section), core, lax.axis_index("x")]).astype(jnp.int32)
+
+    spread = gathered(w_out, "y")
+    spread = jnp.concatenate(
+        [spread[y] for y in range(4)] + [lax.dynamic_slice_in_dim(w_qkv, 896 * core, 1024, axis=1)], axis=1
+    )
     table, outgoing = route(image_patches, image_owner, place, grad_rows, own_tiles, sections)
     arrived = exchanged(outgoing, section)
-    out_w = gathered_z(columns[:, :HW])
+    spread = lax.all_gather(spread, "z", axis=0, tiled=True)
     normed_t = norm_transposed(layer_input, norm_gain, norm_bias)
+    mate_normed_t = to_mate(normed_t)
     attended, attended_t, weights = forward(table, saved_qkv)
-    out_w, arrived, attended_t, normed_t, columns = lax.optimization_barrier(
-        (out_w, arrived, attended_t, normed_t, columns)
+    spread, arrived, attended_t, normed_t = lax.optimization_barrier(
+        (spread, arrived, attended_t, normed_t)
     )
-    mate_normed_t = to_mate(normed_t)
-    out_w = in_order(out_w)
-    qkv_w = gathered_z(columns[:, HW:])
-
-    incoming, d_attn, incoming_t = place_incoming(table, arrived, out_w, own_tiles * TILE)
+    qkv_w = lax.all_gather(spread[:, 4 * HW :], "y", axis=0, tiled=True)
+
+    incoming, d_attn, incoming_t = place_incoming(table, arrived, spread, own_tiles * TILE)
     mate_incoming_t = lax.ppermute(incoming_t, "core", [(0, 1)])
+    d_attn, mate_normed_t = lax.optimization_barrier((d_attn, mate_normed_t))
     value_query, attended_key = backward(table, saved_qkv, d_attn, attended, attended_t, weights)
     first, second = weight_parts(
         table,
@@ -623,18 +646,20 @@
         ),
     )
     first, second, qkv_w = lax.optimization_barrier((first, second, qkv_w))
-    qkv_w = in_order(qkv_w)
     layer_grad = norm_back(
         table, layer_input, incoming, norm_gain, value_query, attended_key, qkv_w, to_mate(qkv_w)
     )
     first = exchanged(first, "y")
-    second = sent_to_owners(second, "x")
+    second = sent_by_distance(second, "x")
     first, second, layer_grad = lax.optimization_barrier((first, second, layer_grad))
     second = added(second).astype(bf16)
     first, second = lax.optimization_barrier((first, second))
     second = exchanged(second, "y")
-    first = added(sent_to_owners(jnp.sum(first.astype(f32), axis=0).astype(bf16), "x"))
+    first = by_distance(jnp.sum(first.astype(f32), axis=0).astype(bf16), "x")
+    first = sent_by_distance(first, "x")
     second = jnp.sum(second.astype(f32), axis=0)
+    first, second = lax.optimization_barrier((first, second))
+    first = added(first)
     columns = jnp.concatenate([unpacked(first), unpacked(second)], axis=1).astype(bf16)
     by_z = exchanged(columns.reshape(8, 40, 320), "z")
     share = jnp.sum(by_z.astype(f32), axis=0) / (AXES["y"] * AXES["z"] * sections)

time: 207 us -> 191 us (0.923)
  Pallas kernels: 70.7 us -> 65.6 us
  local copies, waits for them, and re-layouts: 15 us -> 9.99 us
  other arithmetic: 7.29 us -> 3.16 us
  waiting for transfers between devices: 46.5 us -> 43.5 us
    transpose x2 -> x0, local copies, waits for them, and re-layouts: 4.96 us -> none  [in_order(): jnp.swapaxes(whole.reshape(8, 4, -1, whole.shape[1]), 0, 1)]
    ppermute x1, starting transfers between devices: 1.4 us -> 5.07 us  [on_device(): lax.ppermute(value_query, 'core', [(1, 0)])]
    pallas_call x1, Pallas kernels: 15.9 us -> 13 us  [backward(): pl.pallas_call(backward_kernel, grid_spec=pltpu.PrefetchScalarGridSpec(nu...]
    pallas_call x1, Pallas kernels: 15 us -> 12.1 us  [forward(): pl.pallas_call(forward_kernel, grid_spec=pltpu.PrefetchScalarGridSpec(num...]
    ppermute x1, waiting for transfers between devices: 5.41 us -> 2.6 us  [on_device(): mate_incoming_t = lax.ppermute(incoming_t, 'core', [(0, 1)])]
    ppermute x7, starting transfers between devices: 16.1 us -> 14 us  [gathered(): lax.ppermute(value, axis, [(i, (i + k) % count) for i in range(count)])]
  transfers between devices with their start and end apart: 24 -> 24, of which waited for: 12 -> 15; matrix products, arithmetic and copies ran while one was open for 4% -> 3% of each run, Pallas kernels for 34% -> 35%
where the time goes in v3:
time: 191 us; the launch traced here: 190 us
  Pallas kernels  65.6 us (34%)
  starting transfers between devices  53.4 us (28%)
  waiting for transfers between devices  43.5 us (23%)
  between operations  14.4 us (8%)
  local copies, waits for them, and re-layouts  9.99 us (5%)
  other arithmetic  3.16 us (2%)
    all_to_all x4, waiting for transfers between devices, exchanged(): return lax.all_to_all(value, axes, split_axis=0, concat_axis=0, tiled=True)  24.1 us
    all_to_all x4, starting transfers between devices, exchanged(): return lax.all_to_all(value, axes, split_axis=0, concat_axis=0, tiled=True)  20.3 us
    ppermute x7, starting transfers between devices, gathered(): lax.ppermute(value, axis, [(i, (i + k) % count) for i in range(count)])  14 us
    pallas_call x1, Pallas kernels, weight_parts(): pl.pallas_call(weight_kernel, grid_spec=pltpu.PrefetchScalarGridSpec(num_...  13.2 us
    pallas_call x1, Pallas kernels, backward(): pl.pallas_call(backward_kernel, grid_spec=pltpu.PrefetchScalarGridSpec(nu...  13 us
    pallas_call x1, Pallas kernels, forward(): pl.pallas_call(forward_kernel, grid_spec=pltpu.PrefetchScalarGridSpec(num...  12.1 us
    pallas_call x1, Pallas kernels, norm_back(): pl.pallas_call(norm_back_kernel, grid_spec=pltpu.PrefetchScalarGridSpec(n...  11.4 us
    ppermute x6, starting transfers between devices, sent_by_distance(): lax.ppermute(value[k], axis, [(i, (i + k) % count) for i in range(count)])  11.1 us
  transfers between devices with their start and end apart: 24, of which 15 were waited for; matrix products, arithmetic and copies ran while one was open for 3% of the time, Pallas kernels for 35%

profile of v3, /device:TPU:1, one launch (start us, length us, event | category | flops | bytes accessed | tf_op | source)
XLA Modules:
  0.0 190.0 jit_solution(15921213273081318510)
XLA Ops:
  7.2 2.2 %collective-permute-start = (bf16[40,640]{1,0:T(8,128)(2,1)}, bf16[40,640]{1,0:T(8,128)(2,1)S(1)}, u32[]{:S(2)}, u32[]{:S(2)}) collective-permute-start(bf16[40,640]{1,0:T(8,128)(2,1)} %param.17), channel_id=1, source_target_pairs={{0,64},{64,128},{128,192},{192,0},{1,65},{65,129},{129,193},{193,1... | collective-permute-start | bytes 153608 | tf_op jit(solution)/shard_map/ppermute | solution.py:573
  9.4 2.6 %collective-permute-start.1 = (bf16[40,640]{1,0:T(8,128)(2,1)}, bf16[40,640]{1,0:T(8,128)(2,1)S(1)}, u32[]{:S(2)}, u32[]{:S(2)}) collective-permute-start(bf16[40,640]{1,0:T(8,128)(2,1)} %param.17), channel_id=1, source_target_pairs={{0,128},{64,192},{128,0},{192,64},{1,129},{65,193},{129,1},{193,65... | collective-permute-start | bytes 153608 | tf_op jit(solution)/shard_map/ppermute | solution.py:573
  12.0 1.1 collective-permute-start.2
  13.1 0.8 bitcast_dynamic-update-slice_fusion.9
  14.0 0.3 collective-permute-done.1
  14.3 1.2 collective-permute-done.2
  15.6 0.9 dynamic-slice_dynamic-update-slice_fusion
  16.5 0.7 copy-done.3
  17.2 0.6 pad_add_fusion.place
  17.8 3.9 %route.1 = (s32[32]{0:T(128)}, bf16[1024,1280]{1,0:T(8,128)(2,1)}) custom-call(s32[1,32]{1,0:T(1,128)} %patches.1, s32[1,32]{1,0:T(1,128)} %owners.1, s32[3]{0:T(128)} %pad_add_fusion.place, bf16[512,1280]{1,0:T(8,128)(2,1)} %rows.1), custom_call_target="tpu_custom_call" | custom-call | bytes 2621440 | tf_op jit(solution)/shard_map/route/pallas_call | solution.py:135
  21.7 6.4 %all-to-all-start = ((bf16[8,128,1280]{2,1,0:T(8,128)(2,1)}), bf16[8,128,1280]{2,1,0:T(8,128)(2,1)S(1)}, u32[]{:S(2)}, u32[]{:S(2)}) async-start(bf16[8,128,1280]{2,1,0:T(8,128)(2,1)} %bitcast.78), calls=%async_computation | async-start | bytes 5242880 | tf_op jit(solution)/shard_map/all_to_all | solution.py:595
  28.1 0.6 reshape.33.gain
  28.7 0.6 reshape.34.bias
  29.3 5.8 %norm.1.normed = bf16[1280,768]{1,0:T(8,128)(2,1)} custom-call(bf16[768,1280]{1,0:T(8,128)(2,1)} %x.3, f32[1,1280]{1,0:T(1,128)} %reshape.33.gain, f32[1,1280]{1,0:T(1,128)} %reshape.34.bias), custom_call_target="tpu_custom_call" | custom-call | flops 1000000 | bytes 100000 | tf_op jit(solution)/shard_map/norm/pallas_call | solution.py:166
  35.2 12.1 %attend.1 = (bf16[768,640]{1,0:T(8,128)(2,1)}, bf16[4,640,256]{2,1,0:T(8,128)(2,1)}, bf16[4,8,256,256]{3,2,1,0:T(8,128)(2,1)}) custom-call(s32[32]{0:T(128)} %get-tuple-element.37.table, bf16[768,1920]{1,0:T(8,128)(2,1)} %qkv.3), custom_call_target="tpu_custom_call" | custom-call | flops 1000000 | bytes 100000 | tf_op jit(solution)/shard_map/attend/pallas_call | solution.py:255
  47.3 12.7 %all-to-all-done = bf16[8,128,1280]{2,1,0:T(8,128)(2,1)S(1)} async-done(((bf16[8,128,1280]{2,1,0:T(8,128)(2,1)}), bf16[8,128,1280]{2,1,0:T(8,128)(2,1)S(1)}, u32[]{:S(2)}, u32[]{:S(2)}) %all-to-all-start) | async-done | bytes 2621472 | tf_op jit(solution)/shard_map/all_to_all | solution.py:595
  60.0 2.4 %slice.269 = bf16[320,1024]{1,0:T(8,128)(2,1)} slice(bf16[320,3584]{1,0:T(8,128)(2,1)} %all-gather.3.cloned.1.call-done.spread), slice={[0:320], [2560:3584]} | slice | bytes 1310720 | tf_op jit(solution)/shard_map/slice | solution.py:629
  62.5 6.1 %incoming.1 = (bf16[768,1280]{1,0:T(8,128)(2,1)}, bf16[768,640]{1,0:T(8,128)(2,1)}, bf16[1280,768]{1,0:T(8,128)(2,1)}) custom-call(s32[32]{0:T(128)} %get-tuple-element.37.table, bf16[1024,1280]{1,0:T(8,128)(2,1)} %bitcast.77, bf16[320,3584]{1,0:T(8,128)(2,1)} %all-gather.3.cloned.1.call-done.spread), custom_call_target="tpu_custom_call" | custom-call | flops 1258291200 | bytes 9830400 | tf_op jit(solution)/shard_map/incoming/pallas_call | solution.py:326
  68.7 13.0 %attend_back.1 = (bf16[768,1280]{1,0:T(8,128)(2,1)}, bf16[768,1280]{1,0:T(8,128)(2,1)}) custom-call(s32[32]{0:T(128)} %get-tuple-element.37.table, bf16[768,1920]{1,0:T(8,128)(2,1)} %qkv.3, bf16[768,640]{1,0:T(8,128)(2,1)} %get-tuple-element.46.d_attn, bf16[768,640]{1,0:T(8,128)(2,1)} %get-tuple-element.47.attended, ...), custom_call_target="tpu_custom_call" | custom-call | flops 12000000000 | bytes 20000000 | tf_op jit(solution)/shard_map/attend_back/pallas_call | solution.py:399
  81.7 5.1 %collective-permute-start.5 = (bf16[768,1280]{1,0:T(8,128)(2,1)}, bf16[768,1280]{1,0:T(8,128)(2,1)S(1)}, u32[]{:S(2)}, u32[]{:S(2)}) collective-permute-start(bf16[768,1280]{1,0:T(8,128)(2,1)} %get-tuple-element.50.zero.d_query.d_value), channel_id=1, source_target_pairs={{1,0},{3,2},{5,4},{7,6},{9,8},{11,10},{13,12},{15,14},{17,16},{19,... | collective-permute-start | bytes 5898248 | tf_op jit(solution)/shard_map/ppermute | solution.py:644
  86.8 1.3 collective-permute-start.6
  88.1 1.5 collective-permute-start.4
  89.6 0.9 collective-permute-done.5.mate_zero
  90.4 2.5 %collective-permute-done.6.mate_one = bf16[768,1280]{1,0:T(8,128)(2,1)} collective-permute-done((bf16[768,1280]{1,0:T(8,128)(2,1)}, bf16[768,1280]{1,0:T(8,128)(2,1)}, u32[]{:S(2)}, u32[]{:S(2)}) %collective-permute-start.6) | collective-permute-done | bytes 1966112 | tf_op jit(solution)/shard_map/ppermute | solution.py:645
  93.0 2.6 %collective-permute-done.4.mate_incoming = bf16[1280,768]{1,0:T(8,128)(2,1)} collective-permute-done((bf16[1280,768]{1,0:T(8,128)(2,1)S(1)}, bf16[1280,768]{1,0:T(8,128)(2,1)}, u32[]{:S(2)}, u32[]{:S(2)}) %collective-permute-start.4) | collective-permute-done | bytes 1966112 | tf_op jit(solution)/shard_map/ppermute | solution.py:632
  95.6 13.2 %weight_parts.1 = (bf16[4,4,400,128]{3,2,1,0:T(8,128)(2,1)}, bf16[4,4,400,128]{3,2,1,0:T(8,128)(2,1)}) custom-call(s32[32]{0:T(128)} %get-tuple-element.37.table, bf16[1280,768]{1,0:T(8,128)(2,1)} %norm.1.normed, bf16[1280,768]{1,0:T(8,128)(2,1)} %collective-permute-done.3.mate_normed, bf16[1280,768]{1,0:T(8,128)(2,1)} %get-tuple-element.45.incoming, ...), custom_call_target="tpu_custom_call" | custom-call | flops 5033164800 | bytes 11141120 | tf_op jit(solution)/shard_map/weight_parts/pallas_call | solution.py:537
  108.8 0.1 collective-permute-start.10
  108.9 4.0 %all-to-all-start.1 = ((bf16[4,4,400,128]{3,2,1,0:T(8,128)(2,1)}), bf16[4,4,400,128]{3,2,1,0:T(8,128)(2,1)S(1)}, u32[]{:S(2)}, u32[]{:S(2)}) async-start(bf16[4,4,400,128]{3,2,1,0:T(8,128)(2,1)} %get-tuple-element.54), calls=%async_computation.1 | async-start | bytes 3276800 | tf_op jit(solution)/shard_map/all_to_all | solution.py:595
  112.9 1.2 slice_bitcast_fusion
  114.1 3.5 %collective-permute-start.7 = (bf16[4,400,128]{2,1,0:T(8,128)(2,1)}, bf16[4,400,128]{2,1,0:T(8,128)(2,1)S(1)}, u32[]{:S(2)}, u32[]{:S(2)}) collective-permute-start(bf16[4,400,128]{2,1,0:T(8,128)(2,1)} %get-tuple-element.73), channel_id=1, source_target_pairs={{0,2},{2,4},{4,6},{6,0},{1,3},{3,5},{5,7},{7,1},{8,10},{10,12},{12... | collective-permute-start | bytes 1228808 | tf_op jit(solution)/shard_map/ppermute | solution.py:581
  117.6 2.3 %collective-permute-start.8 = (bf16[4,400,128]{2,1,0:T(8,128)(2,1)}, bf16[4,400,128]{2,1,0:T(8,128)(2,1)S(1)}, u32[]{:S(2)}, u32[]{:S(2)}) collective-permute-start(bf16[4,400,128]{2,1,0:T(8,128)(2,1)} %get-tuple-element.72), channel_id=1, source_target_pairs={{0,4},{2,6},{4,0},{6,2},{1,5},{3,7},{5,1},{7,3},{8,12},{10,14},{12... | collective-permute-start | bytes 1228808 | tf_op jit(solution)/shard_map/ppermute | solution.py:581
  119.9 1.1 collective-permute-start.9
  121.0 11.4 %norm_back.1 = bf16[768,1280]{1,0:T(8,128)(2,1)} custom-call(s32[32]{0:T(128)} %get-tuple-element.37.table, bf16[768,1280]{1,0:T(8,128)(2,1)} %x.3, bf16[768,1280]{1,0:T(8,128)(2,1)} %get-tuple-element.56.incoming, f32[1,1280]{1,0:T(1,128)} %reshape.33.gain, bf16[768,1280]{1,0:T(8,128)(2,1)} %get-tuple-element.50.zero.d_query.d_value, ...), custom_call_target="tpu_custom_call" | custom-call | flops 3774873600 | bytes 20000000 | tf_op jit(solution)/shard_map/norm_back/pallas_call | solution.py:459
  132.4 5.7 %collective-permute-done.8 = bf16[4,400,128]{2,1,0:T(8,128)(2,1)S(1)} collective-permute-done((bf16[4,400,128]{2,1,0:T(8,128)(2,1)}, bf16[4,400,128]{2,1,0:T(8,128)(2,1)S(1)}, u32[]{:S(2)}, u32[]{:S(2)}) %collective-permute-start.8) | collective-permute-done | bytes 409632 | tf_op jit(solution)/shard_map/ppermute | solution.py:581
  138.1 1.0 add_convert_fusion
  139.1 0.4 reduce_sum.30
  139.5 3.9 %all-to-all-start.2 = ((bf16[4,400,128]{2,1,0:T(8,128)(2,1)}), bf16[4,400,128]{2,1,0:T(8,128)(2,1)S(1)}, u32[]{:S(2)}, u32[]{:S(2)}) async-start(bf16[4,400,128]{2,1,0:T(8,128)(2,1)} %add_convert_fusion), calls=%async_computation.2 | async-start | bytes 819200 | tf_op jit(solution)/shard_map/all_to_all | solution.py:595
  143.4 0.2 fusion
  143.6 1.1 collective-permute-start.11
  144.7 3.0 %collective-permute-start.12 = (bf16[400,128]{1,0:T(8,128)(2,1)S(1)}, bf16[400,128]{1,0:T(8,128)(2,1)S(1)}, u32[]{:S(2)}, u32[]{:S(2)}) collective-permute-start(bf16[400,128]{1,0:T(8,128)(2,1)S(1)} %get-tuple-element.84), channel_id=1, source_target_pairs={{0,4},{2,6},{4,0},{6,2},{1,5},{3,7},{5,1},{7,3},{8,12},{10,14},{12... | collective-permute-start | bytes 307208 | tf_op jit(solution)/shard_map/ppermute | solution.py:581
  147.6 0.2 collective-permute-start.13
  147.8 1.9 %all-to-all-done.2 = bf16[4,400,128]{2,1,0:T(8,128)(2,1)S(1)} async-done(((bf16[4,400,128]{2,1,0:T(8,128)(2,1)}), bf16[4,400,128]{2,1,0:T(8,128)(2,1)S(1)}, u32[]{:S(2)}, u32[]{:S(2)}) %all-to-all-start.2) | async-done | bytes 409632 | tf_op jit(solution)/shard_map/all_to_all | solution.py:595
  149.8 2.2 %collective-permute-done.12 = bf16[400,128]{1,0:T(8,128)(2,1)S(1)} collective-permute-done((bf16[400,128]{1,0:T(8,128)(2,1)S(1)}, bf16[400,128]{1,0:T(8,128)(2,1)S(1)}, u32[]{:S(2)}, u32[]{:S(2)}) %collective-permute-start.12) | collective-permute-done | bytes 102432 | tf_op jit(solution)/shard_map/ppermute | solution.py:581
  152.0 0.2 collective-permute-done.13
  152.3 0.1 fusion.5
  152.4 0.1 fusion.6
  152.5 0.8 pad_maximum_fusion
  153.4 6.0 %all-to-all-start.3 = ((bf16[8,40,320]{2,1,0:T(8,128)(2,1)}), bf16[8,40,320]{2,1,0:T(8,128)(2,1)S(1)}, u32[]{:S(2)}, u32[]{:S(2)}) async-start(bf16[8,40,320]{2,1,0:T(8,128)(2,1)} %pad_maximum_fusion), calls=%async_computation.3 | async-start | bytes 491520 | tf_op jit(solution)/shard_map/all_to_all | solution.py:595
  159.4 9.4 %all-to-all-done.3 = bf16[8,40,320]{2,1,0:T(8,128)(2,1)S(1)} async-done(((bf16[8,40,320]{2,1,0:T(8,128)(2,1)}), bf16[8,40,320]{2,1,0:T(8,128)(2,1)S(1)}, u32[]{:S(2)}, u32[]{:S(2)}) %all-to-all-start.3) | async-done | bytes 204832 | tf_op jit(solution)/shard_map/all_to_all | solution.py:595
  168.9 0.4 collective-permute-start.14
  169.3 2.2 %collective-permute-start.15 = (f32[40,320]{1,0:T(8,128)S(1)}, f32[40,320]{1,0:T(8,128)S(1)}, u32[]{:S(2)}, u32[]{:S(2)}) collective-permute-start(f32[40,320]{1,0:T(8,128)S(1)} %broadcast_multiply_fusion), channel_id=1, source_target_pairs={{0,4},{2,6},{4,0},{6,2},{1,5},{3,7},{5,1},{7,3},{8,12},{10,14},{12... | collective-permute-start | bytes 153608 | tf_op jit(solution)/shard_map/ppermute | solution.py:573
  171.5 0.3 collective-permute-start.16
  171.8 1.4 collective-permute-done.14
  173.3 0.6 collective-permute-done.15
  173.9 0.6 collective-permute-done.16
  174.5 5.2 %collective-permute-start.17 = (f32[4,40,320]{2,1,0:T(8,128)S(1)}, f32[4,40,320]{2,1,0:T(8,128)S(1)}, u32[]{:S(2)}, u32[]{:S(2)}) collective-permute-start(f32[4,40,320]{2,1,0:T(8,128)S(1)} %bitcast_dynamic-update-slice_fusion.2), channel_id=1, source_target_pairs={{0,1},{1,0},{2,3},{3,2},{4,5},{5,4},{6,7},{7,6},{8,9},{9,8},{10,11... | collective-permute-start | bytes 614408 | tf_op jit(solution)/shard_map/ppermute | solution.py:573
  179.8 1.1 collective-permute-done.17
  181.2 0.1 fusion.13
  181.3 0.1 fusion.15
  181.4 0.1 fusion.19
  181.5 0.1 fusion.17
  181.5 0.1 fusion.21
  181.6 0.7 concatenate.44
  182.3 0.8 concatenate.43
  (58 shorter events, 1.0 us)
Async XLA Ops:
  7.2 52.9 %all-gather.3.cloned.1.call-start = ((), (), s32[]{:S(2)}) async-start(), calls=%async_computation.4 | async-start | bytes 2580480 | tf_op jit(solution)/shard_map/all_gather | solution.py:622
  7.2 6.7 %collective-permute-start = (bf16[40,640]{1,0:T(8,128)(2,1)}, bf16[40,640]{1,0:T(8,128)(2,1)S(1)}, u32[]{:S(2)}, u32[]{:S(2)}) collective-permute-start(bf16[40,640]{1,0:T(8,128)(2,1)} %param.17), channel_id=1, source_target_pairs={{0,64},{64,128},{128,192},{192,0},{1,65},{65,129},{129,193},{193,1... | collective-permute-start | bytes 153608 | tf_op jit(solution)/shard_map/ppermute | solution.py:573
  9.4 4.9 %collective-permute-start.1 = (bf16[40,640]{1,0:T(8,128)(2,1)}, bf16[40,640]{1,0:T(8,128)(2,1)S(1)}, u32[]{:S(2)}, u32[]{:S(2)}) collective-permute-start(bf16[40,640]{1,0:T(8,128)(2,1)} %param.17), channel_id=1, source_target_pairs={{0,128},{64,192},{128,0},{192,64},{1,129},{65,193},{129,1},{193,65... | collective-permute-start | bytes 153608 | tf_op jit(solution)/shard_map/ppermute | solution.py:573
  12.0 3.5 %collective-permute-start.2 = (bf16[40,640]{1,0:T(8,128)(2,1)}, bf16[40,640]{1,0:T(8,128)(2,1)S(1)}, u32[]{:S(2)}, u32[]{:S(2)}) collective-permute-start(bf16[40,640]{1,0:T(8,128)(2,1)} %param.17), channel_id=1, source_target_pairs={{0,192},{64,0},{128,64},{192,128},{1,193},{65,1},{129,65},{193,129... | collective-permute-start | bytes 153608 | tf_op jit(solution)/shard_map/ppermute | solution.py:573
  16.5 0.7 copy-start.3
  21.7 6.4 %copy-start.4 = (f32[1280]{0:T(1024)S(1)}, f32[1280]{0:T(1024)}, u32[]{:S(2)}) copy-start(f32[1280]{0:T(1024)} %param.14) | copy-start | bytes 15364
  21.7 7.0 %copy-start.5 = (f32[1280]{0:T(1024)S(1)}, f32[1280]{0:T(1024)}, u32[]{:S(2)}) copy-start(f32[1280]{0:T(1024)} %param.15) | copy-start | bytes 15364
  21.7 38.3 %all-to-all-start = ((bf16[8,128,1280]{2,1,0:T(8,128)(2,1)}), bf16[8,128,1280]{2,1,0:T(8,128)(2,1)S(1)}, u32[]{:S(2)}, u32[]{:S(2)}) async-start(bf16[8,128,1280]{2,1,0:T(8,128)(2,1)} %bitcast.78), calls=%async_computation | async-start | bytes 5242880 | tf_op jit(solution)/shard_map/all_to_all | solution.py:595
  28.1 80.8 %all-gather.5.cloned.1.call-start = ((), (), s32[]{:S(2)}) async-start(), calls=%async_computation.5 | async-start | bytes 3276800 | tf_op jit(solution)/shard_map/all_gather | solution.py:629
  35.1 33.6 %collective-permute-start.3 = (bf16[1280,768]{1,0:T(8,128)(2,1)}, bf16[1280,768]{1,0:T(8,128)(2,1)}, u32[]{:S(2)}, u32[]{:S(2)}) collective-permute-start(bf16[1280,768]{1,0:T(8,128)(2,1)} %norm.1.normed), channel_id=1, source_target_pairs={{0,1},{1,0},{2,3},{3,2},{4,5},{5,4},{6,7},{7,6},{8,9},{9,8},{10,11... | collective-permute-start | bytes 5898248 | tf_op jit(solution)/shard_map/ppermute | solution.py:564
  60.0 2.5 %copy-start = (bf16[8,128,1280]{2,1,0:T(8,128)(2,1)}, bf16[8,128,1280]{2,1,0:T(8,128)(2,1)S(1)}, u32[]{:S(2)}) copy-start(bf16[8,128,1280]{2,1,0:T(8,128)(2,1)S(1)} %all-to-all-done) | copy-start | bytes 7864324
  68.7 19.4 %copy-start.6 = (bf16[1280,768]{1,0:T(8,128)(2,1)S(1)}, bf16[1280,768]{1,0:T(8,128)(2,1)}, u32[]{:S(2)}) copy-start(bf16[1280,768]{1,0:T(8,128)(2,1)} %get-tuple-element.45.incoming) | copy-start | bytes 5898244
  81.7 8.7 %collective-permute-start.5 = (bf16[768,1280]{1,0:T(8,128)(2,1)}, bf16[768,1280]{1,0:T(8,128)(2,1)S(1)}, u32[]{:S(2)}, u32[]{:S(2)}) collective-permute-start(bf16[768,1280]{1,0:T(8,128)(2,1)} %get-tuple-element.50.zero.d_query.d_value), channel_id=1, source_target_pairs={{1,0},{3,2},{5,4},{7,6},{9,8},{11,10},{13,12},{15,14},{17,16},{19,... | collective-permute-start | bytes 5898248 | tf_op jit(solution)/shard_map/ppermute | solution.py:644
  86.8 6.2 %collective-permute-start.6 = (bf16[768,1280]{1,0:T(8,128)(2,1)}, bf16[768,1280]{1,0:T(8,128)(2,1)}, u32[]{:S(2)}, u32[]{:S(2)}) collective-permute-start(bf16[768,1280]{1,0:T(8,128)(2,1)} %get-tuple-element.51.one.d_key), channel_id=1, source_target_pairs={{0,1},{2,3},{4,5},{6,7},{8,9},{10,11},{12,13},{14,15},{16,17},{18,... | collective-permute-start | bytes 5898248 | tf_op jit(solution)/shard_map/ppermute | solution.py:645
  88.1 7.5 %collective-permute-start.4 = (bf16[1280,768]{1,0:T(8,128)(2,1)S(1)}, bf16[1280,768]{1,0:T(8,128)(2,1)}, u32[]{:S(2)}, u32[]{:S(2)}) collective-permute-start(bf16[1280,768]{1,0:T(8,128)(2,1)S(1)} %copy-done.6), channel_id=1, source_target_pairs={{0,1},{2,3},{4,5},{6,7},{8,9},{10,11},{12,13},{14,15},{16,17},{18,... | collective-permute-start | bytes 5898248 | tf_op jit(solution)/shard_map/ppermute | solution.py:632
  90.4 5.1 %copy-start.7 = (bf16[768,1280]{1,0:T(8,128)(2,1)}, bf16[768,1280]{1,0:T(8,128)(2,1)S(1)}, u32[]{:S(2)}) copy-start(bf16[768,1280]{1,0:T(8,128)(2,1)S(1)} %collective-permute-done.5.mate_zero) | copy-start | bytes 5898244
  108.8 4.1 %copy-start.1 = (bf16[4,4,400,128]{3,2,1,0:T(8,128)(2,1)S(1)}, bf16[4,4,400,128]{3,2,1,0:T(8,128)(2,1)}, u32[]{:S(2)}) copy-start(bf16[4,4,400,128]{3,2,1,0:T(8,128)(2,1)} %get-tuple-element.55) | copy-start | bytes 4915204
  108.8 12.2 %collective-permute-start.10 = (bf16[1280,1024]{1,0:T(8,128)(2,1)}, bf16[1280,1024]{1,0:T(8,128)(2,1)}, u32[]{:S(2)}, u32[]{:S(2)}) collective-permute-start(bf16[1280,1024]{1,0:T(8,128)(2,1)} %all-gather.5.cloned.1.call-done.own_w), channel_id=1, source_target_pairs={{0,1},{1,0},{2,3},{3,2},{4,5},{5,4},{6,7},{7,6},{8,9},{9,8},{10,11... | collective-permute-start | bytes 7864328 | tf_op jit(solution)/shard_map/ppermute | solution.py:564
  108.9 29.2 %all-to-all-start.1 = ((bf16[4,4,400,128]{3,2,1,0:T(8,128)(2,1)}), bf16[4,4,400,128]{3,2,1,0:T(8,128)(2,1)S(1)}, u32[]{:S(2)}, u32[]{:S(2)}) async-start(bf16[4,4,400,128]{3,2,1,0:T(8,128)(2,1)} %get-tuple-element.54), calls=%async_computation.1 | async-start | bytes 3276800 | tf_op jit(solution)/shard_map/all_to_all | solution.py:595
  114.1 18.3 %collective-permute-start.7 = (bf16[4,400,128]{2,1,0:T(8,128)(2,1)}, bf16[4,400,128]{2,1,0:T(8,128)(2,1)S(1)}, u32[]{:S(2)}, u32[]{:S(2)}) collective-permute-start(bf16[4,400,128]{2,1,0:T(8,128)(2,1)} %get-tuple-element.73), channel_id=1, source_target_pairs={{0,2},{2,4},{4,6},{6,0},{1,3},{3,5},{5,7},{7,1},{8,10},{10,12},{12... | collective-permute-start | bytes 1228808 | tf_op jit(solution)/shard_map/ppermute | solution.py:581
  117.6 20.5 %collective-permute-start.8 = (bf16[4,400,128]{2,1,0:T(8,128)(2,1)}, bf16[4,400,128]{2,1,0:T(8,128)(2,1)S(1)}, u32[]{:S(2)}, u32[]{:S(2)}) collective-permute-start(bf16[4,400,128]{2,1,0:T(8,128)(2,1)} %get-tuple-element.72), channel_id=1, source_target_pairs={{0,4},{2,6},{4,0},{6,2},{1,5},{3,7},{5,1},{7,3},{8,12},{10,14},{12... | collective-permute-start | bytes 1228808 | tf_op jit(solution)/shard_map/ppermute | solution.py:581
  119.9 18.2 %collective-permute-start.9 = (bf16[4,400,128]{2,1,0:T(8,128)(2,1)}, bf16[4,400,128]{2,1,0:T(8,128)(2,1)S(1)}, u32[]{:S(2)}, u32[]{:S(2)}) collective-permute-start(bf16[4,400,128]{2,1,0:T(8,128)(2,1)} %get-tuple-element.71), channel_id=1, source_target_pairs={{0,6},{2,0},{4,2},{6,4},{1,7},{3,1},{5,3},{7,5},{8,14},{10,8},{12,... | collective-permute-start | bytes 1228808 | tf_op jit(solution)/shard_map/ppermute | solution.py:581
  121.0 17.1 %copy-start.2 = (bf16[4,400,128]{2,1,0:T(8,128)(2,1)S(1)}, bf16[4,400,128]{2,1,0:T(8,128)(2,1)}, u32[]{:S(2)}) copy-start(bf16[4,400,128]{2,1,0:T(8,128)(2,1)} %get-tuple-element.60) | copy-start | bytes 1228804
  139.5 10.2 %all-to-all-start.2 = ((bf16[4,400,128]{2,1,0:T(8,128)(2,1)}), bf16[4,400,128]{2,1,0:T(8,128)(2,1)S(1)}, u32[]{:S(2)}, u32[]{:S(2)}) async-start(bf16[4,400,128]{2,1,0:T(8,128)(2,1)} %add_convert_fusion), calls=%async_computation.2 | async-start | bytes 819200 | tf_op jit(solution)/shard_map/all_to_all | solution.py:595
  143.6 6.2 %collective-permute-start.11 = (bf16[400,128]{1,0:T(8,128)(2,1)S(1)}, bf16[400,128]{1,0:T(8,128)(2,1)S(1)}, u32[]{:S(2)}, u32[]{:S(2)}) collective-permute-start(bf16[400,128]{1,0:T(8,128)(2,1)S(1)} %get-tuple-element.85), channel_id=1, source_target_pairs={{0,2},{2,4},{4,6},{6,0},{1,3},{3,5},{5,7},{7,1},{8,10},{10,12},{12... | collective-permute-start | bytes 307208 | tf_op jit(solution)/shard_map/ppermute | solution.py:581
  144.7 7.3 %collective-permute-start.12 = (bf16[400,128]{1,0:T(8,128)(2,1)S(1)}, bf16[400,128]{1,0:T(8,128)(2,1)S(1)}, u32[]{:S(2)}, u32[]{:S(2)}) collective-permute-start(bf16[400,128]{1,0:T(8,128)(2,1)S(1)} %get-tuple-element.84), channel_id=1, source_target_pairs={{0,4},{2,6},{4,0},{6,2},{1,5},{3,7},{5,1},{7,3},{8,12},{10,14},{12... | collective-permute-start | bytes 307208 | tf_op jit(solution)/shard_map/ppermute | solution.py:581
  147.6 4.6 %collective-permute-start.13 = (bf16[400,128]{1,0:T(8,128)(2,1)S(1)}, bf16[400,128]{1,0:T(8,128)(2,1)S(1)}, u32[]{:S(2)}, u32[]{:S(2)}) collective-permute-start(bf16[400,128]{1,0:T(8,128)(2,1)S(1)} %get-tuple-element.83), channel_id=1, source_target_pairs={{0,6},{2,0},{4,2},{6,4},{1,7},{3,1},{5,3},{7,5},{8,14},{10,8},{12,... | collective-permute-start | bytes 307208 | tf_op jit(solution)/shard_map/ppermute | solution.py:581
  153.4 15.5 %all-to-all-start.3 = ((bf16[8,40,320]{2,1,0:T(8,128)(2,1)}), bf16[8,40,320]{2,1,0:T(8,128)(2,1)S(1)}, u32[]{:S(2)}, u32[]{:S(2)}) async-start(bf16[8,40,320]{2,1,0:T(8,128)(2,1)} %pad_maximum_fusion), calls=%async_computation.3 | async-start | bytes 491520 | tf_op jit(solution)/shard_map/all_to_all | solution.py:595
  168.9 4.4 %collective-permute-start.14 = (f32[40,320]{1,0:T(8,128)S(1)}, f32[40,320]{1,0:T(8,128)S(1)}, u32[]{:S(2)}, u32[]{:S(2)}) collective-permute-start(f32[40,320]{1,0:T(8,128)S(1)} %broadcast_multiply_fusion), channel_id=1, source_target_pairs={{0,2},{2,4},{4,6},{6,0},{1,3},{3,5},{5,7},{7,1},{8,10},{10,12},{12... | collective-permute-start | bytes 153608 | tf_op jit(solution)/shard_map/ppermute | solution.py:573
  169.3 4.6 %collective-permute-start.15 = (f32[40,320]{1,0:T(8,128)S(1)}, f32[40,320]{1,0:T(8,128)S(1)}, u32[]{:S(2)}, u32[]{:S(2)}) collective-permute-start(f32[40,320]{1,0:T(8,128)S(1)} %broadcast_multiply_fusion), channel_id=1, source_target_pairs={{0,4},{2,6},{4,0},{6,2},{1,5},{3,7},{5,1},{7,3},{8,12},{10,14},{12... | collective-permute-start | bytes 153608 | tf_op jit(solution)/shard_map/ppermute | solution.py:573
  171.5 3.1 %collective-permute-start.16 = (f32[40,320]{1,0:T(8,128)S(1)}, f32[40,320]{1,0:T(8,128)S(1)}, u32[]{:S(2)}, u32[]{:S(2)}) collective-permute-start(f32[40,320]{1,0:T(8,128)S(1)} %broadcast_multiply_fusion), channel_id=1, source_target_pairs={{0,6},{2,0},{4,2},{6,4},{1,7},{3,1},{5,3},{7,5},{8,14},{10,8},{12,... | collective-permute-start | bytes 153608 | tf_op jit(solution)/shard_map/ppermute | solution.py:573
  174.5 6.4 %collective-permute-start.17 = (f32[4,40,320]{2,1,0:T(8,128)S(1)}, f32[4,40,320]{2,1,0:T(8,128)S(1)}, u32[]{:S(2)}, u32[]{:S(2)}) collective-permute-start(f32[4,40,320]{2,1,0:T(8,128)S(1)} %bitcast_dynamic-update-slice_fusion.2), channel_id=1, source_target_pairs={{0,1},{1,0},{2,3},{3,2},{4,5},{5,4},{6,7},{7,6},{8,9},{9,8},{10,11... | collective-permute-start | bytes 614408 | tf_op jit(solution)/shard_map/ppermute | solution.py:573
Sparse Core Ops, SparseCore 0:
  17.3 42.3 all-gather.2
  62.6 38.5 all-gather.4

commit v4 on v3

--- a/solution.py
+++ b/solution.py
@@ -15,6 +15,7 @@
 HW = HEADS * HEAD_DIM
 SCALE = 1.0 / math.sqrt(HEAD_DIM)
 BLOCKS = 4
+QKV_PART = 1024
 AXES = {"y": 4, "z": 8, "x": 4, "core": 2}
 VMEM_LIMIT = 60 * 1024 * 1024
 
@@ -275,14 +276,16 @@
     )(table, qkv)
 
 
-def incoming_kernel(table, arrived, spread, incoming, d_attn, incoming_t, landing, w, sems, *, tiles):
+def incoming_kernel(
+    table, arrived, spread, qkv_in, incoming, d_attn, incoming_t, qkv_out, landing, w, sems, *, tiles
+):
     t = pl.program_id(0)
     places = AXES["y"]
     piece = spread.shape[0]
 
     def w_copy(y):
         return pltpu.make_async_copy(
-            spread.at[:, pl.ds(y * HW, HW)], w.at[pl.ds(y * piece, piece)], sems.at[tiles + y]
+            spread.at[:, pl.ds(QKV_PART + y * HW, HW)], w.at[pl.ds(y * piece, piece)], sems.at[tiles + y]
         )
 
     def row_copy(j, source):
@@ -315,6 +318,7 @@
 
     @pl.when(t == 0)
     def _():
+        qkv_out[...] = qkv_in[...]
         for y in range(places):
             w_copy(y).wait()
 
@@ -323,6 +327,7 @@
 
 def place_incoming(table, arrived, spread, rows):
     width = arrived.shape[1]
+    qkv_part = pl.BlockSpec((spread.shape[0], QKV_PART), lambda i, t: (0, 0))
     return pl.pallas_call(
         functools.partial(incoming_kernel, tiles=rows // TILE),
         grid_spec=pltpu.PrefetchScalarGridSpec(
@@ -331,11 +336,13 @@
             in_specs=[
                 pl.BlockSpec(memory_space=pl.ANY),
                 pl.BlockSpec(memory_space=pl.ANY),
+                qkv_part,
             ],
             out_specs=(
                 pl.BlockSpec((WINDOW, width), lambda i, t: (i, 0)),
                 pl.BlockSpec((WINDOW, HW), lambda i, t: (i, 0)),
                 pl.BlockSpec((width, WINDOW), lambda i, t: (0, i)),
+                qkv_part,
             ),
             scratch_shapes=[
                 pltpu.VMEM((rows, width), bf16),
@@ -347,11 +354,12 @@
             jax.ShapeDtypeStruct((rows, width), bf16),
             jax.ShapeDtypeStruct((rows, HW), bf16),
             jax.ShapeDtypeStruct((width, rows), bf16),
+            jax.ShapeDtypeStruct((spread.shape[0], QKV_PART), bf16),
         ),
         compiler_params=params(),
         cost_estimate=cost(2 * rows * width * HW, 10 * rows * width),
         name="incoming",
-    )(table, arrived, spread)
+    )(table, arrived, spread, spread)
 
 
 def add_lanes(tiles, low, part):
@@ -361,14 +369,13 @@
         tiles[at] = piece if tiles[at] is None else tiles[at] + piece
 
 
-def backward_kernel(
-    table, qkv, d_attn, attended, attended_t, weights, value_query, attended_key
-):
+def backward_kernel(table, qkv, d_attn, attended, attended_t, weights, own, send):
     b = pl.program_id(0)
-
-    @pl.when(b < table[META])
-    def _():
-        rows = pl.ds(pl.multiple_of(table[START + b] * TILE, TILE), WINDOW)
+    rows = pl.ds(pl.multiple_of(table[START + b] * TILE, TILE), WINDOW)
+    joined = table[JOINED + b] == 1
+    first = table[META + 1] == 0
+
+    def grads(whole_window):
         grad_t = jnp.transpose(d_attn[rows, :])
         keys_t = jnp.transpose(qkv[rows, HW : 2 * HW])
         query_grads = []
@@ -382,15 +389,42 @@
             row_delta = jnp.sum(
                 grad_t[mine].astype(f32) * attended_t[0, mine].astype(f32), axis=0, keepdims=True
             )
-            dscore = (weights[0, h].astype(f32) * ((prob_grad - row_delta) * SCALE)).astype(bf16)
+
+            def score_grad(keys, queries):
+                change = (prob_grad[keys, queries] - row_delta[:, queries]) * SCALE
+                return (weights[0, h, keys, queries].astype(f32) * change).astype(bf16)
+
+            if whole_window:
+                dscore = score_grad(slice(0, WINDOW), slice(0, WINDOW))
+            else:
+                nothing = jnp.zeros((TILE, TILE), bf16)
+                top = score_grad(slice(0, TILE), slice(0, TILE))
+                bottom = score_grad(slice(TILE, WINDOW), slice(TILE, WINDOW))
+                dscore = jnp.concatenate(
+                    [
+                        jnp.concatenate([top, nothing], axis=1),
+                        jnp.concatenate([nothing, bottom], axis=1),
+                    ],
+                    axis=0,
+                )
             query_grads.append(matmul(keys_t[mine], dscore).astype(bf16))
             add_lanes(key_tiles, low, matmul(dscore, qkv[rows, low:high] * mask))
             add_lanes(value_tiles, low, matmul(weights[0, h], d_attn[rows, low:high] * mask))
-        value_query[rows, HW:] = jnp.transpose(jnp.concatenate(query_grads, axis=0))
+
+        def store(lanes, on_zero, on_one):
+            own[rows, lanes] = jnp.where(first, on_zero, on_one)
+            send[rows, lanes] = jnp.where(first, on_one, on_zero)
+
+        d_query = jnp.transpose(jnp.concatenate(query_grads, axis=0))
         for j in range(HW // 128):
-            value_query[rows, j * 128 : (j + 1) * 128] = value_tiles[j].astype(bf16)
-            attended_key[rows, HW + j * 128 : HW + (j + 1) * 128] = key_tiles[j].astype(bf16)
-        attended_key[rows, :HW] = attended[rows, :]
+            lanes = slice(j * 128, (j + 1) * 128)
+            store(lanes, value_tiles[j].astype(bf16), attended[rows, lanes])
+            store(
+                slice(HW + j * 128, HW + (j + 1) * 128), d_query[:, lanes], key_tiles[j].astype(bf16)
+            )
+
+    pl.when((b < table[META]) & joined)(lambda: grads(True))
+    pl.when((b < table[META]) & jnp.logical_not(joined))(lambda: grads(False))
 
 
 def backward(table, qkv, d_attn, attended, attended_t, weights):
@@ -417,9 +451,11 @@
     )(table, qkv, d_attn, attended, attended_t, weights)
 
 
-def norm_back_kernel(table, x, incoming, gain, d_query, d_key, d_value, own_w, mate_w, out):
-    def halves(low, high):
-        grads = jnp.concatenate([d_query[...], d_key[...], d_value[...]], axis=1)
+def norm_back_kernel(table, x, incoming, gain, own, send, own_w, mate_w, out):
+    def halves(value_query, attended_key, low, high):
+        grads = jnp.concatenate(
+            [value_query[:, HW:], attended_key[:, HW:], value_query[:, :HW]], axis=1
+        )
         contract = (((1,), (1,)), ((), ()))
         return lax.dot_general(
             grads[:, :1024], low[...], contract, preferred_element_type=f32
@@ -445,14 +481,14 @@
 
     @pl.when(first)
     def _():
-        finish(halves(own_w, mate_w))
+        finish(halves(own, send, own_w, mate_w))
 
     @pl.when(jnp.logical_not(first))
     def _():
-        finish(halves(mate_w, own_w))
-
-
-def norm_back(table, x, incoming, gain, value_query, attended_key, own_w, mate_w):
+        finish(halves(send, own, mate_w, own_w))
+
+
+def norm_back(table, x, incoming, gain, own, send, own_w, mate_w):
     rows, width = x.shape
     wide = pl.BlockSpec((WINDOW, width), lambda i, t: (i, 0))
     weights = pl.BlockSpec((width, 1024), lambda i, t: (0, 0))
@@ -465,9 +501,8 @@
                 wide,
                 wide,
                 pl.BlockSpec((1, width), lambda i, t: (0, 0)),
-                pl.BlockSpec((WINDOW, HW), lambda i, t: (i, 1)),
-                pl.BlockSpec((WINDOW, HW), lambda i, t: (i, 1)),
-                pl.BlockSpec((WINDOW, HW), lambda i, t: (i, 0)),
+                pl.BlockSpec((WINDOW, 2 * HW), lambda i, t: (i, 0)),
+                pl.BlockSpec((WINDOW, 2 * HW), lambda i, t: (i, 0)),
                 weights,
                 weights,
             ],
@@ -477,7 +512,7 @@
         compiler_params=params(),
         cost_estimate=cost(2 * rows * width * 3 * HW, 20 * 10**6),
         name="norm_back",
-    )(table, x, incoming, gain.reshape(1, width), value_query, attended_key, value_query, own_w, mate_w)
+    )(table, x, incoming, gain.reshape(1, width), own, send, own_w, mate_w)
 
 
 def packed_columns(total, store):
@@ -494,63 +529,46 @@
         store(x, jnp.concatenate([total[:, x * 128 : (x + 1) * 128], packed], axis=0).astype(bf16))
 
 
-def weight_kernel(
-    table, normed, mate_normed, incoming, mate_incoming, zero, one, mate_zero, mate_one, by_y, by_x, right, sems
-):
+def weight_kernel(table, normed, mate_normed, incoming, mate_incoming, own, mate, by_y, by_x):
     first = table[META + 1] == 0
-    depth = zero.shape[0]
-
-    def copy(side, source):
-        return pltpu.make_async_copy(source, right.at[pl.ds(side * depth, depth)], sems.at[side])
-
-    @pl.when(pl.program_id(0) == 0)
-    def _():
-        for side, (on_zero, on_one) in enumerate(((zero, one), (mate_zero, mate_one))):
-            pl.when(first)(copy(side, on_zero).start)
-            pl.when(jnp.logical_not(first))(copy(side, on_one).start)
-        for side in range(2):
-            copy(side, zero).wait()
-
-    normed_both = jnp.concatenate([normed[...], mate_normed[...]], axis=1)
-    incoming_both = jnp.concatenate([incoming[...], mate_incoming[...]], axis=1)
-    left = jnp.where(first, normed_both, incoming_both)
-    to_y, to_x = matmul(left, right[:, :HW]), matmul(normed_both, right[:, HW:])
-    piece = to_y.shape[0] // 2
-    for i in range(2):
-
-        def store_y(x, value):
-            by_y[i, x] = value
-
-        def store_x(x, value):
-            by_x[lax.rem(x - table[META + 3] + 4, 4), i] = value
-
-        packed_columns(to_y[i * piece : (i + 1) * piece], store_y)
-        packed_columns(to_x[i * piece : (i + 1) * piece], store_x)
-
-
-def weight_parts(table, normed, mate_normed, incoming, mate_incoming, rights):
+    left = jnp.where(first, normed[...], incoming[...])
+    mate_left = jnp.where(first, mate_normed[...], mate_incoming[...])
+    to_x = matmul(normed[...], own[:, HW:]) + matmul(mate_normed[...], mate[:, HW:])
+    to_y = matmul(left, own[:, :HW]) + matmul(mate_left, mate[:, :HW])
+
+    def store_x(x, value):
+        by_x[lax.rem(x - table[META + 3] + 4, 4)] = value
+
+    def store_y(x, value):
+        by_y[x] = value
+
+    packed_columns(to_x, store_x)
+    packed_columns(to_y, store_y)
+
+
+def weight_parts(table, normed, mate_normed, incoming, mate_incoming, own, mate):
     width, rows = normed.shape
     piece = width // 4
     packed = piece * 5 // 4
-    left = pl.BlockSpec((2 * piece, rows), lambda i, t: (i, 0))
-    on_one = pl.BlockSpec((2 * piece, rows), lambda i, t: (i * t[META + 1], 0))
+    left = pl.BlockSpec((piece, rows), lambda i, t: (i, 0))
+    on_one = pl.BlockSpec((piece, rows), lambda i, t: (i * t[META + 1], 0))
+    right = pl.BlockSpec((rows, 2 * HW), lambda i, t: (0, 0))
     return pl.pallas_call(
         weight_kernel,
         grid_spec=pltpu.PrefetchScalarGridSpec(
             num_scalar_prefetch=1,
-            grid=(2,),
-            in_specs=[left, left, on_one, on_one] + [pl.BlockSpec(memory_space=pl.ANY)] * 4,
+            grid=(4,),
+            in_specs=[left, left, on_one, on_one, right, right],
             out_specs=(
-                pl.BlockSpec((2, 4, packed, 128), lambda i, t: (i, 0, 0, 0)),
-                pl.BlockSpec((4, 2, packed, 128), lambda i, t: (0, i, 0, 0)),
+                pl.BlockSpec((None, 4, packed, 128), lambda i, t: (i, 0, 0, 0)),
+                pl.BlockSpec((4, None, packed, 128), lambda i, t: (0, i, 0, 0)),
             ),
-            scratch_shapes=[pltpu.VMEM((2 * rows, 2 * HW), bf16), pltpu.SemaphoreType.DMA((2,))],
         ),
         out_shape=(jax.ShapeDtypeStruct((4, 4, packed, 128), bf16),) * 2,
         compiler_params=params(),
         cost_estimate=cost(8 * width * rows * HW, 8 * width * rows + 4 * width * HW),
         name="weight_parts",
-    )(table, normed, mate_normed, incoming, mate_incoming, *rights)
+    )(table, normed, mate_normed, incoming, mate_incoming, own, mate)
 
 
 def unpacked(part):
@@ -575,10 +593,10 @@
     return out
 
 
-def sent_by_distance(value, axis):
+def sent_by_distance(parts, axis):
     count = AXES[axis]
-    return [value[0]] + [
-        lax.ppermute(value[k], axis, [(i, (i + k) % count) for i in range(count)])
+    return [parts[0]] + [
+        lax.ppermute(parts[k], axis, [(i, (i + k) % count) for i in range(count)])
         for k in range(1, count)
     ]
 
@@ -615,7 +633,7 @@
 
     spread = gathered(w_out, "y")
     spread = jnp.concatenate(
-        [spread[y] for y in range(4)] + [lax.dynamic_slice_in_dim(w_qkv, 896 * core, 1024, axis=1)], axis=1
+        [lax.dynamic_slice_in_dim(w_qkv, 896 * core, QKV_PART, axis=1)] + [spread[y] for y in range(4)], axis=1
     )
     table, outgoing = route(image_patches, image_owner, place, grad_rows, own_tiles, sections)
     arrived = exchanged(outgoing, section)
@@ -626,28 +644,17 @@
     spread, arrived, attended_t, normed_t = lax.optimization_barrier(
         (spread, arrived, attended_t, normed_t)
     )
-    qkv_w = lax.all_gather(spread[:, 4 * HW :], "y", axis=0, tiled=True)
-
-    incoming, d_attn, incoming_t = place_incoming(table, arrived, spread, own_tiles * TILE)
-    mate_incoming_t = lax.ppermute(incoming_t, "core", [(0, 1)])
+    incoming, d_attn, incoming_t, qkv_w = place_incoming(table, arrived, spread, own_tiles * TILE)
+    qkv_w = lax.all_gather(qkv_w, "y", axis=0, tiled=True)
+    mate_incoming_t = to_mate(incoming_t)
     d_attn, mate_normed_t = lax.optimization_barrier((d_attn, mate_normed_t))
-    value_query, attended_key = backward(table, saved_qkv, d_attn, attended, attended_t, weights)
+    own, send = backward(table, saved_qkv, d_attn, attended, attended_t, weights)
     first, second = weight_parts(
-        table,
-        normed_t,
-        mate_normed_t,
-        incoming_t,
-        mate_incoming_t,
-        (
-            value_query,
-            attended_key,
-            lax.ppermute(value_query, "core", [(1, 0)]),
-            lax.ppermute(attended_key, "core", [(0, 1)]),
-        ),
+        table, normed_t, mate_normed_t, incoming_t, mate_incoming_t, own, to_mate(send)
     )
-    first, second, qkv_w = lax.optimization_barrier((first, second, qkv_w))
+    second, qkv_w = lax.optimization_barrier(([second[k] for k in range(AXES["x"])], qkv_w))
     layer_grad = norm_back(
-        table, layer_input, incoming, norm_gain, value_query, attended_key, qkv_w, to_mate(qkv_w)
+        table, layer_input, incoming, norm_gain, own, send, qkv_w, to_mate(qkv_w)
     )
     first = exchanged(first, "y")
     second = sent_by_distance(second, "x")

time: 191 us -> 188 us (0.984)
  starting transfers between devices: 53.4 us -> 45.5 us
  Pallas kernels: 65.6 us -> 70 us
    ppermute x9 -> x6, waiting for transfers between devices: 14.1 us -> 3.02 us  [sent_by_distance(): lax.ppermute(parts[k], axis, [(i, (i + k) % count) for i in range(count)])]
    ppermute x9 -> x6, starting transfers between devices: 18.9 us -> 9.35 us  [sent_by_distance(): lax.ppermute(parts[k], axis, [(i, (i + k) % count) for i in range(count)])]
    ppermute x2 -> x4, waiting for transfers between devices: 0.01 us -> 6.27 us  [to_mate(): return lax.ppermute(value, 'core', [(0, 1), (1, 0)])]
    unnamed x20 -> x18, local copies, waits for them, and re-layouts: 0.79 us -> 4.45 us
    all_to_all x4, waiting for transfers between devices: 24.1 us -> 26.8 us  [exchanged(): return lax.all_to_all(value, axes, split_axis=0, concat_axis=0, tiled=True)]
    slice x1 -> x0, local copies, waits for them, and re-layouts: 2.44 us -> none  [on_device(): qkv_w = lax.all_gather(spread[:, 4 * HW:], 'y', axis=0, tiled=True)]
    pallas_call x1, Pallas kernels: 12.1 us -> 14.5 us  [forward(): pl.pallas_call(forward_kernel, grid_spec=pltpu.PrefetchScalarGridSpec(num...]
    pallas_call x1, Pallas kernels: 13 us -> 15.3 us  [backward(): pl.pallas_call(backward_kernel, grid_spec=pltpu.PrefetchScalarGridSpec(nu...]
  transfers between devices with their start and end apart: 24 -> 23, of which waited for: 15 -> 15; matrix products, arithmetic and copies ran while one was open for 3% -> 3% of each run, Pallas kernels for 35% -> 37%
where the time goes in v4:
time: 188 us; the launch traced here: 187 us
  Pallas kernels  70 us (37%)
  starting transfers between devices  45.5 us (24%)
  waiting for transfers between devices  42.4 us (23%)
  between operations  14.3 us (8%)
  local copies, waits for them, and re-layouts  10.6 us (6%)
  other arithmetic  4.41 us (2%)
    all_to_all x4, waiting for transfers between devices, exchanged(): return lax.all_to_all(value, axes, split_axis=0, concat_axis=0, tiled=True)  26.8 us
    all_to_all x4, starting transfers between devices, exchanged(): return lax.all_to_all(value, axes, split_axis=0, concat_axis=0, tiled=True)  20.3 us
    pallas_call x1, Pallas kernels, backward(): pl.pallas_call(backward_kernel, grid_spec=pltpu.PrefetchScalarGridSpec(nu...  15.3 us
    ppermute x7, starting transfers between devices, gathered(): lax.ppermute(value, axis, [(i, (i + k) % count) for i in range(count)])  14.6 us
    pallas_call x1, Pallas kernels, forward(): pl.pallas_call(forward_kernel, grid_spec=pltpu.PrefetchScalarGridSpec(num...  14.5 us
    pallas_call x1, Pallas kernels, weight_parts(): pl.pallas_call(weight_kernel, grid_spec=pltpu.PrefetchScalarGridSpec(num_...  11.9 us
    pallas_call x1, Pallas kernels, norm_back(): pl.pallas_call(norm_back_kernel, grid_spec=pltpu.PrefetchScalarGridSpec(n...  11.3 us
    ppermute x6, starting transfers between devices, sent_by_distance(): lax.ppermute(parts[k], axis, [(i, (i + k) % count) for i in range(count)])  9.35 us
  transfers between devices with their start and end apart: 23, of which 15 were waited for; matrix products, arithmetic and copies ran while one was open for 3% of the time, Pallas kernels for 37%

profile of v4, /device:TPU:1, one launch (start us, length us, event | category | flops | bytes accessed | tf_op | source)
XLA Modules:
  0.0 187.2 jit_solution(120743420792140782)
XLA Ops:
  7.2 2.2 %collective-permute-start = (bf16[40,640]{1,0:T(8,128)(2,1)}, bf16[40,640]{1,0:T(8,128)(2,1)S(1)}, u32[]{:S(2)}, u32[]{:S(2)}) collective-permute-start(bf16[40,640]{1,0:T(8,128)(2,1)} %param.17), channel_id=1, source_target_pairs={{0,64},{64,128},{128,192},{192,0},{1,65},{65,129},{129,193},{193,1... | collective-permute-start | bytes 153608 | tf_op jit(solution)/shard_map/ppermute | solution.py:591
  9.4 2.6 %collective-permute-start.1 = (bf16[40,640]{1,0:T(8,128)(2,1)}, bf16[40,640]{1,0:T(8,128)(2,1)S(1)}, u32[]{:S(2)}, u32[]{:S(2)}) collective-permute-start(bf16[40,640]{1,0:T(8,128)(2,1)} %param.17), channel_id=1, source_target_pairs={{0,128},{64,192},{128,0},{192,64},{1,129},{65,193},{129,1},{193,65... | collective-permute-start | bytes 153608 | tf_op jit(solution)/shard_map/ppermute | solution.py:591
  12.0 1.1 collective-permute-start.2
  13.1 0.8 bitcast_dynamic-update-slice_fusion.9
  14.0 0.9 dynamic-slice_dynamic-update-slice_fusion
  14.9 0.6 collective-permute-done.2
  15.6 0.7 copy-done.1
  16.3 0.6 pad_add_fusion.place
  16.9 3.8 %route.1 = (s32[32]{0:T(128)}, bf16[1024,1280]{1,0:T(8,128)(2,1)}) custom-call(s32[1,32]{1,0:T(1,128)} %patches.1, s32[1,32]{1,0:T(1,128)} %owners.1, s32[3]{0:T(128)} %pad_add_fusion.place, bf16[512,1280]{1,0:T(8,128)(2,1)} %rows.1), custom_call_target="tpu_custom_call" | custom-call | bytes 2621440 | tf_op jit(solution)/shard_map/route/pallas_call | solution.py:136
  20.8 6.4 %all-to-all-start = ((bf16[8,128,1280]{2,1,0:T(8,128)(2,1)}), bf16[8,128,1280]{2,1,0:T(8,128)(2,1)S(1)}, u32[]{:S(2)}, u32[]{:S(2)}) async-start(bf16[8,128,1280]{2,1,0:T(8,128)(2,1)} %bitcast.78), calls=%async_computation | async-start | bytes 5242880 | tf_op jit(solution)/shard_map/all_to_all | solution.py:613
  27.2 0.6 reshape.33.gain
  27.8 0.6 reshape.34.bias
  28.4 5.8 %norm.1.normed = bf16[1280,768]{1,0:T(8,128)(2,1)} custom-call(bf16[768,1280]{1,0:T(8,128)(2,1)} %x.3, f32[1,1280]{1,0:T(1,128)} %reshape.33.gain, f32[1,1280]{1,0:T(1,128)} %reshape.34.bias), custom_call_target="tpu_custom_call" | custom-call | flops 1000000 | bytes 100000 | tf_op jit(solution)/shard_map/norm/pallas_call | solution.py:167
  34.3 14.5 %attend.1 = (bf16[768,640]{1,0:T(8,128)(2,1)}, bf16[4,640,256]{2,1,0:T(8,128)(2,1)}, bf16[4,8,256,256]{3,2,1,0:T(8,128)(2,1)}) custom-call(s32[32]{0:T(128)} %get-tuple-element.40.table, bf16[768,1920]{1,0:T(8,128)(2,1)} %qkv.3), custom_call_target="tpu_custom_call" | custom-call | flops 1000000 | bytes 100000 | tf_op jit(solution)/shard_map/attend/pallas_call | solution.py:256
  48.8 10.4 %all-to-all-done = bf16[8,128,1280]{2,1,0:T(8,128)(2,1)S(1)} async-done(((bf16[8,128,1280]{2,1,0:T(8,128)(2,1)}), bf16[8,128,1280]{2,1,0:T(8,128)(2,1)S(1)}, u32[]{:S(2)}, u32[]{:S(2)}) %all-to-all-start) | async-done | bytes 2621472 | tf_op jit(solution)/shard_map/all_to_all | solution.py:613
  59.1 1.5 copy-done
  60.7 7.3 %incoming.1 = (bf16[768,1280]{1,0:T(8,128)(2,1)}, bf16[768,640]{1,0:T(8,128)(2,1)}, bf16[1280,768]{1,0:T(8,128)(2,1)}, bf16[320,1024]{1,0:T(8,128)(2,1)}) custom-call(s32[32]{0:T(128)} %get-tuple-element.40.table, bf16[1024,1280]{1,0:T(8,128)(2,1)} %bitcast.77, bf16[320,3584]{1,0:T(8,128)(2,1)} %all-gather.3.cloned.1.call-done.spread.qkv_in, ...), custom_call_target="tpu_custom_call" | custom-call | flops 1258291200 | bytes 9830400 | tf_op jit(solution)/shard_map/incoming/pallas_call | solution.py:331
  68.0 15.3 %attend_back.1 = (bf16[768,1280]{1,0:T(8,128)(2,1)}, bf16[768,1280]{1,0:T(8,128)(2,1)}) custom-call(s32[32]{0:T(128)} %get-tuple-element.40.table, bf16[768,1920]{1,0:T(8,128)(2,1)} %qkv.3, bf16[768,640]{1,0:T(8,128)(2,1)} %get-tuple-element.49.d_attn, bf16[768,640]{1,0:T(8,128)(2,1)} %get-tuple-element.50.attended, ...), custom_call_target="tpu_custom_call" | custom-call | flops 12000000000 | bytes 20000000 | tf_op jit(solution)/shard_map/attend_back/pallas_call | solution.py:433
  83.4 0.5 collective-permute-start.4
  83.9 5.5 %collective-permute-done.5.mate = bf16[768,1280]{1,0:T(8,128)(2,1)S(1)} collective-permute-done((bf16[768,1280]{1,0:T(8,128)(2,1)}, bf16[768,1280]{1,0:T(8,128)(2,1)S(1)}, u32[]{:S(2)}, u32[]{:S(2)}) %collective-permute-start.5) | collective-permute-done | bytes 1966112 | tf_op jit(solution)/shard_map/ppermute | solution.py:582
  89.4 0.7 collective-permute-done.4.mate_incoming
  90.1 1.3 copy-done.6
  91.4 11.9 %weight_parts.1 = (bf16[4,4,400,128]{3,2,1,0:T(8,128)(2,1)}, bf16[4,4,400,128]{3,2,1,0:T(8,128)(2,1)}) custom-call(s32[32]{0:T(128)} %get-tuple-element.40.table, bf16[1280,768]{1,0:T(8,128)(2,1)} %norm.1.normed, bf16[1280,768]{1,0:T(8,128)(2,1)} %collective-permute-done.3.mate_normed, bf16[1280,768]{1,0:T(8,128)(2,1)} %get-tuple-element.48.incoming, ...), custom_call_target="tpu_custom_call" | custom-call | flops 5033164800 | bytes 11141120 | tf_op jit(solution)/shard_map/weight_parts/pallas_call | solution.py:556
  103.3 1.5 slice_bitcast_fusion
  104.8 1.8 all-gather.5.cloned.1.call-done.own_w
  106.6 0.7 collective-permute-start.9
  107.3 3.6 %all-to-all-start.1 = ((bf16[4,4,400,128]{3,2,1,0:T(8,128)(2,1)}), bf16[4,4,400,128]{3,2,1,0:T(8,128)(2,1)S(1)}, u32[]{:S(2)}, u32[]{:S(2)}) async-start(bf16[4,4,400,128]{3,2,1,0:T(8,128)(2,1)} %get-tuple-element.55), calls=%async_computation.1 | async-start | bytes 3276800 | tf_op jit(solution)/shard_map/all_to_all | solution.py:613
  110.8 1.5 collective-permute-start.6
  112.3 2.4 %collective-permute-start.7 = (bf16[4,400,128]{2,1,0:T(8,128)(2,1)S(1)}, bf16[4,400,128]{2,1,0:T(8,128)(2,1)}, u32[]{:S(2)}, u32[]{:S(2)}) collective-permute-start(bf16[4,400,128]{2,1,0:T(8,128)(2,1)S(1)} %get-tuple-element.60), channel_id=1, source_target_pairs={{0,4},{2,6},{4,0},{6,2},{1,5},{3,7},{5,1},{7,3},{8,12},{10,14},{12... | collective-permute-start | bytes 1228808 | tf_op jit(solution)/shard_map/ppermute | solution.py:599
  114.7 1.2 collective-permute-start.8
  115.9 11.3 %norm_back.1 = bf16[768,1280]{1,0:T(8,128)(2,1)} custom-call(s32[32]{0:T(128)} %get-tuple-element.40.table, bf16[768,1280]{1,0:T(8,128)(2,1)} %x.3, bf16[768,1280]{1,0:T(8,128)(2,1)} %get-tuple-element.62.incoming, f32[1,1280]{1,0:T(1,128)} %reshape.33.gain, bf16[768,1280]{1,0:T(8,128)(2,1)} %get-tuple-element.53.own, ...), custom_call_target="tpu_custom_call" | custom-call | flops 3774873600 | bytes 20000000 | tf_op jit(solution)/shard_map/norm_back/pallas_call | solution.py:495
  127.2 5.3 %all-to-all-done.1 = bf16[4,4,400,128]{3,2,1,0:T(8,128)(2,1)S(1)} async-done(((bf16[4,4,400,128]{3,2,1,0:T(8,128)(2,1)}), bf16[4,4,400,128]{3,2,1,0:T(8,128)(2,1)S(1)}, u32[]{:S(2)}, u32[]{:S(2)}) %all-to-all-start.1) | async-done | bytes 1638432 | tf_op jit(solution)/shard_map/all_to_all | solution.py:613
  132.5 0.7 collective-permute-done.7
  133.2 2.2 %add_convert_fusion = bf16[4,400,128]{2,1,0:T(8,128)(2,1)} fusion(bf16[4,400,128]{2,1,0:T(8,128)(2,1)} %collective-permute-done.8, bf16[4,400,128]{2,1,0:T(8,128)(2,1)} %collective-permute-done.7, bf16[4,400,128]{2,1,0:T(8,128)(2,1)} %collective-permute-done.6, bf16[4,400,128]{2,1,0:T(8,128)(2,1)S(1)} %get-tuple-element.66), kind=kLoop, calls=%fused_computation.3 | loop fusion | flops 1638400 | bytes 2048000 | tf_op jit(solution)/shard_map/convert_element_type | solution.py:662
  135.5 0.4 reduce_sum.30
  135.9 3.6 %all-to-all-start.2 = ((bf16[4,400,128]{2,1,0:T(8,128)(2,1)}), bf16[4,400,128]{2,1,0:T(8,128)(2,1)S(1)}, u32[]{:S(2)}, u32[]{:S(2)}) async-start(bf16[4,400,128]{2,1,0:T(8,128)(2,1)} %add_convert_fusion), calls=%async_computation.2 | async-start | bytes 819200 | tf_op jit(solution)/shard_map/all_to_all | solution.py:613
  139.5 0.2 fusion
  139.7 1.1 collective-permute-start.10
  140.8 2.8 %collective-permute-start.11 = (bf16[400,128]{1,0:T(8,128)(2,1)S(1)}, bf16[400,128]{1,0:T(8,128)(2,1)S(1)}, u32[]{:S(2)}, u32[]{:S(2)}) collective-permute-start(bf16[400,128]{1,0:T(8,128)(2,1)S(1)} %get-tuple-element.90), channel_id=1, source_target_pairs={{0,4},{2,6},{4,0},{6,2},{1,5},{3,7},{5,1},{7,3},{8,12},{10,14},{12... | collective-permute-start | bytes 307208 | tf_op jit(solution)/shard_map/ppermute | solution.py:599
  143.6 0.4 collective-permute-start.12
  143.9 2.1 %all-to-all-done.2 = bf16[4,400,128]{2,1,0:T(8,128)(2,1)S(1)} async-done(((bf16[4,400,128]{2,1,0:T(8,128)(2,1)}), bf16[4,400,128]{2,1,0:T(8,128)(2,1)S(1)}, u32[]{:S(2)}, u32[]{:S(2)}) %all-to-all-start.2) | async-done | bytes 409632 | tf_op jit(solution)/shard_map/all_to_all | solution.py:613
  146.1 1.8 collective-permute-done.11
  147.9 0.5 collective-permute-done.12
  148.5 0.1 fusion.5
  148.6 0.1 fusion.6
  148.7 0.8 pad_maximum_fusion
  149.6 6.7 %all-to-all-start.3 = ((bf16[8,40,320]{2,1,0:T(8,128)(2,1)}), bf16[8,40,320]{2,1,0:T(8,128)(2,1)S(1)}, u32[]{:S(2)}, u32[]{:S(2)}) async-start(bf16[8,40,320]{2,1,0:T(8,128)(2,1)} %pad_maximum_fusion), calls=%async_computation.3 | async-start | bytes 491520 | tf_op jit(solution)/shard_map/all_to_all | solution.py:613
  156.3 9.0 %all-to-all-done.3 = bf16[8,40,320]{2,1,0:T(8,128)(2,1)S(1)} async-done(((bf16[8,40,320]{2,1,0:T(8,128)(2,1)}), bf16[8,40,320]{2,1,0:T(8,128)(2,1)S(1)}, u32[]{:S(2)}, u32[]{:S(2)}) %all-to-all-start.3) | async-done | bytes 204832 | tf_op jit(solution)/shard_map/all_to_all | solution.py:613
  165.4 0.1 collective-permute-start.13
  165.5 2.7 %collective-permute-start.14 = (f32[40,320]{1,0:T(8,128)S(1)}, f32[40,320]{1,0:T(8,128)S(1)}, u32[]{:S(2)}, u32[]{:S(2)}) collective-permute-start(f32[40,320]{1,0:T(8,128)S(1)} %broadcast_multiply_fusion), channel_id=1, source_target_pairs={{0,4},{2,6},{4,0},{6,2},{1,5},{3,7},{5,1},{7,3},{8,12},{10,14},{12... | collective-permute-start | bytes 153608 | tf_op jit(solution)/shard_map/ppermute | solution.py:591
  168.2 0.2 collective-permute-start.15
  168.5 1.3 collective-permute-done.13
  169.8 0.7 collective-permute-done.14
  170.5 0.8 collective-permute-done.15
  171.3 5.6 %collective-permute-start.16 = (f32[4,40,320]{2,1,0:T(8,128)S(1)}, f32[4,40,320]{2,1,0:T(8,128)S(1)}, u32[]{:S(2)}, u32[]{:S(2)}) collective-permute-start(f32[4,40,320]{2,1,0:T(8,128)S(1)} %bitcast_dynamic-update-slice_fusion.2), channel_id=1, source_target_pairs={{0,1},{1,0},{2,3},{3,2},{4,5},{5,4},{6,7},{7,6},{8,9},{9,8},{10,11... | collective-permute-start | bytes 614408 | tf_op jit(solution)/shard_map/ppermute | solution.py:591
  177.0 1.1 collective-permute-done.16
  178.1 0.1 fusion.7
  178.4 0.1 fusion.13
  178.4 0.1 fusion.15
  178.5 0.1 fusion.19
  178.6 0.1 fusion.17
  178.7 0.1 fusion.21
  178.8 0.7 concatenate.44
  179.5 0.8 concatenate.43
  (53 shorter events, 0.9 us)
Async XLA Ops:
  7.2 52.0 %all-gather.3.cloned.1.call-start = ((), (), s32[]{:S(2)}) async-start(), calls=%async_computation.4 | async-start | bytes 2580480 | tf_op jit(solution)/shard_map/all_gather | solution.py:640
  7.2 7.6 %collective-permute-start = (bf16[40,640]{1,0:T(8,128)(2,1)}, bf16[40,640]{1,0:T(8,128)(2,1)S(1)}, u32[]{:S(2)}, u32[]{:S(2)}) collective-permute-start(bf16[40,640]{1,0:T(8,128)(2,1)} %param.17), channel_id=1, source_target_pairs={{0,64},{64,128},{128,192},{192,0},{1,65},{65,129},{129,193},{193,1... | collective-permute-start | bytes 153608 | tf_op jit(solution)/shard_map/ppermute | solution.py:591
  9.4 5.5 %collective-permute-start.1 = (bf16[40,640]{1,0:T(8,128)(2,1)}, bf16[40,640]{1,0:T(8,128)(2,1)S(1)}, u32[]{:S(2)}, u32[]{:S(2)}) collective-permute-start(bf16[40,640]{1,0:T(8,128)(2,1)} %param.17), channel_id=1, source_target_pairs={{0,128},{64,192},{128,0},{192,64},{1,129},{65,193},{129,1},{193,65... | collective-permute-start | bytes 153608 | tf_op jit(solution)/shard_map/ppermute | solution.py:591
  12.0 3.5 %collective-permute-start.2 = (bf16[40,640]{1,0:T(8,128)(2,1)}, bf16[40,640]{1,0:T(8,128)(2,1)S(1)}, u32[]{:S(2)}, u32[]{:S(2)}) collective-permute-start(bf16[40,640]{1,0:T(8,128)(2,1)} %param.17), channel_id=1, source_target_pairs={{0,192},{64,0},{128,64},{192,128},{1,193},{65,1},{129,65},{193,129... | collective-permute-start | bytes 153608 | tf_op jit(solution)/shard_map/ppermute | solution.py:591
  15.6 0.7 copy-start.1
  20.8 6.4 %copy-start.2 = (f32[1280]{0:T(1024)S(1)}, f32[1280]{0:T(1024)}, u32[]{:S(2)}) copy-start(f32[1280]{0:T(1024)} %param.14) | copy-start | bytes 15364
  20.8 7.0 %copy-start.3 = (f32[1280]{0:T(1024)S(1)}, f32[1280]{0:T(1024)}, u32[]{:S(2)}) copy-start(f32[1280]{0:T(1024)} %param.15) | copy-start | bytes 15364
  20.8 38.4 %all-to-all-start = ((bf16[8,128,1280]{2,1,0:T(8,128)(2,1)}), bf16[8,128,1280]{2,1,0:T(8,128)(2,1)S(1)}, u32[]{:S(2)}, u32[]{:S(2)}) async-start(bf16[8,128,1280]{2,1,0:T(8,128)(2,1)} %bitcast.78), calls=%async_computation | async-start | bytes 5242880 | tf_op jit(solution)/shard_map/all_to_all | solution.py:613
  27.2 79.4 %all-gather.5.cloned.1.call-start = ((), (), s32[]{:S(2)}) async-start(), calls=%async_computation.5 | async-start | bytes 3276800 | tf_op jit(solution)/shard_map/all_gather | solution.py:648
  34.2 33.8 %collective-permute-start.3 = (bf16[1280,768]{1,0:T(8,128)(2,1)}, bf16[1280,768]{1,0:T(8,128)(2,1)}, u32[]{:S(2)}, u32[]{:S(2)}) collective-permute-start(bf16[1280,768]{1,0:T(8,128)(2,1)} %norm.1.normed), channel_id=1, source_target_pairs={{0,1},{1,0},{2,3},{3,2},{4,5},{5,4},{6,7},{7,6},{8,9},{9,8},{10,11... | collective-permute-start | bytes 5898248 | tf_op jit(solution)/shard_map/ppermute | solution.py:582
  59.1 1.5 copy-start
  68.0 15.4 %copy-start.4 = (bf16[1280,768]{1,0:T(8,128)(2,1)S(1)}, bf16[1280,768]{1,0:T(8,128)(2,1)}, u32[]{:S(2)}) copy-start(bf16[1280,768]{1,0:T(8,128)(2,1)} %get-tuple-element.48.incoming) | copy-start | bytes 5898244
  83.4 6.0 %collective-permute-start.5 = (bf16[768,1280]{1,0:T(8,128)(2,1)}, bf16[768,1280]{1,0:T(8,128)(2,1)S(1)}, u32[]{:S(2)}, u32[]{:S(2)}) collective-permute-start(bf16[768,1280]{1,0:T(8,128)(2,1)} %get-tuple-element.54.send), channel_id=1, source_target_pairs={{0,1},{1,0},{2,3},{3,2},{4,5},{5,4},{6,7},{7,6},{8,9},{9,8},{10,11... | collective-permute-start | bytes 5898248 | tf_op jit(solution)/shard_map/ppermute | solution.py:582
  83.4 6.8 %collective-permute-start.4 = (bf16[1280,768]{1,0:T(8,128)(2,1)S(1)}, bf16[1280,768]{1,0:T(8,128)(2,1)S(1)}, u32[]{:S(2)}, u32[]{:S(2)}) collective-permute-start(bf16[1280,768]{1,0:T(8,128)(2,1)S(1)} %copy-done.4), channel_id=1, source_target_pairs={{0,1},{1,0},{2,3},{3,2},{4,5},{5,4},{6,7},{7,6},{8,9},{9,8},{10,11... | collective-permute-start | bytes 5898248 | tf_op jit(solution)/shard_map/ppermute | solution.py:582
  89.4 2.0 %copy-start.5 = (bf16[768,1280]{1,0:T(8,128)(2,1)}, bf16[768,1280]{1,0:T(8,128)(2,1)S(1)}, u32[]{:S(2)}) copy-start(bf16[768,1280]{1,0:T(8,128)(2,1)S(1)} %collective-permute-done.5.mate) | copy-start | bytes 5898244
  90.1 1.3 copy-start.6
  106.6 9.3 %collective-permute-start.9 = (bf16[1280,1024]{1,0:T(8,128)(2,1)}, bf16[1280,1024]{1,0:T(8,128)(2,1)}, u32[]{:S(2)}, u32[]{:S(2)}) collective-permute-start(bf16[1280,1024]{1,0:T(8,128)(2,1)} %all-gather.5.cloned.1.call-done.own_w), channel_id=1, source_target_pairs={{0,1},{1,0},{2,3},{3,2},{4,5},{5,4},{6,7},{7,6},{8,9},{9,8},{10,11... | collective-permute-start | bytes 7864328 | tf_op jit(solution)/shard_map/ppermute | solution.py:582
  107.3 25.2 %all-to-all-start.1 = ((bf16[4,4,400,128]{3,2,1,0:T(8,128)(2,1)}), bf16[4,4,400,128]{3,2,1,0:T(8,128)(2,1)S(1)}, u32[]{:S(2)}, u32[]{:S(2)}) async-start(bf16[4,4,400,128]{3,2,1,0:T(8,128)(2,1)} %get-tuple-element.55), calls=%async_computation.1 | async-start | bytes 3276800 | tf_op jit(solution)/shard_map/all_to_all | solution.py:613
  110.8 21.7 %collective-permute-start.6 = (bf16[4,400,128]{2,1,0:T(8,128)(2,1)S(1)}, bf16[4,400,128]{2,1,0:T(8,128)(2,1)}, u32[]{:S(2)}, u32[]{:S(2)}) collective-permute-start(bf16[4,400,128]{2,1,0:T(8,128)(2,1)S(1)} %get-tuple-element.59), channel_id=1, source_target_pairs={{0,2},{2,4},{4,6},{6,0},{1,3},{3,5},{5,7},{7,1},{8,10},{10,12},{12... | collective-permute-start | bytes 1228808 | tf_op jit(solution)/shard_map/ppermute | solution.py:599
  112.3 20.9 %collective-permute-start.7 = (bf16[4,400,128]{2,1,0:T(8,128)(2,1)S(1)}, bf16[4,400,128]{2,1,0:T(8,128)(2,1)}, u32[]{:S(2)}, u32[]{:S(2)}) collective-permute-start(bf16[4,400,128]{2,1,0:T(8,128)(2,1)S(1)} %get-tuple-element.60), channel_id=1, source_target_pairs={{0,4},{2,6},{4,0},{6,2},{1,5},{3,7},{5,1},{7,3},{8,12},{10,14},{12... | collective-permute-start | bytes 1228808 | tf_op jit(solution)/shard_map/ppermute | solution.py:599
  114.7 18.5 %collective-permute-start.8 = (bf16[4,400,128]{2,1,0:T(8,128)(2,1)S(1)}, bf16[4,400,128]{2,1,0:T(8,128)(2,1)}, u32[]{:S(2)}, u32[]{:S(2)}) collective-permute-start(bf16[4,400,128]{2,1,0:T(8,128)(2,1)S(1)} %get-tuple-element.61), channel_id=1, source_target_pairs={{0,6},{2,0},{4,2},{6,4},{1,7},{3,1},{5,3},{7,5},{8,14},{10,8},{12,... | collective-permute-start | bytes 1228808 | tf_op jit(solution)/shard_map/ppermute | solution.py:599
  135.9 10.2 %all-to-all-start.2 = ((bf16[4,400,128]{2,1,0:T(8,128)(2,1)}), bf16[4,400,128]{2,1,0:T(8,128)(2,1)S(1)}, u32[]{:S(2)}, u32[]{:S(2)}) async-start(bf16[4,400,128]{2,1,0:T(8,128)(2,1)} %add_convert_fusion), calls=%async_computation.2 | async-start | bytes 819200 | tf_op jit(solution)/shard_map/all_to_all | solution.py:613
  139.7 6.5 %collective-permute-start.10 = (bf16[400,128]{1,0:T(8,128)(2,1)S(1)}, bf16[400,128]{1,0:T(8,128)(2,1)S(1)}, u32[]{:S(2)}, u32[]{:S(2)}) collective-permute-start(bf16[400,128]{1,0:T(8,128)(2,1)S(1)} %get-tuple-element.91), channel_id=1, source_target_pairs={{0,2},{2,4},{4,6},{6,0},{1,3},{3,5},{5,7},{7,1},{8,10},{10,12},{12... | collective-permute-start | bytes 307208 | tf_op jit(solution)/shard_map/ppermute | solution.py:599
  140.8 7.1 %collective-permute-start.11 = (bf16[400,128]{1,0:T(8,128)(2,1)S(1)}, bf16[400,128]{1,0:T(8,128)(2,1)S(1)}, u32[]{:S(2)}, u32[]{:S(2)}) collective-permute-start(bf16[400,128]{1,0:T(8,128)(2,1)S(1)} %get-tuple-element.90), channel_id=1, source_target_pairs={{0,4},{2,6},{4,0},{6,2},{1,5},{3,7},{5,1},{7,3},{8,12},{10,14},{12... | collective-permute-start | bytes 307208 | tf_op jit(solution)/shard_map/ppermute | solution.py:599
  143.6 4.8 %collective-permute-start.12 = (bf16[400,128]{1,0:T(8,128)(2,1)S(1)}, bf16[400,128]{1,0:T(8,128)(2,1)S(1)}, u32[]{:S(2)}, u32[]{:S(2)}) collective-permute-start(bf16[400,128]{1,0:T(8,128)(2,1)S(1)} %get-tuple-element.89), channel_id=1, source_target_pairs={{0,6},{2,0},{4,2},{6,4},{1,7},{3,1},{5,3},{7,5},{8,14},{10,8},{12,... | collective-permute-start | bytes 307208 | tf_op jit(solution)/shard_map/ppermute | solution.py:599
  149.6 15.8 %all-to-all-start.3 = ((bf16[8,40,320]{2,1,0:T(8,128)(2,1)}), bf16[8,40,320]{2,1,0:T(8,128)(2,1)S(1)}, u32[]{:S(2)}, u32[]{:S(2)}) async-start(bf16[8,40,320]{2,1,0:T(8,128)(2,1)} %pad_maximum_fusion), calls=%async_computation.3 | async-start | bytes 491520 | tf_op jit(solution)/shard_map/all_to_all | solution.py:613
  165.4 4.4 %collective-permute-start.13 = (f32[40,320]{1,0:T(8,128)S(1)}, f32[40,320]{1,0:T(8,128)S(1)}, u32[]{:S(2)}, u32[]{:S(2)}) collective-permute-start(f32[40,320]{1,0:T(8,128)S(1)} %broadcast_multiply_fusion), channel_id=1, source_target_pairs={{0,2},{2,4},{4,6},{6,0},{1,3},{3,5},{5,7},{7,1},{8,10},{10,12},{12... | collective-permute-start | bytes 153608 | tf_op jit(solution)/shard_map/ppermute | solution.py:591
  165.5 4.9 %collective-permute-start.14 = (f32[40,320]{1,0:T(8,128)S(1)}, f32[40,320]{1,0:T(8,128)S(1)}, u32[]{:S(2)}, u32[]{:S(2)}) collective-permute-start(f32[40,320]{1,0:T(8,128)S(1)} %broadcast_multiply_fusion), channel_id=1, source_target_pairs={{0,4},{2,6},{4,0},{6,2},{1,5},{3,7},{5,1},{7,3},{8,12},{10,14},{12... | collective-permute-start | bytes 153608 | tf_op jit(solution)/shard_map/ppermute | solution.py:591
  168.2 3.1 %collective-permute-start.15 = (f32[40,320]{1,0:T(8,128)S(1)}, f32[40,320]{1,0:T(8,128)S(1)}, u32[]{:S(2)}, u32[]{:S(2)}) collective-permute-start(f32[40,320]{1,0:T(8,128)S(1)} %broadcast_multiply_fusion), channel_id=1, source_target_pairs={{0,6},{2,0},{4,2},{6,4},{1,7},{3,1},{5,3},{7,5},{8,14},{10,8},{12,... | collective-permute-start | bytes 153608 | tf_op jit(solution)/shard_map/ppermute | solution.py:591
  171.3 6.8 %collective-permute-start.16 = (f32[4,40,320]{2,1,0:T(8,128)S(1)}, f32[4,40,320]{2,1,0:T(8,128)S(1)}, u32[]{:S(2)}, u32[]{:S(2)}) collective-permute-start(f32[4,40,320]{2,1,0:T(8,128)S(1)} %bitcast_dynamic-update-slice_fusion.2), channel_id=1, source_target_pairs={{0,1},{1,0},{2,3},{3,2},{4,5},{5,4},{6,7},{7,6},{8,9},{9,8},{10,11... | collective-permute-start | bytes 614408 | tf_op jit(solution)/shard_map/ppermute | solution.py:591
Sparse Core Ops, SparseCore 0:
  16.4 42.2 all-gather.2
  68.1 38.4 all-gather.4

commit v5 on v4

--- a/solution.py
+++ b/solution.py
@@ -90,6 +90,7 @@
         table[META + b] = 0
     table[META + 1] = place[1]
     table[META + 3] = place[2]
+    table[META + 4] = place[3]
 
     def step(at):
         here = segment[at]
@@ -283,9 +284,10 @@
     places = AXES["y"]
     piece = spread.shape[0]
 
-    def w_copy(y):
+    def w_copy(k):
+        row = pl.multiple_of(lax.rem(table[META + 4] - k + places, places) * piece, piece)
         return pltpu.make_async_copy(
-            spread.at[:, pl.ds(QKV_PART + y * HW, HW)], w.at[pl.ds(y * piece, piece)], sems.at[tiles + y]
+            spread.at[:, pl.ds(QKV_PART + k * HW, HW)], w.at[pl.ds(row, piece)], sems.at[tiles + k]
         )
 
     def row_copy(j, source):
@@ -629,11 +631,12 @@
     section = ("x", "core")
     sections = AXES["x"] * AXES["core"]
     core = lax.axis_index("core")
-    place = jnp.stack([lax.axis_index(section), core, lax.axis_index("x")]).astype(jnp.int32)
-
-    spread = gathered(w_out, "y")
+    place = jnp.stack([lax.axis_index(section), core, lax.axis_index("x"), lax.axis_index("y")]).astype(jnp.int32)
+
     spread = jnp.concatenate(
-        [lax.dynamic_slice_in_dim(w_qkv, 896 * core, QKV_PART, axis=1)] + [spread[y] for y in range(4)], axis=1
+        [lax.dynamic_slice_in_dim(w_qkv, 896 * core, QKV_PART, axis=1)]
+        + sent_by_distance([w_out] * AXES["y"], "y"),
+        axis=1,
     )
     table, outgoing = route(image_patches, image_owner, place, grad_rows, own_tiles, sections)
     arrived = exchanged(outgoing, section)

time: 188 us -> 188 us (level)
  Pallas kernels: 70 us -> 64.3 us
  starting transfers between devices: 45.5 us -> 49.5 us
    ppermute x6 -> x9, starting transfers between devices: 9.35 us -> 15.1 us  [sent_by_distance(): lax.ppermute(parts[k], axis, [(i, (i + k) % count) for i in range(count)])]
    ppermute x7 -> x4, starting transfers between devices: 14.6 us -> 8.95 us  [gathered(): lax.ppermute(value, axis, [(i, (i + k) % count) for i in range(count)])]
    ppermute x4, starting transfers between devices: 1.26 us -> 5.2 us  [to_mate(): return lax.ppermute(value, 'core', [(0, 1), (1, 0)])]
    pallas_call x1, Pallas kernels: 14.5 us -> 11.2 us  [forward(): pl.pallas_call(forward_kernel, grid_spec=pltpu.PrefetchScalarGridSpec(num...]
    all_to_all x4, waiting for transfers between devices: 26.8 us -> 29.8 us  [exchanged(): return lax.all_to_all(value, axes, split_axis=0, concat_axis=0, tiled=True)]
    pallas_call x1, Pallas kernels: 15.3 us -> 12.9 us  [backward(): pl.pallas_call(backward_kernel, grid_spec=pltpu.PrefetchScalarGridSpec(nu...]
    ppermute x6 -> x9, waiting for transfers between devices: 3.02 us -> 4.25 us  [sent_by_distance(): lax.ppermute(parts[k], axis, [(i, (i + k) % count) for i in range(count)])]
    ppermute x7 -> x4, waiting for transfers between devices: 4.44 us -> 3.55 us  [gathered(): lax.ppermute(value, axis, [(i, (i + k) % count) for i in range(count)])]
  transfers between devices with their start and end apart: 23 -> 23, of which waited for: 15 -> 14; matrix products, arithmetic and copies ran while one was open for 3% -> 3% of each run, Pallas kernels for 37% -> 34%
where the time goes in v5:
time: 188 us; the launch traced here: 187 us
  Pallas kernels  64.3 us (34%)
  starting transfers between devices  49.5 us (26%)
  waiting for transfers between devices  44.2 us (24%)
  between operations  14.3 us (8%)
  local copies, waits for them, and re-layouts  10.5 us (6%)
  other arithmetic  4.49 us (2%)
    all_to_all x4, waiting for transfers between devices, exchanged(): return lax.all_to_all(value, axes, split_axis=0, concat_axis=0, tiled=True)  29.8 us
    all_to_all x4, starting transfers between devices, exchanged(): return lax.all_to_all(value, axes, split_axis=0, concat_axis=0, tiled=True)  20.2 us
    ppermute x9, starting transfers between devices, sent_by_distance(): lax.ppermute(parts[k], axis, [(i, (i + k) % count) for i in range(count)])  15.1 us
    pallas_call x1, Pallas kernels, backward(): pl.pallas_call(backward_kernel, grid_spec=pltpu.PrefetchScalarGridSpec(nu...  12.9 us
    pallas_call x1, Pallas kernels, weight_parts(): pl.pallas_call(weight_kernel, grid_spec=pltpu.PrefetchScalarGridSpec(num_...  11.9 us
    pallas_call x1, Pallas kernels, norm_back(): pl.pallas_call(norm_back_kernel, grid_spec=pltpu.PrefetchScalarGridSpec(n...  11.3 us
    pallas_call x1, Pallas kernels, forward(): pl.pallas_call(forward_kernel, grid_spec=pltpu.PrefetchScalarGridSpec(num...  11.2 us
    ppermute x4, starting transfers between devices, gathered(): lax.ppermute(value, axis, [(i, (i + k) % count) for i in range(count)])  8.95 us
  transfers between devices with their start and end apart: 23, of which 14 were waited for; matrix products, arithmetic and copies ran while one was open for 3% of the time, Pallas kernels for 34%

profile of v5, /device:TPU:1, one launch (start us, length us, event | category | flops | bytes accessed | tf_op | source)
XLA Modules:
  0.0 187.2 jit_solution(8329160133183066562)
XLA Ops:
  7.2 2.2 %collective-permute-start = (bf16[40,640]{1,0:T(8,128)(2,1)}, bf16[40,640]{1,0:T(8,128)(2,1)S(1)}, u32[]{:S(2)}, u32[]{:S(2)}) collective-permute-start(bf16[40,640]{1,0:T(8,128)(2,1)} %param.17), channel_id=1, source_target_pairs={{0,64},{64,128},{128,192},{192,0},{1,65},{65,129},{129,193},{193,1... | collective-permute-start | bytes 153608 | tf_op jit(solution)/shard_map/ppermute | solution.py:601
  9.4 2.6 %collective-permute-start.1 = (bf16[40,640]{1,0:T(8,128)(2,1)}, bf16[40,640]{1,0:T(8,128)(2,1)S(1)}, u32[]{:S(2)}, u32[]{:S(2)}) collective-permute-start(bf16[40,640]{1,0:T(8,128)(2,1)} %param.17), channel_id=1, source_target_pairs={{0,128},{64,192},{128,0},{192,64},{1,129},{65,193},{129,1},{193,65... | collective-permute-start | bytes 153608 | tf_op jit(solution)/shard_map/ppermute | solution.py:601
  12.0 1.1 collective-permute-start.2
  13.1 0.9 dynamic-slice_dynamic-update-slice_fusion
  14.0 0.8 constant_dynamic-update-slice_fusion.3
  14.9 0.6 collective-permute-done.2
  15.5 0.7 copy-done.1
  16.3 0.7 pad_add_fusion.place
  16.9 3.8 %route.1 = (s32[32]{0:T(128)}, bf16[1024,1280]{1,0:T(8,128)(2,1)}) custom-call(s32[1,32]{1,0:T(1,128)} %patches.1, s32[1,32]{1,0:T(1,128)} %owners.1, s32[4]{0:T(128)} %pad_add_fusion.place, bf16[512,1280]{1,0:T(8,128)(2,1)} %rows.1), custom_call_target="tpu_custom_call" | custom-call | bytes 2621440 | tf_op jit(solution)/shard_map/route/pallas_call | solution.py:137
  20.8 6.4 %all-to-all-start = ((bf16[8,128,1280]{2,1,0:T(8,128)(2,1)}), bf16[8,128,1280]{2,1,0:T(8,128)(2,1)S(1)}, u32[]{:S(2)}, u32[]{:S(2)}) async-start(bf16[8,128,1280]{2,1,0:T(8,128)(2,1)} %bitcast.55), calls=%async_computation | async-start | bytes 5242880 | tf_op jit(solution)/shard_map/all_to_all | solution.py:615
  27.2 0.6 reshape.33.gain
  27.8 0.6 reshape.34.bias
  28.4 5.8 %norm.1.normed = bf16[1280,768]{1,0:T(8,128)(2,1)} custom-call(bf16[768,1280]{1,0:T(8,128)(2,1)} %x.3, f32[1,1280]{1,0:T(1,128)} %reshape.33.gain, f32[1,1280]{1,0:T(1,128)} %reshape.34.bias), custom_call_target="tpu_custom_call" | custom-call | flops 1000000 | bytes 100000 | tf_op jit(solution)/shard_map/norm/pallas_call | solution.py:168
  34.3 11.2 %attend.1 = (bf16[768,640]{1,0:T(8,128)(2,1)}, bf16[4,640,256]{2,1,0:T(8,128)(2,1)}, bf16[4,8,256,256]{3,2,1,0:T(8,128)(2,1)}) custom-call(s32[32]{0:T(128)} %get-tuple-element.40.table, bf16[768,1920]{1,0:T(8,128)(2,1)} %qkv.3), custom_call_target="tpu_custom_call" | custom-call | flops 1000000 | bytes 100000 | tf_op jit(solution)/shard_map/attend/pallas_call | solution.py:257
  45.5 13.6 %all-to-all-done = bf16[8,128,1280]{2,1,0:T(8,128)(2,1)S(1)} async-done(((bf16[8,128,1280]{2,1,0:T(8,128)(2,1)}), bf16[8,128,1280]{2,1,0:T(8,128)(2,1)S(1)}, u32[]{:S(2)}, u32[]{:S(2)}) %all-to-all-start) | async-done | bytes 2621472 | tf_op jit(solution)/shard_map/all_to_all | solution.py:615
  59.1 1.5 copy-done
  60.6 7.3 %incoming.1 = (bf16[768,1280]{1,0:T(8,128)(2,1)}, bf16[768,640]{1,0:T(8,128)(2,1)}, bf16[1280,768]{1,0:T(8,128)(2,1)}, bf16[320,1024]{1,0:T(8,128)(2,1)}) custom-call(s32[32]{0:T(128)} %get-tuple-element.40.table, bf16[1024,1280]{1,0:T(8,128)(2,1)} %bitcast.54, bf16[320,3584]{1,0:T(8,128)(2,1)} %all-gather.3.cloned.1.call-done.spread.qkv_in, ...), custom_call_target="tpu_custom_call" | custom-call | flops 1258291200 | bytes 9830400 | tf_op jit(solution)/shard_map/incoming/pallas_call | solution.py:333
  68.0 12.9 %attend_back.1 = (bf16[768,1280]{1,0:T(8,128)(2,1)}, bf16[768,1280]{1,0:T(8,128)(2,1)}) custom-call(s32[32]{0:T(128)} %get-tuple-element.40.table, bf16[768,1920]{1,0:T(8,128)(2,1)} %qkv.3, bf16[768,640]{1,0:T(8,128)(2,1)} %get-tuple-element.49.d_attn, bf16[768,640]{1,0:T(8,128)(2,1)} %get-tuple-element.50.attended, ...), custom_call_target="tpu_custom_call" | custom-call | flops 12000000000 | bytes 20000000 | tf_op jit(solution)/shard_map/attend_back/pallas_call | solution.py:435
  80.9 4.4 %collective-permute-start.5 = (bf16[768,1280]{1,0:T(8,128)(2,1)}, bf16[768,1280]{1,0:T(8,128)(2,1)S(1)}, u32[]{:S(2)}, u32[]{:S(2)}) collective-permute-start(bf16[768,1280]{1,0:T(8,128)(2,1)} %get-tuple-element.54.send), channel_id=1, source_target_pairs={{0,1},{1,0},{2,3},{3,2},{4,5},{5,4},{6,7},{7,6},{8,9},{9,8},{10,11... | collective-permute-start | bytes 5898248 | tf_op jit(solution)/shard_map/ppermute | solution.py:584
  85.3 0.1 collective-permute-start.4
  85.4 5.6 %collective-permute-done.5.mate = bf16[768,1280]{1,0:T(8,128)(2,1)S(1)} collective-permute-done((bf16[768,1280]{1,0:T(8,128)(2,1)}, bf16[768,1280]{1,0:T(8,128)(2,1)S(1)}, u32[]{:S(2)}, u32[]{:S(2)}) %collective-permute-start.5) | collective-permute-done | bytes 1966112 | tf_op jit(solution)/shard_map/ppermute | solution.py:584
  91.0 0.7 collective-permute-done.4.mate_incoming
  91.7 1.3 copy-done.6
  93.0 11.9 %weight_parts.1 = (bf16[4,4,400,128]{3,2,1,0:T(8,128)(2,1)}, bf16[4,4,400,128]{3,2,1,0:T(8,128)(2,1)}) custom-call(s32[32]{0:T(128)} %get-tuple-element.40.table, bf16[1280,768]{1,0:T(8,128)(2,1)} %norm.1.normed, bf16[1280,768]{1,0:T(8,128)(2,1)} %collective-permute-done.3.mate_normed, bf16[1280,768]{1,0:T(8,128)(2,1)} %get-tuple-element.48.incoming, ...), custom_call_target="tpu_custom_call" | custom-call | flops 5033164800 | bytes 11141120 | tf_op jit(solution)/shard_map/weight_parts/pallas_call | solution.py:558
  104.9 1.5 slice_bitcast_fusion
  106.4 0.2 all-gather.5.cloned.1.call-done.own_w
  106.6 0.7 collective-permute-start.9
  107.3 3.6 %all-to-all-start.1 = ((bf16[4,4,400,128]{3,2,1,0:T(8,128)(2,1)}), bf16[4,4,400,128]{3,2,1,0:T(8,128)(2,1)S(1)}, u32[]{:S(2)}, u32[]{:S(2)}) async-start(bf16[4,4,400,128]{3,2,1,0:T(8,128)(2,1)} %get-tuple-element.55), calls=%async_computation.1 | async-start | bytes 3276800 | tf_op jit(solution)/shard_map/all_to_all | solution.py:615
  110.9 1.5 collective-permute-start.6
  112.4 2.4 %collective-permute-start.7 = (bf16[4,400,128]{2,1,0:T(8,128)(2,1)S(1)}, bf16[4,400,128]{2,1,0:T(8,128)(2,1)}, u32[]{:S(2)}, u32[]{:S(2)}) collective-permute-start(bf16[4,400,128]{2,1,0:T(8,128)(2,1)S(1)} %get-tuple-element.60), channel_id=1, source_target_pairs={{0,4},{2,6},{4,0},{6,2},{1,5},{3,7},{5,1},{7,3},{8,12},{10,14},{12... | collective-permute-start | bytes 1228808 | tf_op jit(solution)/shard_map/ppermute | solution.py:601
  114.8 1.2 collective-permute-start.8
  115.9 11.3 %norm_back.1 = bf16[768,1280]{1,0:T(8,128)(2,1)} custom-call(s32[32]{0:T(128)} %get-tuple-element.40.table, bf16[768,1280]{1,0:T(8,128)(2,1)} %x.3, bf16[768,1280]{1,0:T(8,128)(2,1)} %get-tuple-element.62.incoming, f32[1,1280]{1,0:T(1,128)} %reshape.33.gain, bf16[768,1280]{1,0:T(8,128)(2,1)} %get-tuple-element.53.own, ...), custom_call_target="tpu_custom_call" | custom-call | flops 3774873600 | bytes 20000000 | tf_op jit(solution)/shard_map/norm_back/pallas_call | solution.py:497
  127.2 5.3 %all-to-all-done.1 = bf16[4,4,400,128]{3,2,1,0:T(8,128)(2,1)S(1)} async-done(((bf16[4,4,400,128]{3,2,1,0:T(8,128)(2,1)}), bf16[4,4,400,128]{3,2,1,0:T(8,128)(2,1)S(1)}, u32[]{:S(2)}, u32[]{:S(2)}) %all-to-all-start.1) | async-done | bytes 1638432 | tf_op jit(solution)/shard_map/all_to_all | solution.py:615
  132.5 0.7 collective-permute-done.7
  133.3 2.2 %add_convert_fusion = bf16[4,400,128]{2,1,0:T(8,128)(2,1)} fusion(bf16[4,400,128]{2,1,0:T(8,128)(2,1)} %collective-permute-done.8, bf16[4,400,128]{2,1,0:T(8,128)(2,1)} %collective-permute-done.7, bf16[4,400,128]{2,1,0:T(8,128)(2,1)} %collective-permute-done.6, bf16[4,400,128]{2,1,0:T(8,128)(2,1)S(1)} %get-tuple-element.66), kind=kLoop, calls=%fused_computation.3 | loop fusion | flops 1638400 | bytes 2048000 | tf_op jit(solution)/shard_map/convert_element_type | solution.py:665
  135.5 3.5 %all-to-all-start.2 = ((bf16[4,400,128]{2,1,0:T(8,128)(2,1)}), bf16[4,400,128]{2,1,0:T(8,128)(2,1)S(1)}, u32[]{:S(2)}, u32[]{:S(2)}) async-start(bf16[4,400,128]{2,1,0:T(8,128)(2,1)} %add_convert_fusion), calls=%async_computation.2 | async-start | bytes 819200 | tf_op jit(solution)/shard_map/all_to_all | solution.py:615
  139.0 0.4 reduce_sum.30
  139.4 0.2 fusion
  139.6 1.2 collective-permute-start.10
  140.9 2.8 %collective-permute-start.11 = (bf16[400,128]{1,0:T(8,128)(2,1)S(1)}, bf16[400,128]{1,0:T(8,128)(2,1)S(1)}, u32[]{:S(2)}, u32[]{:S(2)}) collective-permute-start(bf16[400,128]{1,0:T(8,128)(2,1)S(1)} %get-tuple-element.90), channel_id=1, source_target_pairs={{0,4},{2,6},{4,0},{6,2},{1,5},{3,7},{5,1},{7,3},{8,12},{10,14},{12... | collective-permute-start | bytes 307208 | tf_op jit(solution)/shard_map/ppermute | solution.py:601
  143.6 0.1 collective-permute-start.12
  143.7 1.8 all-to-all-done.2
  145.6 2.2 %collective-permute-done.11 = bf16[400,128]{1,0:T(8,128)(2,1)S(1)} collective-permute-done((bf16[400,128]{1,0:T(8,128)(2,1)S(1)}, bf16[400,128]{1,0:T(8,128)(2,1)S(1)}, u32[]{:S(2)}, u32[]{:S(2)}) %collective-permute-start.11) | collective-permute-done | bytes 102432 | tf_op jit(solution)/shard_map/ppermute | solution.py:601
  147.8 0.6 collective-permute-done.12
  148.5 0.1 fusion.1
  148.6 0.1 fusion.2
  148.8 0.8 pad_maximum_fusion
  149.6 6.7 %all-to-all-start.3 = ((bf16[8,40,320]{2,1,0:T(8,128)(2,1)}), bf16[8,40,320]{2,1,0:T(8,128)(2,1)S(1)}, u32[]{:S(2)}, u32[]{:S(2)}) async-start(bf16[8,40,320]{2,1,0:T(8,128)(2,1)} %pad_maximum_fusion), calls=%async_computation.3 | async-start | bytes 491520 | tf_op jit(solution)/shard_map/all_to_all | solution.py:615
  156.3 9.0 %all-to-all-done.3 = bf16[8,40,320]{2,1,0:T(8,128)(2,1)S(1)} async-done(((bf16[8,40,320]{2,1,0:T(8,128)(2,1)}), bf16[8,40,320]{2,1,0:T(8,128)(2,1)S(1)}, u32[]{:S(2)}, u32[]{:S(2)}) %all-to-all-start.3) | async-done | bytes 204832 | tf_op jit(solution)/shard_map/all_to_all | solution.py:615
  165.4 0.1 collective-permute-start.13
  165.6 2.3 %collective-permute-start.14 = (f32[40,320]{1,0:T(8,128)S(1)}, f32[40,320]{1,0:T(8,128)S(1)}, u32[]{:S(2)}, u32[]{:S(2)}) collective-permute-start(f32[40,320]{1,0:T(8,128)S(1)} %broadcast_multiply_fusion), channel_id=1, source_target_pairs={{0,4},{2,6},{4,0},{6,2},{1,5},{3,7},{5,1},{7,3},{8,12},{10,14},{12... | collective-permute-start | bytes 153608 | tf_op jit(solution)/shard_map/ppermute | solution.py:593
  167.8 0.7 collective-permute-start.15
  168.5 1.9 %collective-permute-done.13 = f32[40,320]{1,0:T(8,128)S(1)} collective-permute-done((f32[40,320]{1,0:T(8,128)S(1)}, f32[40,320]{1,0:T(8,128)S(1)}, u32[]{:S(2)}, u32[]{:S(2)}) %collective-permute-start.13) | collective-permute-done | bytes 51232 | tf_op jit(solution)/shard_map/ppermute | solution.py:593
  170.5 0.5 collective-permute-done.15
  171.1 5.9 %collective-permute-start.16 = (f32[4,40,320]{2,1,0:T(8,128)S(1)}, f32[4,40,320]{2,1,0:T(8,128)S(1)}, u32[]{:S(2)}, u32[]{:S(2)}) collective-permute-start(f32[4,40,320]{2,1,0:T(8,128)S(1)} %bitcast_dynamic-update-slice_fusion.2), channel_id=1, source_target_pairs={{0,1},{1,0},{2,3},{3,2},{4,5},{5,4},{6,7},{7,6},{8,9},{9,8},{10,11... | collective-permute-start | bytes 614408 | tf_op jit(solution)/shard_map/ppermute | solution.py:593
  177.0 1.1 collective-permute-done.16
  178.2 0.1 fusion.3
  178.4 0.1 fusion.9
  178.5 0.1 fusion.11
  178.6 0.1 fusion.15
  178.7 0.1 fusion.13
  178.7 0.1 fusion.17
  178.8 0.7 concatenate.44
  179.6 0.8 concatenate.43
  (48 shorter events, 0.8 us)
Async XLA Ops:
  7.2 52.0 %all-gather.3.cloned.1.call-start = ((), (), s32[]{:S(2)}) async-start(), calls=%async_computation.4 | async-start | bytes 2580480 | tf_op jit(solution)/shard_map/all_gather | solution.py:643
  7.2 7.6 %collective-permute-start = (bf16[40,640]{1,0:T(8,128)(2,1)}, bf16[40,640]{1,0:T(8,128)(2,1)S(1)}, u32[]{:S(2)}, u32[]{:S(2)}) collective-permute-start(bf16[40,640]{1,0:T(8,128)(2,1)} %param.17), channel_id=1, source_target_pairs={{0,64},{64,128},{128,192},{192,0},{1,65},{65,129},{129,193},{193,1... | collective-permute-start | bytes 153608 | tf_op jit(solution)/shard_map/ppermute | solution.py:601
  9.4 5.4 %collective-permute-start.1 = (bf16[40,640]{1,0:T(8,128)(2,1)}, bf16[40,640]{1,0:T(8,128)(2,1)S(1)}, u32[]{:S(2)}, u32[]{:S(2)}) collective-permute-start(bf16[40,640]{1,0:T(8,128)(2,1)} %param.17), channel_id=1, source_target_pairs={{0,128},{64,192},{128,0},{192,64},{1,129},{65,193},{129,1},{193,65... | collective-permute-start | bytes 153608 | tf_op jit(solution)/shard_map/ppermute | solution.py:601
  12.0 3.5 %collective-permute-start.2 = (bf16[40,640]{1,0:T(8,128)(2,1)}, bf16[40,640]{1,0:T(8,128)(2,1)S(1)}, u32[]{:S(2)}, u32[]{:S(2)}) collective-permute-start(bf16[40,640]{1,0:T(8,128)(2,1)} %param.17), channel_id=1, source_target_pairs={{0,192},{64,0},{128,64},{192,128},{1,193},{65,1},{129,65},{193,129... | collective-permute-start | bytes 153608 | tf_op jit(solution)/shard_map/ppermute | solution.py:601
  15.5 0.7 copy-start.1
  20.8 6.4 %copy-start.2 = (f32[1280]{0:T(1024)S(1)}, f32[1280]{0:T(1024)}, u32[]{:S(2)}) copy-start(f32[1280]{0:T(1024)} %param.14) | copy-start | bytes 15364
  20.8 7.0 %copy-start.3 = (f32[1280]{0:T(1024)S(1)}, f32[1280]{0:T(1024)}, u32[]{:S(2)}) copy-start(f32[1280]{0:T(1024)} %param.15) | copy-start | bytes 15364
  20.8 38.3 %all-to-all-start = ((bf16[8,128,1280]{2,1,0:T(8,128)(2,1)}), bf16[8,128,1280]{2,1,0:T(8,128)(2,1)S(1)}, u32[]{:S(2)}, u32[]{:S(2)}) async-start(bf16[8,128,1280]{2,1,0:T(8,128)(2,1)} %bitcast.55), calls=%async_computation | async-start | bytes 5242880 | tf_op jit(solution)/shard_map/all_to_all | solution.py:615
  27.2 79.5 %all-gather.5.cloned.1.call-start = ((), (), s32[]{:S(2)}) async-start(), calls=%async_computation.5 | async-start | bytes 3276800 | tf_op jit(solution)/shard_map/all_gather | solution.py:651
  34.2 33.8 %collective-permute-start.3 = (bf16[1280,768]{1,0:T(8,128)(2,1)}, bf16[1280,768]{1,0:T(8,128)(2,1)}, u32[]{:S(2)}, u32[]{:S(2)}) collective-permute-start(bf16[1280,768]{1,0:T(8,128)(2,1)} %norm.1.normed), channel_id=1, source_target_pairs={{0,1},{1,0},{2,3},{3,2},{4,5},{5,4},{6,7},{7,6},{8,9},{9,8},{10,11... | collective-permute-start | bytes 5898248 | tf_op jit(solution)/shard_map/ppermute | solution.py:584
  59.1 1.5 copy-start
  68.0 17.3 %copy-start.4 = (bf16[1280,768]{1,0:T(8,128)(2,1)S(1)}, bf16[1280,768]{1,0:T(8,128)(2,1)}, u32[]{:S(2)}) copy-start(bf16[1280,768]{1,0:T(8,128)(2,1)} %get-tuple-element.48.incoming) | copy-start | bytes 5898244
  80.9 10.0 %collective-permute-start.5 = (bf16[768,1280]{1,0:T(8,128)(2,1)}, bf16[768,1280]{1,0:T(8,128)(2,1)S(1)}, u32[]{:S(2)}, u32[]{:S(2)}) collective-permute-start(bf16[768,1280]{1,0:T(8,128)(2,1)} %get-tuple-element.54.send), channel_id=1, source_target_pairs={{0,1},{1,0},{2,3},{3,2},{4,5},{5,4},{6,7},{7,6},{8,9},{9,8},{10,11... | collective-permute-start | bytes 5898248 | tf_op jit(solution)/shard_map/ppermute | solution.py:584
  85.3 6.4 %collective-permute-start.4 = (bf16[1280,768]{1,0:T(8,128)(2,1)S(1)}, bf16[1280,768]{1,0:T(8,128)(2,1)S(1)}, u32[]{:S(2)}, u32[]{:S(2)}) collective-permute-start(bf16[1280,768]{1,0:T(8,128)(2,1)S(1)} %copy-done.4), channel_id=1, source_target_pairs={{0,1},{1,0},{2,3},{3,2},{4,5},{5,4},{6,7},{7,6},{8,9},{9,8},{10,11... | collective-permute-start | bytes 5898248 | tf_op jit(solution)/shard_map/ppermute | solution.py:584
  91.0 2.0 %copy-start.5 = (bf16[768,1280]{1,0:T(8,128)(2,1)}, bf16[768,1280]{1,0:T(8,128)(2,1)S(1)}, u32[]{:S(2)}) copy-start(bf16[768,1280]{1,0:T(8,128)(2,1)S(1)} %collective-permute-done.5.mate) | copy-start | bytes 5898244
  91.7 1.3 copy-start.6
  106.6 9.3 %collective-permute-start.9 = (bf16[1280,1024]{1,0:T(8,128)(2,1)}, bf16[1280,1024]{1,0:T(8,128)(2,1)}, u32[]{:S(2)}, u32[]{:S(2)}) collective-permute-start(bf16[1280,1024]{1,0:T(8,128)(2,1)} %all-gather.5.cloned.1.call-done.own_w), channel_id=1, source_target_pairs={{0,1},{1,0},{2,3},{3,2},{4,5},{5,4},{6,7},{7,6},{8,9},{9,8},{10,11... | collective-permute-start | bytes 7864328 | tf_op jit(solution)/shard_map/ppermute | solution.py:584
  107.3 25.2 %all-to-all-start.1 = ((bf16[4,4,400,128]{3,2,1,0:T(8,128)(2,1)}), bf16[4,4,400,128]{3,2,1,0:T(8,128)(2,1)S(1)}, u32[]{:S(2)}, u32[]{:S(2)}) async-start(bf16[4,4,400,128]{3,2,1,0:T(8,128)(2,1)} %get-tuple-element.55), calls=%async_computation.1 | async-start | bytes 3276800 | tf_op jit(solution)/shard_map/all_to_all | solution.py:615
  110.9 21.7 %collective-permute-start.6 = (bf16[4,400,128]{2,1,0:T(8,128)(2,1)S(1)}, bf16[4,400,128]{2,1,0:T(8,128)(2,1)}, u32[]{:S(2)}, u32[]{:S(2)}) collective-permute-start(bf16[4,400,128]{2,1,0:T(8,128)(2,1)S(1)} %get-tuple-element.59), channel_id=1, source_target_pairs={{0,2},{2,4},{4,6},{6,0},{1,3},{3,5},{5,7},{7,1},{8,10},{10,12},{12... | collective-permute-start | bytes 1228808 | tf_op jit(solution)/shard_map/ppermute | solution.py:601
  112.4 20.9 %collective-permute-start.7 = (bf16[4,400,128]{2,1,0:T(8,128)(2,1)S(1)}, bf16[4,400,128]{2,1,0:T(8,128)(2,1)}, u32[]{:S(2)}, u32[]{:S(2)}) collective-permute-start(bf16[4,400,128]{2,1,0:T(8,128)(2,1)S(1)} %get-tuple-element.60), channel_id=1, source_target_pairs={{0,4},{2,6},{4,0},{6,2},{1,5},{3,7},{5,1},{7,3},{8,12},{10,14},{12... | collective-permute-start | bytes 1228808 | tf_op jit(solution)/shard_map/ppermute | solution.py:601
  114.8 18.5 %collective-permute-start.8 = (bf16[4,400,128]{2,1,0:T(8,128)(2,1)S(1)}, bf16[4,400,128]{2,1,0:T(8,128)(2,1)}, u32[]{:S(2)}, u32[]{:S(2)}) collective-permute-start(bf16[4,400,128]{2,1,0:T(8,128)(2,1)S(1)} %get-tuple-element.61), channel_id=1, source_target_pairs={{0,6},{2,0},{4,2},{6,4},{1,7},{3,1},{5,3},{7,5},{8,14},{10,8},{12,... | collective-permute-start | bytes 1228808 | tf_op jit(solution)/shard_map/ppermute | solution.py:601
  135.5 10.0 %all-to-all-start.2 = ((bf16[4,400,128]{2,1,0:T(8,128)(2,1)}), bf16[4,400,128]{2,1,0:T(8,128)(2,1)S(1)}, u32[]{:S(2)}, u32[]{:S(2)}) async-start(bf16[4,400,128]{2,1,0:T(8,128)(2,1)} %add_convert_fusion), calls=%async_computation.2 | async-start | bytes 819200 | tf_op jit(solution)/shard_map/all_to_all | solution.py:615
  139.6 5.9 %collective-permute-start.10 = (bf16[400,128]{1,0:T(8,128)(2,1)S(1)}, bf16[400,128]{1,0:T(8,128)(2,1)S(1)}, u32[]{:S(2)}, u32[]{:S(2)}) collective-permute-start(bf16[400,128]{1,0:T(8,128)(2,1)S(1)} %get-tuple-element.91), channel_id=1, source_target_pairs={{0,2},{2,4},{4,6},{6,0},{1,3},{3,5},{5,7},{7,1},{8,10},{10,12},{12... | collective-permute-start | bytes 307208 | tf_op jit(solution)/shard_map/ppermute | solution.py:601
  140.9 7.0 %collective-permute-start.11 = (bf16[400,128]{1,0:T(8,128)(2,1)S(1)}, bf16[400,128]{1,0:T(8,128)(2,1)S(1)}, u32[]{:S(2)}, u32[]{:S(2)}) collective-permute-start(bf16[400,128]{1,0:T(8,128)(2,1)S(1)} %get-tuple-element.90), channel_id=1, source_target_pairs={{0,4},{2,6},{4,0},{6,2},{1,5},{3,7},{5,1},{7,3},{8,12},{10,14},{12... | collective-permute-start | bytes 307208 | tf_op jit(solution)/shard_map/ppermute | solution.py:601
  143.6 4.8 %collective-permute-start.12 = (bf16[400,128]{1,0:T(8,128)(2,1)S(1)}, bf16[400,128]{1,0:T(8,128)(2,1)S(1)}, u32[]{:S(2)}, u32[]{:S(2)}) collective-permute-start(bf16[400,128]{1,0:T(8,128)(2,1)S(1)} %get-tuple-element.89), channel_id=1, source_target_pairs={{0,6},{2,0},{4,2},{6,4},{1,7},{3,1},{5,3},{7,5},{8,14},{10,8},{12,... | collective-permute-start | bytes 307208 | tf_op jit(solution)/shard_map/ppermute | solution.py:601
  149.6 15.8 %all-to-all-start.3 = ((bf16[8,40,320]{2,1,0:T(8,128)(2,1)}), bf16[8,40,320]{2,1,0:T(8,128)(2,1)S(1)}, u32[]{:S(2)}, u32[]{:S(2)}) async-start(bf16[8,40,320]{2,1,0:T(8,128)(2,1)} %pad_maximum_fusion), calls=%async_computation.3 | async-start | bytes 491520 | tf_op jit(solution)/shard_map/all_to_all | solution.py:615
  165.4 5.0 %collective-permute-start.13 = (f32[40,320]{1,0:T(8,128)S(1)}, f32[40,320]{1,0:T(8,128)S(1)}, u32[]{:S(2)}, u32[]{:S(2)}) collective-permute-start(f32[40,320]{1,0:T(8,128)S(1)} %broadcast_multiply_fusion), channel_id=1, source_target_pairs={{0,2},{2,4},{4,6},{6,0},{1,3},{3,5},{5,7},{7,1},{8,10},{10,12},{12... | collective-permute-start | bytes 153608 | tf_op jit(solution)/shard_map/ppermute | solution.py:593
  165.6 4.9 %collective-permute-start.14 = (f32[40,320]{1,0:T(8,128)S(1)}, f32[40,320]{1,0:T(8,128)S(1)}, u32[]{:S(2)}, u32[]{:S(2)}) collective-permute-start(f32[40,320]{1,0:T(8,128)S(1)} %broadcast_multiply_fusion), channel_id=1, source_target_pairs={{0,4},{2,6},{4,0},{6,2},{1,5},{3,7},{5,1},{7,3},{8,12},{10,14},{12... | collective-permute-start | bytes 153608 | tf_op jit(solution)/shard_map/ppermute | solution.py:593
  167.8 3.2 %collective-permute-start.15 = (f32[40,320]{1,0:T(8,128)S(1)}, f32[40,320]{1,0:T(8,128)S(1)}, u32[]{:S(2)}, u32[]{:S(2)}) collective-permute-start(f32[40,320]{1,0:T(8,128)S(1)} %broadcast_multiply_fusion), channel_id=1, source_target_pairs={{0,6},{2,0},{4,2},{6,4},{1,7},{3,1},{5,3},{7,5},{8,14},{10,8},{12,... | collective-permute-start | bytes 153608 | tf_op jit(solution)/shard_map/ppermute | solution.py:593
  171.1 7.1 %collective-permute-start.16 = (f32[4,40,320]{2,1,0:T(8,128)S(1)}, f32[4,40,320]{2,1,0:T(8,128)S(1)}, u32[]{:S(2)}, u32[]{:S(2)}) collective-permute-start(f32[4,40,320]{2,1,0:T(8,128)S(1)} %bitcast_dynamic-update-slice_fusion.2), channel_id=1, source_target_pairs={{0,1},{1,0},{2,3},{3,2},{4,5},{5,4},{6,7},{7,6},{8,9},{9,8},{10,11... | collective-permute-start | bytes 614408 | tf_op jit(solution)/shard_map/ppermute | solution.py:593
Sparse Core Ops, SparseCore 0:
  16.4 42.2 all-gather.2
  68.1 38.4 all-gather.4
